TPU v7x, 128 devices: a whole 4x4x4 slice. The times are simulated.
128 devices in a mesh: section: 2 (over z_hi), dp: 8 (over z_lo, y), tensor: 8 (over x, core).
Axes of the slice: x: 4, y: 4, z: 4 (z_hi: 2, z_lo: 2; z = z_hi * 2 + z_lo), core: 2. Of those that a mesh axis runs over, the one named last changes fastest.
Arguments:
- inputs: bfloat16 [2, 1024, 8, 1024], P(None, 'tensor', 'dp'), may hold values from -6 to 6
- memory_states: bfloat16 [2, 256, 8, 1024], P(None, 'tensor', 'dp'), may hold values from -6 to 6
- source_lengths: int32 [2, 8], P(None, 'dp'), may hold values from 64 to 256, as said below
- cotangent: bfloat16 [2, 1024, 8, 1024], P(None, 'tensor', 'dp'), may hold values from -6 to 6
- norm_gain: float32 [2, 3, 1024], P('section'), may hold values from 0.5 to 1.5
- norm_bias: float32 [2, 3, 1024], P('section'), may hold values from -2 to 2
- w_self: bfloat16 [2, 1024, 3, 1024], P('section', None, None, 'tensor'), may hold values from -0.1875 to 0.1875
- w_self_out: bfloat16 [2, 1024, 1024], P('section', 'tensor'), may hold values from -2 to 2
- w_cross_q: bfloat16 [2, 1024, 1024], P('section', None, 'tensor'), may hold values from -0.1875 to 0.1875
- w_cross_kv: bfloat16 [2, 1024, 2, 1024], P('section', None, None, 'tensor'), may hold values from -0.1875 to 0.1875
- w_cross_out: bfloat16 [2, 1024, 1024], P('section', 'tensor'), may hold values from -2 to 2
- up_weight: bfloat16 [2, 1024, 4096], P('section', None, 'tensor'), may hold values from -0.1875 to 0.1875
- down_weight: bfloat16 [2, 4096, 1024], P('section', 'tensor'), may hold values from -0.09375 to 0.09375
Outputs:
- states: bfloat16 [2, 2, 1024, 8, 1024], P('section', None, 'tensor', 'dp')
- input_grads: bfloat16 [2, 2, 1024, 8, 1024], P('section', None, 'tensor', 'dp')
- grad_norm_gain: float32 [2, 2, 1024], P('section')
- grad_norm_bias: float32 [2, 2, 1024], P('section')
- grad_ffn_norm: float32 [2, 2, 1024], P('section')
- grad_w_self: float32 [2, 1024, 3, 1024], P('section', None, None, 'tensor')
- grad_w_self_out: float32 [2, 1024, 1024], P('section', 'tensor')
- grad_w_cross_q: float32 [2, 1024, 1024], P('section', None, 'tensor')
- grad_w_cross_kv: float32 [2, 1024, 2, 1024], P('section', None, None, 'tensor')
- grad_w_cross_out: float32 [2, 1024, 1024], P('section', 'tensor')
- grad_w_up: float32 [2, 1024, 4096], P('section', None, 'tensor')
- grad_w_down: float32 [2, 4096, 1024], P('section', 'tensor')
Inputs may be any that keep to these rules, and one draw needn't show every extreme that they name: `source_lengths`: in each micro-batch one sequence, drawn from the seed, has 256 valid encoder states, and another has 64.
All inputs are finite; a program needn't handle non-finite values.
Results may differ from a plain program's by a relative error of at most 0.033.
Values may be sent and summed in bfloat16 or wider, within the bound.
No kernel may reach another device: no remote copies, remote signals or barrier semaphores. Data moves between devices by JAX's collectives and lax.ppermute only.
A program may use at most 192 MiB of HBM per device.

v0:
```python
import jax
import jax.numpy as jnp
from jax import lax
from jax.sharding import PartitionSpec as P

HD = 64


EPSILON = 1e-05
NEG_FILL = -1000000000.0


def from_behind(value, axis, steps):
    count = lax.axis_size(axis)
    first, last = (max(0, -steps), min(count, count - steps))
    return lax.ppermute(value, axis, [(source, source + steps) for source in range(first, last)])


def normalize(residual_stream, gain_row, bias_row):
    average = jnp.mean(residual_stream, axis=-1, keepdims=True)
    centred = residual_stream - average
    inv_scale = lax.rsqrt(jnp.mean(centred * centred, axis=-1, keepdims=True) + EPSILON)
    standard = centred * inv_scale
    return (standard * gain_row + bias_row, standard, inv_scale)


def normalize_back(incoming, standard, inv_scale, gain_row):
    scaled = incoming * gain_row
    inner = (
        scaled
        - jnp.mean(scaled, axis=-1, keepdims=True)
        - standard * jnp.mean(scaled * standard, axis=-1, keepdims=True)
    )
    return (
        inner * inv_scale,
        jnp.sum(incoming * standard, axis=(0, 1)),
        jnp.sum(incoming, axis=(0, 1)),
    )


def gather_normed(local_part):
    return lax.all_gather(local_part, "tensor", axis=0, tiled=True)


def gather_incoming(local_part):
    return lax.all_gather(local_part, "tensor", axis=0, tiled=True)


def branch_total_sum(operand, weight, pattern):
    return lax.psum_scatter(
        jnp.einsum(pattern, operand, weight, preferred_element_type=jnp.float32).astype(
            jnp.bfloat16
        ),
        "tensor",
        scatter_dimension=0,
        tiled=True,
    ).astype(jnp.float32)


def normed_total_sum(operand, weight, pattern):
    return lax.psum_scatter(
        jnp.einsum(pattern, operand, weight, preferred_element_type=jnp.float32).astype(
            jnp.bfloat16
        ),
        "tensor",
        scatter_dimension=0,
        tiled=True,
    ).astype(jnp.float32)


def causal_bounds(length):
    return (jnp.arange(length, dtype=jnp.int32) + 1)[:, None]


def cross_bounds(lengths, length):
    return jnp.broadcast_to(lengths[None, :], (length, lengths.shape[0]))


def block_mask(bounds, offset, qblock, key_count):
    limits = lax.dynamic_slice_in_dim(bounds, offset, qblock, 0)
    slots = jnp.arange(key_count, dtype=jnp.int32)
    return slots[None, None, None, :] < jnp.transpose(limits)[:, None, :, None]


def attend_forward(query_in, key_in, value_in, bounds):
    length = query_in.shape[0]
    qblock = min(512, length)
    factor = query_in.shape[3] ** (-0.5)

    def one_block(offset):
        row_slice = lax.dynamic_slice_in_dim(query_in, offset, qblock, 0)
        scores = (
            jnp.einsum("qshe,kshe->shqk", row_slice, key_in, preferred_element_type=jnp.float32)
            * factor
        )
        scores = jnp.where(block_mask(bounds, offset, qblock, key_in.shape[0]), scores, NEG_FILL)
        highest = jnp.max(scores, axis=-1, keepdims=True)
        raised = jnp.exp(scores - highest)
        summed = jnp.sum(raised, axis=-1, keepdims=True)
        chances = (raised / summed).astype(jnp.bfloat16)
        mixed = jnp.einsum("shqk,kshe->qshe", chances, value_in, preferred_element_type=jnp.float32)
        return (mixed.astype(jnp.bfloat16), highest + jnp.log(summed))

    starts = jnp.arange(length // qblock, dtype=jnp.int32) * qblock
    mixed, log_total = lax.map(one_block, starts)
    return (mixed.reshape(length, query_in.shape[1], -1), log_total)


def attend_back(query_in, key_in, value_in, log_total, incoming, bounds):
    length = query_in.shape[0]
    qblock = min(512, length)
    factor = query_in.shape[3] ** (-0.5)

    def one_block(running, element):
        offset, block_total = element
        row_slice = lax.dynamic_slice_in_dim(query_in, offset, qblock, 0)
        grad_rows = lax.dynamic_slice_in_dim(incoming, offset, qblock, 0)
        scores = (
            jnp.einsum("qshe,kshe->shqk", row_slice, key_in, preferred_element_type=jnp.float32)
            * factor
        )
        scores = jnp.where(block_mask(bounds, offset, qblock, key_in.shape[0]), scores, NEG_FILL)
        chances = jnp.exp(scores - block_total)
        dchances = jnp.einsum(
            "qshe,kshe->shqk", grad_rows, value_in, preferred_element_type=jnp.float32
        )
        dscores = (
            chances * (dchances - jnp.sum(dchances * chances, axis=-1, keepdims=True))
        ).astype(jnp.bfloat16)
        grad_query = (
            jnp.einsum("shqk,kshe->qshe", dscores, key_in, preferred_element_type=jnp.float32)
            * factor
        )
        grad_key = (
            running[0]
            + jnp.einsum("shqk,qshe->kshe", dscores, row_slice, preferred_element_type=jnp.float32)
            * factor
        )
        grad_value = running[1] + jnp.einsum(
            "shqk,qshe->kshe",
            chances.astype(jnp.bfloat16),
            grad_rows,
            preferred_element_type=jnp.float32,
        )
        return ((grad_key, grad_value), grad_query)

    starts = jnp.arange(length // qblock, dtype=jnp.int32) * qblock
    empty = jnp.zeros(key_in.shape, jnp.float32)
    (grad_key, grad_value), grad_query = lax.scan(one_block, (empty, empty), (starts, log_total))
    return (grad_query.reshape(query_in.shape), grad_key, grad_value)


def layer_forward(residual_stream, memory, lengths, gain_rows, bias_rows, weights):
    w_self, w_self_out, w_cross_q, w_cross_kv, w_cross_out, up_weight, down_weight = weights
    seq_count = residual_stream.shape[1]
    normed, standard_a, inv_a = normalize(residual_stream, gain_rows[0], bias_rows[0])
    full_a = gather_normed(normed.astype(jnp.bfloat16))
    length = full_a.shape[0]
    packed = jnp.einsum("lsd,dkh->lskh", full_a, w_self, preferred_element_type=jnp.float32).astype(
        jnp.bfloat16
    )
    divided = packed.reshape(length, seq_count, 3, -1, HD)
    mixed_a, total_a = attend_forward(
        divided[:, :, 0], divided[:, :, 1], divided[:, :, 2], causal_bounds(length)
    )
    residual_stream = residual_stream + branch_total_sum(mixed_a, w_self_out, "lsh,hd->lsd")
    normed, standard_c, inv_c = normalize(residual_stream, gain_rows[1], bias_rows[1])
    full_c = gather_normed(normed.astype(jnp.bfloat16))
    cross_query = jnp.einsum(
        "lsd,dh->lsh", full_c, w_cross_q, preferred_element_type=jnp.float32
    ).astype(jnp.bfloat16)
    cross_query = cross_query.reshape(length, seq_count, -1, HD)
    cross_pair = jnp.einsum(
        "esd,dkh->eskh", memory, w_cross_kv, preferred_element_type=jnp.float32
    ).astype(jnp.bfloat16)
    cross_pair = cross_pair.reshape(memory.shape[0], seq_count, 2, -1, HD)
    mixed_c, total_c = attend_forward(
        cross_query, cross_pair[:, :, 0], cross_pair[:, :, 1], cross_bounds(lengths, length)
    )
    residual_stream = residual_stream + branch_total_sum(mixed_c, w_cross_out, "lsh,hd->lsd")
    normed, standard_f, inv_f = normalize(residual_stream, gain_rows[2], bias_rows[2])
    feed_forward_normed = gather_normed(normed.astype(jnp.bfloat16))
    before_activation = jnp.einsum(
        "wqi,ix->wqx", feed_forward_normed, up_weight, preferred_element_type=jnp.float32
    )
    activated_hidden = jax.nn.gelu(before_activation).astype(jnp.bfloat16)
    residual_stream = residual_stream + branch_total_sum(
        activated_hidden, down_weight, "yei,ic->yec"
    )
    stored = (
        standard_a,
        inv_a,
        full_a,
        divided,
        mixed_a,
        total_a,
        standard_c,
        inv_c,
        full_c,
        cross_query,
        cross_pair,
        mixed_c,
        total_c,
        standard_f,
        inv_f,
        feed_forward_normed,
        before_activation,
        activated_hidden,
    )
    return (residual_stream, stored)


def layer_back(incoming, stored, memory, lengths, gain_rows, weights):
    (
        standard_a,
        inv_a,
        full_a,
        divided,
        mixed_a,
        total_a,
        standard_c,
        inv_c,
        full_c,
        cross_query,
        cross_pair,
        mixed_c,
        total_c,
        standard_f,
        inv_f,
        feed_forward_normed,
        before_activation,
        activated_hidden,
    ) = stored
    w_self, w_self_out, w_cross_q, w_cross_kv, w_cross_out, up_weight, down_weight = weights
    seq_count = incoming.shape[1]
    length = full_a.shape[0]
    output_gradient = gather_incoming(incoming.astype(jnp.bfloat16))
    down_gradient = jnp.einsum(
        "evr,evi->ri", activated_hidden, output_gradient, preferred_element_type=jnp.float32
    )
    activation_gradient = jnp.einsum(
        "phu,ju->phj", output_gradient, down_weight, preferred_element_type=jnp.float32
    )
    preactivation_gradient = jax.vjp(jax.nn.gelu, before_activation)[1](activation_gradient)[
        0
    ].astype(jnp.bfloat16)
    up_gradient = jnp.einsum(
        "nto,ntu->ou",
        feed_forward_normed,
        preactivation_gradient,
        preferred_element_type=jnp.float32,
    )
    normed_gradient = normed_total_sum(preactivation_gradient, up_weight, "jgq,mq->jgm")
    delta, gain_f, bias_f = normalize_back(normed_gradient, standard_f, inv_f, gain_rows[2])
    incoming = incoming + delta
    output_gradient = gather_incoming(incoming.astype(jnp.bfloat16))
    grad_cross_out = jnp.einsum(
        "lsh,lsd->hd", mixed_c, output_gradient, preferred_element_type=jnp.float32
    )
    grad_mixed = jnp.einsum(
        "lsd,hd->lsh", output_gradient, w_cross_out, preferred_element_type=jnp.float32
    ).astype(jnp.bfloat16)
    grad_mixed = grad_mixed.reshape(length, seq_count, -1, HD)
    grad_query, grad_key, grad_value = attend_back(
        cross_query,
        cross_pair[:, :, 0],
        cross_pair[:, :, 1],
        total_c,
        grad_mixed,
        cross_bounds(lengths, length),
    )
    grad_query = grad_query.astype(jnp.bfloat16).reshape(length, seq_count, -1)
    grad_pair = (
        jnp.stack([grad_key, grad_value], axis=2)
        .astype(jnp.bfloat16)
        .reshape(memory.shape[0], seq_count, 2, -1)
    )
    grad_cross_q = jnp.einsum("lsd,lsh->dh", full_c, grad_query, preferred_element_type=jnp.float32)
    grad_cross_kv = jnp.einsum(
        "esd,eskh->dkh", memory, grad_pair, preferred_element_type=jnp.float32
    )
    normed_gradient = normed_total_sum(grad_query, w_cross_q, "lsh,dh->lsd")
    delta, gain_c, bias_c = normalize_back(normed_gradient, standard_c, inv_c, gain_rows[1])
    incoming = incoming + delta
    output_gradient = gather_incoming(incoming.astype(jnp.bfloat16))
    grad_self_out = jnp.einsum(
        "lsh,lsd->hd", mixed_a, output_gradient, preferred_element_type=jnp.float32
    )
    grad_mixed = jnp.einsum(
        "lsd,hd->lsh", output_gradient, w_self_out, preferred_element_type=jnp.float32
    ).astype(jnp.bfloat16)
    grad_mixed = grad_mixed.reshape(length, seq_count, -1, HD)
    grad_query, grad_key, grad_value = attend_back(
        divided[:, :, 0],
        divided[:, :, 1],
        divided[:, :, 2],
        total_a,
        grad_mixed,
        causal_bounds(length),
    )
    grad_packed = (
        jnp.stack([grad_query, grad_key, grad_value], axis=2)
        .astype(jnp.bfloat16)
        .reshape(length, seq_count, 3, -1)
    )
    grad_self = jnp.einsum("lsd,lskh->dkh", full_a, grad_packed, preferred_element_type=jnp.float32)
    normed_gradient = normed_total_sum(grad_packed, w_self, "lskh,dkh->lsd")
    delta, gain_a, bias_a = normalize_back(normed_gradient, standard_a, inv_a, gain_rows[0])
    incoming = incoming + delta
    gradients = (
        grad_self,
        grad_self_out,
        grad_cross_q,
        grad_cross_kv,
        grad_cross_out,
        up_gradient,
        down_gradient,
    )
    return (
        incoming,
        gradients,
        jnp.stack([gain_a, gain_c, gain_f]),
        jnp.stack([bias_a, bias_c, bias_f]),
    )


def shards(
    inputs,
    memory_states,
    source_lengths,
    cotangent,
    norm_gain,
    norm_bias,
    w_self,
    w_self_out,
    w_cross_q,
    w_cross_kv,
    w_cross_out,
    up_weight,
    down_weight,
):
    section_index = lax.axis_index("section")
    is_first = section_index == 0
    micro = inputs.shape[0]
    weights = (
        w_self[0],
        w_self_out[0],
        w_cross_q[0],
        w_cross_kv[0],
        w_cross_out[0],
        up_weight[0],
        down_weight[0],
    )
    gain_rows = norm_gain[0]
    bias_rows = norm_bias[0]
    outgoing = jnp.zeros(inputs.shape[1:], jnp.bfloat16)
    produced = []
    archive = []
    for moment in range(micro + 1):
        arrived = from_behind(outgoing, "section", 1)
        which_batch = jnp.clip(jnp.where(is_first, moment, moment - 1), 0, micro - 1)
        own_rows = lax.dynamic_index_in_dim(inputs, which_batch, 0, keepdims=False)
        residual_stream = jnp.where(is_first, own_rows, arrived).astype(jnp.float32)
        memory = lax.all_gather(
            lax.dynamic_index_in_dim(memory_states, which_batch, 0, keepdims=False),
            "tensor",
            axis=0,
            tiled=True,
        )
        lengths = lax.dynamic_index_in_dim(source_lengths, which_batch, 0, keepdims=False)
        result, stored = layer_forward(
            residual_stream, memory, lengths, gain_rows, bias_rows, weights
        )
        outgoing = result.astype(jnp.bfloat16)
        produced.append(outgoing)
        archive.append((stored, memory, lengths))
    returning = jnp.zeros(inputs.shape[1:], jnp.bfloat16)
    totals = tuple((jnp.zeros(weight.shape, jnp.float32) for weight in weights))
    gain_total = jnp.zeros(gain_rows.shape, jnp.float32)
    bias_total = jnp.zeros(bias_rows.shape, jnp.float32)
    handed_back = []
    for rewind in range(micro + 1):
        kept_at = micro - rewind
        arrived = from_behind(returning, "section", -1)
        which_batch = jnp.clip(jnp.where(is_first, kept_at, kept_at - 1), 0, micro - 1)
        given = lax.dynamic_index_in_dim(cotangent, which_batch, 0, keepdims=False)
        upstream = jnp.where(is_first, arrived, given).astype(jnp.float32)
        useful = jnp.where(is_first, float(kept_at < micro), float(kept_at >= 1))
        stored, memory, lengths = archive[kept_at]
        grad_residual, gradients, gain_grad, bias_grad = layer_back(
            upstream, stored, memory, lengths, gain_rows, weights
        )
        returning = grad_residual.astype(jnp.bfloat16)
        handed_back.append(returning)
        gradients = tuple((useful * member for member in gradients))
        totals = tuple((earlier + later for earlier, later in zip(totals, gradients)))
        gain_total = gain_total + useful * gain_grad
        bias_total = bias_total + useful * bias_grad
    totals = (
        lax.psum(totals[0].astype(jnp.bfloat16), "dp").astype(jnp.float32),
        lax.psum(totals[1].astype(jnp.bfloat16), "dp").astype(jnp.float32),
        lax.psum(totals[2].astype(jnp.bfloat16), "dp").astype(jnp.float32),
        lax.psum(totals[3].astype(jnp.bfloat16), "dp").astype(jnp.float32),
        lax.psum(totals[4].astype(jnp.bfloat16), "dp").astype(jnp.float32),
        lax.psum(totals[5].astype(jnp.bfloat16), "dp").astype(jnp.float32),
        lax.psum(totals[6].astype(jnp.bfloat16), "dp").astype(jnp.float32),
    )
    gain_total, bias_total = lax.psum((gain_total, bias_total), ("dp", "tensor"))
    stacked = jnp.stack(produced)
    states = jnp.where(is_first, stacked[:micro], stacked[1:])[None]
    by_place = jnp.stack(handed_back[::-1])
    input_grads = jnp.where(is_first, by_place[:micro], by_place[1:])[None]
    ffn_norm = jnp.stack([gain_total[2], bias_total[2]])
    return (
        states,
        input_grads,
        gain_total[:2][None],
        bias_total[:2][None],
        ffn_norm[None],
        totals[0][None],
        totals[1][None],
        totals[2][None],
        totals[3][None],
        totals[4][None],
        totals[5][None],
        totals[6][None],
    )


def solution(mesh):
    placed = (
        P(None, "tensor", "dp", None),
        P(None, "tensor", "dp", None),
        P(None, "dp"),
        P(None, "tensor", "dp", None),
        P("section", None, None),
        P("section", None, None),
        P("section", None, None, "tensor"),
        P("section", "tensor", None),
        P("section", None, "tensor"),
        P("section", None, None, "tensor"),
        P("section", "tensor", None),
        P("section", None, "tensor"),
        P("section", "tensor", None),
    )
    return jax.shard_map(
        shards,
        mesh=mesh,
        in_specs=placed,
        out_specs=(
            P("section", None, "tensor", "dp", None),
            P("section", None, "tensor", "dp", None),
            P("section", None, None),
            P("section", None, None),
            P("section", None, None),
            P("section", None, None, "tensor"),
            P("section", "tensor", None),
            P("section", None, "tensor"),
            P("section", None, None, "tensor"),
            P("section", "tensor", None),
            P("section", None, "tensor"),
            P("section", "tensor", None),
        ),
        check_vma=False,
    )
```

profile of v0, /device:TPU:1, one launch (start us, length us, event | category | flops | bytes accessed | tf_op | source)
XLA Modules:
  0.0 1777.8 jit_solution(13346485641779235312)
XLA Ops:
  21.5 28.6 %all-gather.22.cloned.1.call-done = bf16[1024,1,1024]{2,0,1:T(8,128)(2,1)} async-done(((bf16[128,1,1024]{2,0,1:T(8,128)(2,1)}), bf16[1024,1,1024]{2,0,1:T(8,128)(2,1)}) %all-gather.22.cloned.1.call-update) | async-done | bytes 2097168 | tf_op jit(solution)/shard_map/all_gather | solution.py:42
  69.8 30.6 %reduce-scatter.19.cloned.1.call-done = bf16[128,1,1024]{2,0,1:T(8,128)(2,1)} async-done(((bf16[1024,1,1024]{2,0,1:T(8,128)(2,1)}), bf16[128,1,1024]{2,0,1:T(8,128)(2,1)}) %reduce-scatter.19.cloned.1.call-update) | async-done | bytes 262160 | tf_op jit(solution)/shard_map/reduce_scatter | solution.py:50
  147.6 30.6 %reduce-scatter.21.cloned.1.call-done = bf16[128,1,1024]{2,0,1:T(8,128)(2,1)} async-done(((bf16[1024,1,1024]{2,0,1:T(8,128)(2,1)}), bf16[128,1,1024]{2,0,1:T(8,128)(2,1)}) %reduce-scatter.21.cloned.1.call-update) | async-done | bytes 262160 | tf_op jit(solution)/shard_map/reduce_scatter | solution.py:50
  180.8 27.3 %all-gather.26.cloned.1.call-done = bf16[1024,1,1024]{2,0,1:T(8,128)(2,1)} async-done(((bf16[128,1,1024]{2,0,1:T(8,128)(2,1)}), bf16[1024,1,1024]{2,0,1:T(8,128)(2,1)}) %all-gather.26.cloned.1.call-update) | async-done | bytes 2097168 | tf_op jit(solution)/shard_map/all_gather | solution.py:42
  215.4 30.7 %reduce-scatter.23.cloned.1.call-done = bf16[128,1,1024]{2,0,1:T(8,128)(2,1)} async-done(((bf16[1024,1,1024]{2,0,1:T(8,128)(2,1)}), bf16[128,1,1024]{2,0,1:T(8,128)(2,1)}) %reduce-scatter.23.cloned.1.call-update) | async-done | bytes 262160 | tf_op jit(solution)/shard_map/reduce_scatter | solution.py:50
  257.7 30.2 %all-gather.28.cloned.1.call-done = bf16[1024,1,1024]{2,0,1:T(8,128)(2,1)} async-done(((bf16[128,1,1024]{2,0,1:T(8,128)(2,1)}), bf16[1024,1,1024]{2,0,1:T(8,128)(2,1)}) %all-gather.28.cloned.1.call-update) | async-done | bytes 2097168 | tf_op jit(solution)/shard_map/all_gather | solution.py:42
  311.0 30.6 %reduce-scatter.25.cloned.1.call-done = bf16[128,1,1024]{2,0,1:T(8,128)(2,1)} async-done(((bf16[1024,1,1024]{2,0,1:T(8,128)(2,1)}), bf16[128,1,1024]{2,0,1:T(8,128)(2,1)}) %reduce-scatter.25.cloned.1.call-update) | async-done | bytes 262160 | tf_op jit(solution)/shard_map/reduce_scatter | solution.py:50
  387.3 30.5 %reduce-scatter.27.cloned.1.call-done = bf16[128,1,1024]{2,0,1:T(8,128)(2,1)} async-done(((bf16[1024,1,1024]{2,0,1:T(8,128)(2,1)}), bf16[128,1,1024]{2,0,1:T(8,128)(2,1)}) %reduce-scatter.27.cloned.1.call-update) | async-done | bytes 262160 | tf_op jit(solution)/shard_map/reduce_scatter | solution.py:50
  420.2 27.4 %all-gather.32.cloned.1.call-done = bf16[1024,1,1024]{2,0,1:T(8,128)(2,1)} async-done(((bf16[128,1,1024]{2,0,1:T(8,128)(2,1)}), bf16[1024,1,1024]{2,0,1:T(8,128)(2,1)}) %all-gather.32.cloned.1.call-update) | async-done | bytes 2097168 | tf_op jit(solution)/shard_map/all_gather | solution.py:42
  454.8 30.7 %reduce-scatter.29.cloned.1.call-done = bf16[128,1,1024]{2,0,1:T(8,128)(2,1)} async-done(((bf16[1024,1,1024]{2,0,1:T(8,128)(2,1)}), bf16[128,1,1024]{2,0,1:T(8,128)(2,1)}) %reduce-scatter.29.cloned.1.call-update) | async-done | bytes 262160 | tf_op jit(solution)/shard_map/reduce_scatter | solution.py:50
  496.2 30.4 %all-gather.34.cloned.1.call-done = bf16[1024,1,1024]{2,0,1:T(8,128)(2,1)} async-done(((bf16[128,1,1024]{2,0,1:T(8,128)(2,1)}), bf16[1024,1,1024]{2,0,1:T(8,128)(2,1)}) %all-gather.34.cloned.1.call-update) | async-done | bytes 2097168 | tf_op jit(solution)/shard_map/all_gather | solution.py:42
  545.8 30.7 %reduce-scatter.31.cloned.1.call-done = bf16[128,1,1024]{2,0,1:T(8,128)(2,1)} async-done(((bf16[1024,1,1024]{2,0,1:T(8,128)(2,1)}), bf16[128,1,1024]{2,0,1:T(8,128)(2,1)}) %reduce-scatter.31.cloned.1.call-update) | async-done | bytes 262160 | tf_op jit(solution)/shard_map/reduce_scatter | solution.py:50
  627.0 30.6 %reduce-scatter.33.cloned.1.call-done = bf16[128,1,1024]{2,0,1:T(8,128)(2,1)} async-done(((bf16[1024,1,1024]{2,0,1:T(8,128)(2,1)}), bf16[128,1,1024]{2,0,1:T(8,128)(2,1)}) %reduce-scatter.33.cloned.1.call-update) | async-done | bytes 262160 | tf_op jit(solution)/shard_map/reduce_scatter | solution.py:50
  692.6 23.2 %all-gather.40.cloned.1.call-done = bf16[1024,1,1024]{2,0,1:T(8,128)(2,1)} async-done(((bf16[128,1,1024]{2,0,1:T(8,128)(2,1)}), bf16[1024,1,1024]{2,0,1:T(8,128)(2,1)}) %all-gather.40.cloned.1.call-update) | async-done | bytes 2097168 | tf_op jit(solution)/shard_map/all_gather | solution.py:46
  728.6 26.2 %reduce-scatter.37.cloned.1.call-done = bf16[128,1,1024]{2,0,1:T(8,128)(2,1)} async-done(((bf16[1024,1,1024]{2,0,1:T(8,128)(2,1)}), bf16[128,1,1024]{2,0,1:T(8,128)(2,1)}) %reduce-scatter.37.cloned.1.call-update) | async-done | bytes 262160 | tf_op jit(solution)/shard_map/reduce_scatter | solution.py:61
  757.1 32.3 %reduce-scatter.35.cloned.1.call-done = bf16[128,1,1024]{2,0,1:T(8,128)(2,1)} async-done(((bf16[1024,1,1024]{2,0,1:T(8,128)(2,1)}), bf16[128,1,1024]{2,0,1:T(8,128)(2,1)}) %reduce-scatter.35.cloned.1.call-update) | async-done | bytes 262160 | tf_op jit(solution)/shard_map/reduce_scatter | solution.py:50
  792.1 27.3 %all-gather.42.cloned.1.call-done = bf16[1024,1,1024]{2,0,1:T(8,128)(2,1)} async-done(((bf16[128,1,1024]{2,0,1:T(8,128)(2,1)}), bf16[1024,1,1024]{2,0,1:T(8,128)(2,1)}) %all-gather.42.cloned.1.call-update) | async-done | bytes 2097168 | tf_op jit(solution)/shard_map/all_gather | solution.py:46
  843.3 30.6 %reduce-scatter.39.cloned.1.call-done = bf16[128,1,1024]{2,0,1:T(8,128)(2,1)} async-done(((bf16[1024,1,1024]{2,0,1:T(8,128)(2,1)}), bf16[128,1,1024]{2,0,1:T(8,128)(2,1)}) %reduce-scatter.39.cloned.1.call-update) | async-done | bytes 262160 | tf_op jit(solution)/shard_map/reduce_scatter | solution.py:61
  878.2 27.4 %all-gather.44.cloned.1.call-done = bf16[1024,1,1024]{2,0,1:T(8,128)(2,1)} async-done(((bf16[128,1,1024]{2,0,1:T(8,128)(2,1)}), bf16[1024,1,1024]{2,0,1:T(8,128)(2,1)}) %all-gather.44.cloned.1.call-update) | async-done | bytes 2097168 | tf_op jit(solution)/shard_map/all_gather | solution.py:46
  938.8 30.4 %reduce-scatter.41.cloned.1.call-done = bf16[128,1,1024]{2,0,1:T(8,128)(2,1)} async-done(((bf16[1024,1,1024]{2,0,1:T(8,128)(2,1)}), bf16[128,1,1024]{2,0,1:T(8,128)(2,1)}) %reduce-scatter.41.cloned.1.call-update) | async-done | bytes 262160 | tf_op jit(solution)/shard_map/reduce_scatter | solution.py:61
  981.7 28.3 %all-gather.46.cloned.1.call-done = bf16[1024,1,1024]{2,0,1:T(8,128)(2,1)} async-done(((bf16[128,1,1024]{2,0,1:T(8,128)(2,1)}), bf16[1024,1,1024]{2,0,1:T(8,128)(2,1)}) %all-gather.46.cloned.1.call-update) | async-done | bytes 2097168 | tf_op jit(solution)/shard_map/all_gather | solution.py:46
  1019.5 30.6 %reduce-scatter.43.cloned.1.call-done = bf16[128,1,1024]{2,0,1:T(8,128)(2,1)} async-done(((bf16[1024,1,1024]{2,0,1:T(8,128)(2,1)}), bf16[128,1,1024]{2,0,1:T(8,128)(2,1)}) %reduce-scatter.43.cloned.1.call-update) | async-done | bytes 262160 | tf_op jit(solution)/shard_map/reduce_scatter | solution.py:61
  1054.3 27.4 %all-gather.48.cloned.1.call-done = bf16[1024,1,1024]{2,0,1:T(8,128)(2,1)} async-done(((bf16[128,1,1024]{2,0,1:T(8,128)(2,1)}), bf16[1024,1,1024]{2,0,1:T(8,128)(2,1)}) %all-gather.48.cloned.1.call-update) | async-done | bytes 2097168 | tf_op jit(solution)/shard_map/all_gather | solution.py:46
  1096.2 30.7 %reduce-scatter.45.cloned.1.call-done = bf16[128,1,1024]{2,0,1:T(8,128)(2,1)} async-done(((bf16[1024,1,1024]{2,0,1:T(8,128)(2,1)}), bf16[128,1,1024]{2,0,1:T(8,128)(2,1)}) %reduce-scatter.45.cloned.1.call-update) | async-done | bytes 262160 | tf_op jit(solution)/shard_map/reduce_scatter | solution.py:61
  1131.4 26.9 %all-gather.50.cloned.1.call-done = bf16[1024,1,1024]{2,0,1:T(8,128)(2,1)} async-done(((bf16[128,1,1024]{2,0,1:T(8,128)(2,1)}), bf16[1024,1,1024]{2,0,1:T(8,128)(2,1)}) %all-gather.50.cloned.1.call-update) | async-done | bytes 2097168 | tf_op jit(solution)/shard_map/all_gather | solution.py:46
  1162.2 23.7 %while.171 = (s32[]{:T(128)}, f32[1024,1,2,64]{0,3,2,1:T(8,128)S(1)}, f32[1024,1,2,64]{0,3,2,1:T(8,128)}, bf16[2,512,1,2,64]{1,4,3,2,0:T(8,128)(2,1)}, s32[2]{0:...) while((s32[]{:T(128)}, ...), condition=%wide.region_77.78_spmd.clone, body=%wide.region_75.77_spmd.clone.sunk | while | flops 688061440 | bytes 44599660 | solution.py:149
  1194.2 30.6 %reduce-scatter.47.cloned.1.call-done = bf16[128,1,1024]{2,0,1:T(8,128)(2,1)} async-done(((bf16[1024,1,1024]{2,0,1:T(8,128)(2,1)}), bf16[128,1,1024]{2,0,1:T(8,128)(2,1)}) %reduce-scatter.47.cloned.1.call-update) | async-done | bytes 262160 | tf_op jit(solution)/shard_map/reduce_scatter | solution.py:61
  1237.5 28.2 %all-gather.52.cloned.1.call-done = bf16[1024,1,1024]{2,0,1:T(8,128)(2,1)} async-done(((bf16[128,1,1024]{2,0,1:T(8,128)(2,1)}), bf16[1024,1,1024]{2,0,1:T(8,128)(2,1)}) %all-gather.52.cloned.1.call-update) | async-done | bytes 2097168 | tf_op jit(solution)/shard_map/all_gather | solution.py:46
  1275.3 30.7 %reduce-scatter.49.cloned.1.call-done = bf16[128,1,1024]{2,0,1:T(8,128)(2,1)} async-done(((bf16[1024,1,1024]{2,0,1:T(8,128)(2,1)}), bf16[128,1,1024]{2,0,1:T(8,128)(2,1)}) %reduce-scatter.49.cloned.1.call-update) | async-done | bytes 262160 | tf_op jit(solution)/shard_map/reduce_scatter | solution.py:61
  1310.0 27.3 %all-gather.54.cloned.1.call-done = bf16[1024,1,1024]{2,0,1:T(8,128)(2,1)} async-done(((bf16[128,1,1024]{2,0,1:T(8,128)(2,1)}), bf16[1024,1,1024]{2,0,1:T(8,128)(2,1)}) %all-gather.54.cloned.1.call-update) | async-done | bytes 2097168 | tf_op jit(solution)/shard_map/all_gather | solution.py:46
  1352.1 30.6 %reduce-scatter.51.cloned.1.call-done = bf16[128,1,1024]{2,0,1:T(8,128)(2,1)} async-done(((bf16[1024,1,1024]{2,0,1:T(8,128)(2,1)}), bf16[128,1,1024]{2,0,1:T(8,128)(2,1)}) %reduce-scatter.51.cloned.1.call-update) | async-done | bytes 262160 | tf_op jit(solution)/shard_map/reduce_scatter | solution.py:61
  1481.4 275.4 %all-reduce = (f32[3,1024]{1,0:T(4,128)S(1)}, f32[3,1024]{1,0:T(4,128)S(1)}) all-reduce(f32[3,1024]{1,0:T(4,128)S(1)} %fusion.594, f32[3,1024]{1,0:T(4,128)S(1)} %fusion.596), channel_id=1, replica_groups=mesh['section'=2,'dp'=8,'tensor'=8] {'dp','tensor'}, use_global_device_ids=true, to_apply=%region_105.106 | all-reduce | flops 6144 | bytes 49152 | tf_op jit(solution)/shard_map/psum | solution.py:408
  (1140 shorter events, 705.9 us)
Async XLA Ops:
  21.1 79.3 %reduce-scatter.19.cloned.1.call-start = ((), (), s32[]{:S(2)}) async-start(), calls=%async_computation.19 | async-start | bytes 2359296 | tf_op jit(solution)/shard_map/reduce_scatter | solution.py:50
  69.7 62.7 %all-gather.24.cloned.1.call-start = ((), (), s32[]{:S(2)}) async-start(), calls=%async_computation.20 | async-start | bytes 2359296 | tf_op jit(solution)/shard_map/all_gather | solution.py:42
  104.5 73.8 %reduce-scatter.21.cloned.1.call-start = ((), (), s32[]{:S(2)}) async-start(), calls=%async_computation.21 | async-start | bytes 2359296 | tf_op jit(solution)/shard_map/reduce_scatter | solution.py:50
  180.6 65.5 %reduce-scatter.23.cloned.1.call-start = ((), (), s32[]{:S(2)}) async-start(), calls=%async_computation.23 | async-start | bytes 2359296 | tf_op jit(solution)/shard_map/reduce_scatter | solution.py:50
  215.3 72.5 %all-gather.28.cloned.1.call-start = ((), (), s32[]{:S(2)}) async-start(), calls=%async_computation.24 | async-start | bytes 2359296 | tf_op jit(solution)/shard_map/all_gather | solution.py:42
  257.7 83.9 %reduce-scatter.25.cloned.1.call-start = ((), (), s32[]{:S(2)}) async-start(), calls=%async_computation.25 | async-start | bytes 2359296 | tf_op jit(solution)/shard_map/reduce_scatter | solution.py:50
  310.9 62.2 %all-gather.30.cloned.1.call-start = ((), (), s32[]{:S(2)}) async-start(), calls=%async_computation.26 | async-start | bytes 2359296 | tf_op jit(solution)/shard_map/all_gather | solution.py:42
  345.7 72.2 %reduce-scatter.27.cloned.1.call-start = ((), (), s32[]{:S(2)}) async-start(), calls=%async_computation.27 | async-start | bytes 2359296 | tf_op jit(solution)/shard_map/reduce_scatter | solution.py:50
  420.1 65.4 %reduce-scatter.29.cloned.1.call-start = ((), (), s32[]{:S(2)}) async-start(), calls=%async_computation.29 | async-start | bytes 2359296 | tf_op jit(solution)/shard_map/reduce_scatter | solution.py:50
  454.8 71.7 %all-gather.34.cloned.1.call-start = ((), (), s32[]{:S(2)}) async-start(), calls=%async_computation.30 | async-start | bytes 2359296 | tf_op jit(solution)/shard_map/all_gather | solution.py:42
  496.1 80.3 %reduce-scatter.31.cloned.1.call-start = ((), (), s32[]{:S(2)}) async-start(), calls=%async_computation.31 | async-start | bytes 2359296 | tf_op jit(solution)/shard_map/reduce_scatter | solution.py:50
  545.7 62.7 %all-gather.36.cloned.1.call-start = ((), (), s32[]{:S(2)}) async-start(), calls=%async_computation.32 | async-start | bytes 2359296 | tf_op jit(solution)/shard_map/all_gather | solution.py:42
  580.6 77.0 %reduce-scatter.33.cloned.1.call-start = ((), (), s32[]{:S(2)}) async-start(), calls=%async_computation.33 | async-start | bytes 2359296 | tf_op jit(solution)/shard_map/reduce_scatter | solution.py:50
  671.3 83.5 %reduce-scatter.37.cloned.1.call-start = ((), (), s32[]{:S(2)}) async-start(), calls=%async_computation.37 | async-start | bytes 2359296 | tf_op jit(solution)/shard_map/reduce_scatter | solution.py:61
  724.1 65.3 %reduce-scatter.35.cloned.1.call-start = ((), (), s32[]{:S(2)}) async-start(), calls=%async_computation.35 | async-start | bytes 2359296 | tf_op jit(solution)/shard_map/reduce_scatter | solution.py:50
  728.6 90.8 %all-gather.42.cloned.1.call-start = ((), (), s32[]{:S(2)}) async-start(), calls=%async_computation.38 | async-start | bytes 2359296 | tf_op jit(solution)/shard_map/all_gather | solution.py:46
  791.9 82.1 %reduce-scatter.39.cloned.1.call-start = ((), (), s32[]{:S(2)}) async-start(), calls=%async_computation.39 | async-start | bytes 2359296 | tf_op jit(solution)/shard_map/reduce_scatter | solution.py:61
  843.3 62.3 %all-gather.44.cloned.1.call-start = ((), (), s32[]{:S(2)}) async-start(), calls=%async_computation.40 | async-start | bytes 2359296 | tf_op jit(solution)/shard_map/all_gather | solution.py:46
  878.1 91.1 %reduce-scatter.41.cloned.1.call-start = ((), (), s32[]{:S(2)}) async-start(), calls=%async_computation.41 | async-start | bytes 2359296 | tf_op jit(solution)/shard_map/reduce_scatter | solution.py:61
  938.5 71.5 %all-gather.46.cloned.1.call-start = ((), (), s32[]{:S(2)}) async-start(), calls=%async_computation.42 | async-start | bytes 2359296 | tf_op jit(solution)/shard_map/all_gather | solution.py:46
  981.7 68.5 %reduce-scatter.43.cloned.1.call-start = ((), (), s32[]{:S(2)}) async-start(), calls=%async_computation.43 | async-start | bytes 2359296 | tf_op jit(solution)/shard_map/reduce_scatter | solution.py:61
  1019.5 62.2 %all-gather.48.cloned.1.call-start = ((), (), s32[]{:S(2)}) async-start(), calls=%async_computation.44 | async-start | bytes 2359296 | tf_op jit(solution)/shard_map/all_gather | solution.py:46
  1054.2 72.7 %reduce-scatter.45.cloned.1.call-start = ((), (), s32[]{:S(2)}) async-start(), calls=%async_computation.45 | async-start | bytes 2359296 | tf_op jit(solution)/shard_map/reduce_scatter | solution.py:61
  1096.2 62.1 %all-gather.50.cloned.1.call-start = ((), (), s32[]{:S(2)}) async-start(), calls=%async_computation.46 | async-start | bytes 2359296 | tf_op jit(solution)/shard_map/all_gather | solution.py:46
  1130.9 93.9 %reduce-scatter.47.cloned.1.call-start = ((), (), s32[]{:S(2)}) async-start(), calls=%async_computation.47 | async-start | bytes 2359296 | tf_op jit(solution)/shard_map/reduce_scatter | solution.py:61
  1194.2 71.6 %all-gather.52.cloned.1.call-start = ((), (), s32[]{:S(2)}) async-start(), calls=%async_computation.48 | async-start | bytes 2359296 | tf_op jit(solution)/shard_map/all_gather | solution.py:46
  1237.3 68.6 %reduce-scatter.49.cloned.1.call-start = ((), (), s32[]{:S(2)}) async-start(), calls=%async_computation.49 | async-start | bytes 2359296 | tf_op jit(solution)/shard_map/reduce_scatter | solution.py:61
  1275.2 62.1 %all-gather.54.cloned.1.call-start = ((), (), s32[]{:S(2)}) async-start(), calls=%async_computation.50 | async-start | bytes 2359296 | tf_op jit(solution)/shard_map/all_gather | solution.py:46
  1310.0 72.8 %reduce-scatter.51.cloned.1.call-start = ((), (), s32[]{:S(2)}) async-start(), calls=%async_computation.51 | async-start | bytes 2359296 | tf_op jit(solution)/shard_map/reduce_scatter | solution.py:61
  1352.1 62.2 %all-gather.56.cloned.1.call-start = ((), (), s32[]{:S(2)}) async-start(), calls=%async_computation.52 | async-start | bytes 2359296 | tf_op jit(solution)/shard_map/all_gather | solution.py:46
  1386.7 93.2 %reduce-scatter.53.cloned.1.call-start = ((), (), s32[]{:S(2)}) async-start(), calls=%async_computation.53 | async-start | bytes 2359296 | tf_op jit(solution)/shard_map/reduce_scatter | solution.py:61
  1442.3 315.7 %all-reduce.4.cloned.1.call-start = ((), (), s32[]{:S(2)}) async-start(), calls=%async_computation.54 | async-start | bytes 8388608 | tf_op jit(solution)/shard_map/psum | solution.py:403
  (294 other events, 4938.0 us)
Sparse Core Ops, SparseCore 0:
  21.2 28.8 all-gather.21
  69.8 30.4 reduce-scatter.18
  104.6 27.7 all-gather.23
  147.7 30.5 reduce-scatter.20
  180.7 27.3 all-gather.25
  215.5 30.5 reduce-scatter.22
  257.8 30.0 all-gather.27
  311.0 30.4 reduce-scatter.24
  387.2 30.6 reduce-scatter.26
  454.9 30.5 reduce-scatter.28
  496.2 30.2 all-gather.33
  545.8 30.5 reduce-scatter.30
  580.7 27.6 all-gather.35
  627.0 30.4 reduce-scatter.32
  660.8 27.3 all-gather.37
  724.2 30.5 reduce-scatter.36
  757.1 32.3 reduce-scatter.34
  792.0 27.3 all-gather.41
  843.4 30.4 reduce-scatter.38
  878.2 27.3 all-gather.43
  938.6 30.4 reduce-scatter.40
  981.8 28.2 all-gather.45
  1019.6 30.4 reduce-scatter.42
  1054.3 27.3 all-gather.47
  1096.3 30.5 reduce-scatter.44
  1194.3 30.4 reduce-scatter.46
  1237.4 28.2 all-gather.51
  1275.3 30.5 reduce-scatter.48
  1352.2 30.4 reduce-scatter.50
  1386.9 27.3 all-gather.55
  1442.4 30.4 reduce-scatter.52
  1478.3 108.7 all-reduce.3
  (5 shorter events, 134.2 us)
where the time goes:
time: 1790 us; the launch traced here: 1780 us
  waiting for transfers between devices  958 us (54%)
  blocking collectives  327 us (18%)
  matrix products  215 us (12%)
  other arithmetic  101 us (6%)
  local copies, waits for them, and re-layouts  86.7 us (5%)
  loops' own time  48.5 us (3%)
  starting transfers between devices  23.6 us (1%)
  between operations  18.1 us (1%)
    reduce_scatter x9, waiting for transfers between devices, branch_total_sum(): lax.psum_scatter(jnp.einsum(pattern, operand, weight, preferred_element_t...  277 us
    psum x1, blocking collectives, shards(): lax.psum((gain_total, bias_total), ('dp', 'tensor'))  275 us
    reduce_scatter x9, waiting for transfers between devices, normed_total_sum(): lax.psum_scatter(jnp.einsum(pattern, operand, weight, preferred_element_t...  240 us
    all_gather x9, waiting for transfers between devices, gather_incoming(): return lax.all_gather(local_part, 'tensor', axis=0, tiled=True)  221 us
    all_gather x9, waiting for transfers between devices, gather_normed(): return lax.all_gather(local_part, 'tensor', axis=0, tiled=True)  187 us
    all_gather x3, blocking collectives, shards(): lax.all_gather(lax.dynamic_index_in_dim(memory_states, which_batch, 0, ke...  51.4 us
  transfers between devices with their start and end apart: 43, of which 41 were waited for; matrix products, arithmetic and copies ran while one was open for 4% of the time, Pallas kernels for 0%

commit v1 on v0

v1 whole, which is shorter than its diff:
```python
import functools

import jax
import jax.numpy as jnp
from jax import lax
from jax.experimental import pallas as pl
from jax.experimental.pallas import tpu as pltpu
from jax.sharding import Mesh, PartitionSpec as P

HD = 64
EPSILON = 1e-05
NEG_FILL = -1000000000.0
BLOCK = 128
RING = 4
BF16 = jnp.bfloat16
F32 = jnp.float32


def shift(value, axis, steps):
    count = lax.axis_size(axis)
    return lax.ppermute(value, axis, [(i, (i + steps) % count) for i in range(count)])


def swap(value, axis):
    return shift(value, axis, 1)


def gather_x(value):
    return [value] + [shift(value, "tx", k) for k in range(1, RING)]


def scatter_x(own, others):
    arrived = [shift(block, "tx", -k) for k, block in enumerate(others, 1)]
    total = own
    for block in arrived:
        total = total + block.astype(F32)
    return total


def dot(a, b, dims):
    return lax.dot_general(a, b, ((dims[0], dims[1]), ((), ())), preferred_element_type=F32)


def mm(a, b):
    return dot(a, b, ((1,), (0,)))


def mm_nt(a, b):
    return dot(a, b, ((1,), (1,)))


def mm_tn(a, b):
    return dot(a, b, ((0,), (0,)))


def normalize(v, gain, bias):
    average = jnp.mean(v, axis=-1, keepdims=True)
    centred = v - average
    inv = lax.rsqrt(jnp.mean(centred * centred, axis=-1, keepdims=True) + EPSILON)
    standard = centred * inv
    return (standard * gain + bias).astype(BF16), standard, inv


def normalize_back(incoming, standard, inv, gain):
    scaled = incoming * gain
    inner = (
        scaled
        - jnp.mean(scaled, axis=-1, keepdims=True)
        - standard * jnp.mean(scaled * standard, axis=-1, keepdims=True)
    )
    return inner * inv, jnp.sum(incoming * standard, axis=0), jnp.sum(incoming, axis=0)


def block_of(place, b):
    return lax.rem(place[0] - b + RING, RING)


def lay_out_keys(place, own_ref, other_ref, kbuf, vbuf):
    core = place[1]
    for b in range(RING):
        j = block_of(place, b)
        own_at = pl.ds(pl.multiple_of((2 * b + core) * BLOCK, BLOCK), BLOCK)
        other_at = pl.ds(pl.multiple_of((2 * b + 1 - core) * BLOCK, BLOCK), BLOCK)
        for pair in range(2):
            here = slice(pair * 128, pair * 128 + 128)
            kbuf[own_at, here] = own_ref[j, :, 256 * pair : 256 * pair + 128]
            vbuf[own_at, here] = own_ref[j, :, 256 * pair + 128 : 256 * pair + 256]
            theirs = 1 - pair
            kbuf[other_at, here] = other_ref[j, :, 256 * theirs : 256 * theirs + 128]
            vbuf[other_at, here] = other_ref[j, :, 256 * theirs + 128 : 256 * theirs + 256]


def causal_tail(scores, core):
    key_at = lax.broadcasted_iota(jnp.int32, scores.shape, 0)
    query_at = lax.broadcasted_iota(jnp.int32, scores.shape, 1) + core * BLOCK
    return jnp.where(key_at <= query_at, scores, NEG_FILL)


def self_forward_kernel(place, q_ref, own_ref, other_ref, o_ref, lse_ref, kbuf, vbuf):
    lay_out_keys(place, own_ref, other_ref, kbuf, vbuf)
    core = place[1]
    for b in range(RING):
        j = block_of(place, b)
        span = 2 * BLOCK * (b + 1)
        head = span - 2 * BLOCK
        for pair in range(2):
            outs = []
            for h in (2 * pair, 2 * pair + 1):
                cols = slice(HD * h, HD * h + HD)
                q = q_ref[j, :, cols] * 0.125
                last = causal_tail(mm_nt(kbuf[head:span, cols], q), core)
                top = jnp.max(last, axis=0, keepdims=True)
                if head:
                    early = mm_nt(kbuf[0:head, cols], q)
                    top = jnp.maximum(top, jnp.max(early, axis=0, keepdims=True))
                    early = jnp.exp(early - top)
                last = jnp.exp(last - top)
                total = jnp.sum(last, axis=0, keepdims=True)
                mixed = mm_tn(vbuf[head:span, cols], last.astype(BF16))
                if head:
                    total = total + jnp.sum(early, axis=0, keepdims=True)
                    mixed = mixed + mm_tn(vbuf[0:head, cols], early.astype(BF16))
                outs.append(mixed / total)
                lse_ref[h, j] = top + jnp.log(total)
            both = jnp.concatenate(outs, axis=0)
            o_ref[j, :, 128 * pair : 128 * pair + 128] = both.T.astype(BF16)


def self_back_kernel(
    place, q_ref, own_ref, other_ref, do_ref, lse_ref, dq_ref, down_ref, dother_ref, kbuf, vbuf, dk, dv
):
    lay_out_keys(place, own_ref, other_ref, kbuf, vbuf)
    core = place[1]
    for b in reversed(range(RING)):
        j = block_of(place, b)
        span = 2 * BLOCK * (b + 1)
        head = span - 2 * BLOCK
        for pair in range(2):
            lanes = slice(128 * pair, 128 * pair + 128)
            dqs, dks, dvs = [], [], []
            for h in (2 * pair, 2 * pair + 1):
                cols = slice(HD * h, HD * h + HD)
                q = q_ref[j, :, cols] * 0.125
                do = do_ref[j, :, cols]
                k = kbuf[0:span, cols]
                scores = mm_nt(k, q)
                last = causal_tail(scores[head:span], core)
                scores = jnp.concatenate([scores[0:head], last], axis=0) if head else last
                probs = jnp.exp(scores - lse_ref[h, j])
                dprobs = mm_nt(vbuf[0:span, cols], do)
                delta = jnp.sum(probs * dprobs, axis=0, keepdims=True)
                dscores = (probs * (dprobs - delta)).astype(BF16)
                dqs.append(mm_tn(k, dscores) * 0.125)
                dks.append(mm(dscores, q))
                dvs.append(mm(probs.astype(BF16), do))
            dq_ref[j, :, lanes] = jnp.concatenate(dqs, axis=0).T.astype(BF16)
            dk_new = jnp.concatenate(dks, axis=1)
            dv_new = jnp.concatenate(dvs, axis=1)
            if b == RING - 1:
                dk[0:span, lanes] = dk_new
                dv[0:span, lanes] = dv_new
            else:
                dk[0:span, lanes] += dk_new
                dv[0:span, lanes] += dv_new
    for b in range(RING):
        j = block_of(place, b)
        own_at = pl.ds(pl.multiple_of((2 * b + core) * BLOCK, BLOCK), BLOCK)
        other_at = pl.ds(pl.multiple_of((2 * b + 1 - core) * BLOCK, BLOCK), BLOCK)
        for pair in range(2):
            here = slice(pair * 128, pair * 128 + 128)
            theirs = 1 - pair
            down_ref[j, :, 256 * pair : 256 * pair + 128] = dk[own_at, here]
            down_ref[j, :, 256 * pair + 128 : 256 * pair + 256] = dv[own_at, here]
            dother_ref[j, :, 256 * theirs : 256 * theirs + 128] = dk[other_at, here].astype(BF16)
            dother_ref[j, :, 256 * theirs + 128 : 256 * theirs + 256] = dv[other_at, here].astype(BF16)


def cross_mask(scores, length):
    slots = lax.broadcasted_iota(jnp.int32, scores.shape, 0)
    return jnp.where(slots < length, scores, NEG_FILL)


def cross_forward_kernel(length, q_ref, kv_ref, o_ref, lse_ref):
    for g in range(RING):
        outs = []
        for p in range(2):
            h = 2 * g + p
            q = q_ref[:, HD * h : HD * h + HD] * 0.125
            k = kv_ref[g, :, HD * p : HD * p + HD]
            v = kv_ref[g, :, 128 + HD * p : 128 + HD * p + HD]
            scores = cross_mask(mm_nt(k, q), length[0])
            top = jnp.max(scores, axis=0, keepdims=True)
            raised = jnp.exp(scores - top)
            total = jnp.sum(raised, axis=0, keepdims=True)
            outs.append(mm_tn(v, raised.astype(BF16)) / total)
            lse_ref[h] = top + jnp.log(total)
        o_ref[:, 128 * g : 128 * g + 128] = jnp.concatenate(outs, axis=0).T.astype(BF16)


def cross_back_kernel(length, q_ref, kv_ref, do_ref, lse_ref, dq_ref, dkv_ref):
    for g in range(RING):
        dqs, dks, dvs = [], [], []
        for p in range(2):
            h = 2 * g + p
            q = q_ref[:, HD * h : HD * h + HD] * 0.125
            do = do_ref[:, HD * h : HD * h + HD]
            k = kv_ref[g, :, HD * p : HD * p + HD]
            v = kv_ref[g, :, 128 + HD * p : 128 + HD * p + HD]
            probs = jnp.exp(cross_mask(mm_nt(k, q), length[0]) - lse_ref[h])
            dprobs = mm_nt(v, do)
            delta = jnp.sum(probs * dprobs, axis=0, keepdims=True)
            dscores = (probs * (dprobs - delta)).astype(BF16)
            dqs.append(mm_tn(k, dscores) * 0.125)
            dks.append(mm(dscores, q))
            dvs.append(mm(probs.astype(BF16), do))
        dq_ref[:, 128 * g : 128 * g + 128] = jnp.concatenate(dqs, axis=0).T.astype(BF16)
        dkv_ref[g] = jnp.concatenate(dks + dvs, axis=1).astype(BF16)


SMEM = pl.BlockSpec(memory_space=pltpu.SMEM)
VMEM = pl.BlockSpec(memory_space=pltpu.VMEM)
LIMIT = 48 * 1024 * 1024


def call(kernel, outs, scratch, flops, *operands):
    moved = sum(o.size * o.dtype.itemsize for o in operands) + sum(
        o.size * o.dtype.itemsize for o in outs
    )
    return pl.pallas_call(
        kernel,
        out_shape=outs,
        in_specs=[SMEM] + [VMEM] * (len(operands) - 1),
        out_specs=[VMEM] * len(outs),
        scratch_shapes=scratch,
        compiler_params=pltpu.CompilerParams(vmem_limit_bytes=LIMIT),
        cost_estimate=pl.CostEstimate(flops=flops, bytes_accessed=moved, transcendentals=0),
    )(*operands)


def struct(shape, dtype):
    return jax.ShapeDtypeStruct(shape, dtype)


KEYS = 2 * RING * BLOCK


def self_forward(place, q, kv, kv_other):
    return call(
        self_forward_kernel,
        [struct((RING, BLOCK, 256), BF16), struct((4, RING, 1, BLOCK), F32)],
        [pltpu.VMEM((KEYS, 256), BF16), pltpu.VMEM((KEYS, 256), BF16)],
        4 * 2 * 2 * 512 * 1024 * HD,
        place,
        q,
        kv,
        kv_other,
    )


def self_back(place, q, kv, kv_other, do, lse):
    return call(
        self_back_kernel,
        [
            struct((RING, BLOCK, 256), BF16),
            struct((RING, BLOCK, 512), F32),
            struct((RING, BLOCK, 512), BF16),
        ],
        [
            pltpu.VMEM((KEYS, 256), BF16),
            pltpu.VMEM((KEYS, 256), BF16),
            pltpu.VMEM((KEYS, 256), F32),
            pltpu.VMEM((KEYS, 256), F32),
        ],
        4 * 5 * 2 * 512 * 1024 * HD,
        place,
        q,
        kv,
        kv_other,
        do,
        lse,
    )


def cross_forward(length, q, kv):
    return call(
        cross_forward_kernel,
        [struct(q.shape, BF16), struct((2 * RING, 1, q.shape[0]), F32)],
        [],
        8 * 2 * 2 * 256 * 256 * HD,
        length,
        q,
        kv,
    )


def cross_back(length, q, kv, do, lse):
    return call(
        cross_back_kernel,
        [struct(q.shape, BF16), struct(kv.shape, BF16)],
        [],
        8 * 5 * 2 * 256 * 256 * HD,
        length,
        q,
        kv,
        do,
        lse,
    )


def rows_of(full):
    return [full[BLOCK * k : BLOCK * (k + 1)] for k in range(RING)]


def sum_rows(operands, weights, product):
    shares = [None] * RING
    for k in (2, 1, 3, 0):
        total = None
        for operand, weight in zip(operands, weights):
            part = product(operand[BLOCK * k : BLOCK * (k + 1)], weight)
            total = part if total is None else total + part
        shares[k] = total
    return scatter_x(shares[0], [share.astype(BF16) for share in shares[1:]])


def gelu_both(pre):
    root = 0.7978845608028654
    square = pre * pre
    t = jnp.tanh(root * (pre + 0.044715 * pre * square))
    half = 0.5 * (1.0 + t)
    slope = half + 0.5 * pre * (1.0 - t * t) * (root * (1.0 + 3 * 0.044715 * square))
    return (pre * half).astype(BF16), slope


def layer_forward(v, weights, kv, place, length, gain, bias):
    a1, s1, r1 = normalize(v, gain[0], bias[0])
    full1 = jnp.concatenate(gather_x(a1), axis=0)
    kv_self = mm(full1, weights["kv"]).astype(BF16).reshape(RING, BLOCK, 512)
    kv_other = swap(kv_self, "core")
    q = mm(full1, weights["q"]).astype(BF16).reshape(RING, BLOCK, 256)
    mixed1, lse1 = self_forward(place, q, kv_self, kv_other)
    mixed1 = mixed1.reshape(RING * BLOCK, 256)
    v1 = v + sum_rows([mixed1], [weights["out"]], mm)
    a2, s2, r2 = normalize(v1, gain[1], bias[1])
    pair2 = jnp.concatenate([a2, swap(a2, "core")], axis=0)
    cq = mm(pair2, weights["cq"]).astype(BF16)
    mixed2, lse2 = cross_forward(length, cq, kv)
    far = mm(mixed2[BLOCK:], weights["co"]).astype(BF16)
    near = mm(mixed2[:BLOCK], weights["co"])
    v2 = v1 + (near + swap(far, "core").astype(F32))
    a3, s3, r3 = normalize(v2, gain[2], bias[2])
    full3 = jnp.concatenate(gather_x(a3), axis=0)
    hidden, slope = gelu_both(mm(full3, weights["up"]))
    v3 = v2 + sum_rows([hidden], [weights["down"]], mm)
    stored = (
        (s1, r1, full1, q, kv_self, kv_other, mixed1, lse1),
        (s2, r2, pair2, cq, mixed2, lse2),
        (s3, r3, full3, hidden, slope),
    )
    return v3, stored


def pair_sum(left, right):
    half = left.shape[1] // 2
    theirs = mm_tn(left[:, half:], right).astype(BF16)
    ours = mm_tn(left[:, :half], right)
    return (ours + swap(theirs, "core").astype(F32)).astype(BF16)


def layer_back(dv, full_g3, stored, weights, kv, memory, place, length, gain):
    (s1, r1, full1, q, kv_self, kv_other, mixed1, lse1), second, third = stored
    s2, r2, pair2, cq, mixed2, lse2 = second
    s3, r3, full3, hidden, slope = third
    dpre = (mm_nt(full_g3, weights["down"]) * slope).astype(BF16)
    da3 = sum_rows([dpre], [weights["up"]], mm_nt)
    delta, gain3, bias3 = normalize_back(da3, s3, r3, gain[2])
    dv2 = dv + delta
    grad_down = pair_sum(hidden, full_g3)
    grad_up = pair_sum(dpre, full3)

    g2 = dv2.astype(BF16)
    pair_g2 = jnp.concatenate([g2, swap(g2, "core")], axis=0)
    dmixed2 = mm_nt(pair_g2, weights["co"]).astype(BF16)
    dcq, dkv = cross_back(length, cq, kv, dmixed2, lse2)
    far = mm_nt(dcq[BLOCK:], weights["cq"]).astype(BF16)
    near = mm_nt(dcq[:BLOCK], weights["cq"])
    da2 = near + swap(far, "core").astype(F32)
    delta, gain2, bias2 = normalize_back(da2, s2, r2, gain[1])
    dv1 = dv2 + delta

    g1 = dv1.astype(BF16)
    full_g1 = jnp.concatenate(gather_x(g1), axis=0)
    dmixed1 = mm_nt(full_g1, weights["out"]).astype(BF16).reshape(RING, BLOCK, 256)
    dq, dkv_own, dkv_theirs = self_back(place, q, kv_self, kv_other, dmixed1, lse1)
    dkv_self = dkv_own + swap(dkv_theirs, "core").astype(F32)
    dkv_self = dkv_self.astype(BF16).reshape(RING * BLOCK, 512)
    dq = dq.reshape(RING * BLOCK, 256)
    da1 = sum_rows([dq, dkv_self], [weights["q"], weights["kv"]], mm_nt)
    delta, gain1, bias1 = normalize_back(da1, s1, r1, gain[0])
    dv0 = dv1 + delta

    dwco = mm_tn(mixed2, pair_g2)
    grad_co = scatter_x(dwco[:128], [dwco[128 * k : 128 * k + 128].astype(BF16) for k in (1, 2, 3)])
    dwcq = mm_tn(dcq, pair2)
    grad_cq = scatter_x(dwcq[:128], [dwcq[128 * k : 128 * k + 128].astype(BF16) for k in (1, 2, 3)])
    dkv_sum = scatter_x(dkv[0].astype(F32), [dkv[k] for k in (1, 2, 3)]).astype(BF16)
    grad_ckv = mm_tn(dkv_sum, memory)
    grad_out = pair_sum(mixed1, full_g1)
    grad_q = pair_sum(dq, full1)
    grad_kv = pair_sum(dkv_self, full1)
    late = jnp.concatenate(
        [grad_co.astype(BF16), grad_cq.astype(BF16), grad_ckv.astype(BF16), grad_out, grad_q, grad_kv], axis=0
    )
    early = jnp.concatenate([grad_down, grad_up], axis=0)
    norms = jnp.stack([gain1, gain2, gain3, bias1, bias2, bias3])
    return dv0, early, late, norms


def sum_over_mesh(value):
    value = value + swap(value, "core")
    for axis in ("tx", "dy"):
        value = value + sum(shift(value, axis, k) for k in range(1, RING))
    value = value + swap(value, "dz")
    return value + swap(value, "section")


def reduce_dp(grads):
    return lax.psum_scatter(grads, ("dz", "dy"), scatter_dimension=0, tiled=True)


def finish(is_first, first_layer, second_layer):
    mine = jnp.where(is_first, first_layer, second_layer).astype(F32)
    theirs = jnp.where(is_first, second_layer, first_layer)
    total = (mine + swap(theirs, "section").astype(F32)).astype(BF16)
    return lax.all_gather(total, ("dz", "dy"), axis=0, tiled=True).astype(F32)


def shards(
    inputs,
    memory_states,
    source_lengths,
    cotangent,
    norm_gain,
    norm_bias,
    w_self,
    w_self_out,
    w_cross_q,
    w_cross_kv,
    w_cross_out,
    up_weight,
    down_weight,
):
    section = lax.axis_index("section")
    is_first = section == 0
    place = jnp.stack([lax.axis_index("tx"), lax.axis_index("core")]).astype(jnp.int32)

    def pick(array):
        return lax.dynamic_index_in_dim(array, section, 0, keepdims=False)

    def both_layers(mine, other):
        return jnp.where(is_first, mine, other), jnp.where(is_first, other, mine)

    x = pick(inputs)[:, 0]
    g_top = pick(cotangent)[:, 0]
    length = pick(source_lengths)
    memory = lax.all_gather(pick(memory_states)[:, 0], ("tx", "core"), axis=0, tiled=True)

    ws = w_self[0].reshape(w_self.shape[1], -1)
    mine = {
        "self": ws,
        "out": w_self_out[0],
        "cq": w_cross_q[0],
        "co": w_cross_out[0],
        "ckv": w_cross_kv[0].reshape(w_cross_kv.shape[1], -1),
        "up": up_weight[0],
        "down": down_weight[0],
    }
    other = {name: swap(value, "section") for name, value in mine.items()}
    gains = both_layers(norm_gain[0], swap(norm_gain[0], "section"))
    biases = both_layers(norm_bias[0], swap(norm_bias[0], "section"))

    layers = [{}, {}]
    for name, axis in (("self", 1), ("out", 0), ("up", 1), ("down", 0)):
        own = both_layers(mine[name], other[name])
        far = both_layers(swap(mine[name], "core"), swap(other[name], "core"))
        for i in range(2):
            if name == "self":
                layers[i]["q"] = jnp.concatenate([own[i][:, :128], far[i][:, :128]], axis=1)
                layers[i]["kv"] = jnp.concatenate([own[i][:, 128:], far[i][:, 128:]], axis=1)
            else:
                layers[i][name] = jnp.concatenate([own[i], far[i]], axis=axis)
    for name, axis in (("cq", 1), ("co", 0)):
        for i, value in enumerate(both_layers(mine[name], other[name])):
            layers[i][name] = jnp.concatenate(gather_x(value), axis=axis)
    ckv = both_layers(mine["ckv"], other["ckv"])
    pairs = [mm(memory, ckv[i]).astype(BF16) for i in range(2)]
    kvs = [jnp.stack(gather_x(pair)) for pair in pairs]

    text, stored0 = layer_forward(x.astype(F32), layers[0], kvs[0], place, length, gains[0], biases[0])
    text = text.astype(BF16)
    unit, stored1 = layer_forward(text.astype(F32), layers[1], kvs[1], place, length, gains[1], biases[1])
    unit = unit.astype(BF16)

    full_top = jnp.concatenate(gather_x(g_top), axis=0)
    dv, early1, late1, norms1 = layer_back(
        g_top.astype(F32), full_top, stored1, layers[1], kvs[1], memory, place, length, gains[1]
    )
    early1 = reduce_dp(early1)
    late1 = reduce_dp(late1)
    text_grad = dv.astype(BF16)
    full_text = jnp.concatenate(gather_x(text_grad), axis=0)
    dv, early0, late0, norms0 = layer_back(
        text_grad.astype(F32), full_text, stored0, layers[0], kvs[0], memory, place, length, gains[0]
    )
    input_grad = dv.astype(BF16)
    early = finish(is_first, reduce_dp(early0), early1)
    late = finish(is_first, reduce_dp(late0), late1)

    def by_layer(first, second):
        keep = jnp.where(is_first, first, second)
        came = swap(jnp.where(is_first, second, first), "section")
        return jnp.stack([jnp.where(is_first, keep, came), jnp.where(is_first, came, keep)])[None, :, :, None]

    states = by_layer(text, unit)
    input_grads = by_layer(input_grad, text_grad)
    norms = pick(sum_over_mesh(jnp.stack([norms0, norms1])))

    half = down_weight.shape[1]
    grad_down, grad_up = early[:half], early[half:].T
    grad_co, grad_cq = late[:128], late[128:256].T
    grad_ckv = late[256:512].T.reshape(-1, 2, 128)
    grad_out = late[512:640]
    grad_self = late[640:1024].T.reshape(-1, 3, 128)
    return (
        states,
        input_grads,
        norms[None, 0:2],
        norms[None, 3:5],
        jnp.stack([norms[2], norms[5]])[None],
        grad_self[None],
        grad_out[None],
        grad_cq[None],
        grad_ckv[None],
        grad_co[None],
        grad_up[None],
        grad_down[None],
    )


def solution(mesh):
    sections = mesh.devices.shape[0]
    fine = Mesh(
        mesh.devices.reshape(sections, 2, RING, RING, 2), ("section", "dz", "dy", "tx", "core")
    )
    dp, tensor = ("dz", "dy"), ("tx", "core")
    rows = P(None, tensor, dp, None)
    return jax.shard_map(
        shards,
        mesh=fine,
        in_specs=(
            rows,
            rows,
            P(None, dp),
            rows,
            P("section", None, None),
            P("section", None, None),
            P("section", None, None, tensor),
            P("section", tensor, None),
            P("section", None, tensor),
            P("section", None, None, tensor),
            P("section", tensor, None),
            P("section", None, tensor),
            P("section", tensor, None),
        ),
        out_specs=(
            P("section", None, tensor, dp, None),
            P("section", None, tensor, dp, None),
            P("section", None, None),
            P("section", None, None),
            P("section", None, None),
            P("section", None, None, tensor),
            P("section", tensor, None),
            P("section", None, tensor),
            P("section", None, None, tensor),
            P("section", tensor, None),
            P("section", None, tensor),
            P("section", tensor, None),
        ),
        check_vma=False,
    )
```

time: 1790 us -> 683 us (0.38)
  waiting for transfers between devices: 958 us -> 301 us
  blocking collectives: 327 us -> 13.3 us
  starting transfers between devices: 23.6 us -> 161 us
  matrix products: 215 us -> 81.2 us
  other arithmetic: 101 us -> 31.8 us
  local copies, waits for them, and re-layouts: 86.7 us -> 26.7 us
  loops' own time: 48.5 us -> 0 us
  Pallas kernels: 0 us -> 39.2 us
    reduce_scatter x18 -> x4, waiting for transfers between devices: 518 us -> 0.04 us  [reduce_dp(): lax.psum_scatter(grads, ('dz', 'dy'), scatter_dimension=0, tiled=True)]
    all_gather x18 -> x2, waiting for transfers between devices: 408 us -> 18.4 us  [finish(): return lax.all_gather(total, ('dz', 'dy'), axis=0, tiled=True).astype(F32)]
    psum x1 -> x0, blocking collectives: 275 us -> none  [shards(): lax.psum((gain_total, bias_total), ('dp', 'tensor'))]
    ppermute x6 -> x136, waiting for transfers between devices: 31.6 us -> 283 us  [shift(): lax.ppermute(value, axis, [(i, (i + steps) % count) for i in range(count)])]
    ppermute x6 -> x136, starting transfers between devices: 20.2 us -> 160 us  [shift(): lax.ppermute(value, axis, [(i, (i + steps) % count) for i in range(count)])]
    dot_general x138 -> x90, matrix products: 206 us -> 81.2 us  [dot(): lax.dot_general(a, b, ((dims[0], dims[1]), ((), ())), preferred_element_t...]
    another operation x12 -> x0, loops' own time: 48.5 us -> none  [the longest x6 24.8 us: attend_back(): lax.scan(one_block, (empty, empty), (starts, log_total))]
    pallas_call x0 -> x8, Pallas kernels: none -> 39.2 us  [call(): pl.pallas_call(kernel, out_shape=outs, in_specs=[SMEM] + [VMEM] * (len(op...]
  transfers between devices with their start and end apart: 43 -> 142, of which waited for: 41 -> 70; matrix products, arithmetic and copies ran while one was open for 4% -> 16% of each run, Pallas kernels for 0% -> 5%
where the time goes in v1:
time: 683 us; the launch traced here: 671 us
  waiting for transfers between devices  301 us (44%)
  starting transfers between devices  161 us (24%)
  matrix products  81.2 us (12%)
  Pallas kernels  39.2 us (6%)
  other arithmetic  31.8 us (5%)
  local copies, waits for them, and re-layouts  26.7 us (4%)
  between operations  17.1 us (3%)
  blocking collectives  13.3 us (2%)
    ppermute x136, waiting for transfers between devices, shift(): lax.ppermute(value, axis, [(i, (i + steps) % count) for i in range(count)])  283 us
    ppermute x136, starting transfers between devices, shift(): lax.ppermute(value, axis, [(i, (i + steps) % count) for i in range(count)])  160 us
    dot_general x90, matrix products, dot(): lax.dot_general(a, b, ((dims[0], dims[1]), ((), ())), preferred_element_t...  81.2 us
    pallas_call x8, Pallas kernels, call(): pl.pallas_call(kernel, out_shape=outs, in_specs=[SMEM] + [VMEM] * (len(op...  39.2 us
    all_gather x2, waiting for transfers between devices, finish(): return lax.all_gather(total, ('dz', 'dy'), axis=0, tiled=True).astype(F32)  18.4 us
    unnamed x338, local copies, waits for them, and re-layouts  16.5 us
  transfers between devices with their start and end apart: 142, of which 70 were waited for; matrix products, arithmetic and copies ran while one was open for 16% of the time, Pallas kernels for 5%

profile of v1, /device:TPU:1, one launch (start us, length us, event | category | flops | bytes accessed | tf_op | source)
XLA Modules:
  0.0 671.1 jit_solution(3770035106188518768)
XLA Ops:
  20.6 13.3 %all-gather = bf16[1,256,1,1024]{3,1,2,0:T(8,128)(2,1)S(1)} all-gather(bf16[1,32,1,1024]{3,1,2,0:T(8,128)(2,1)S(1)} %constant_dynamic-slice_fusion), channel_id=2, replica_groups=mesh['section'=2,'dz'=2,'dy'=4,'tx'=4,'core'=2] {'tx','core'}, dimensions={1}, use_global_device_ids=true | all-gather | bytes 589824 | tf_op jit(solution)/shard_map/all_gather | solution.py:465
  39.2 22.8 %collective-permute-done.24 = bf16[128,1024]{1,0:T(8,128)(2,1)S(1)} collective-permute-done((bf16[128,1024]{1,0:T(8,128)(2,1)S(1)}, bf16[128,1024]{1,0:T(8,128)(2,1)S(1)}, u32[]{:S(2)}, u32[]{:S(2)}) %collective-permute-start.24) | collective-permute-done | bytes 262176 | tf_op jit(solution)/shard_map/ppermute | solution.py:21
  68.4 9.0 %collective-permute-done.4 = bf16[128,1024]{1,0:T(8,128)(2,1)S(1)} collective-permute-done((bf16[128,1024]{1,0:T(8,128)(2,1)S(1)}, bf16[128,1024]{1,0:T(8,128)(2,1)S(1)}, u32[]{:S(2)}, u32[]{:S(2)}) %collective-permute-start.4) | collective-permute-done | bytes 262176 | tf_op jit(solution)/shard_map/ppermute | solution.py:21
  102.5 5.7 collective-permute-done.32
  118.0 7.0 %collective-permute-done.19 = bf16[1024,128]{1,0:T(8,128)(2,1)S(1)} collective-permute-done((bf16[1024,128]{1,0:T(8,128)(2,1)S(1)}, bf16[1024,128]{1,0:T(8,128)(2,1)S(1)}, u32[]{:S(2)}, u32[]{:S(2)}) %collective-permute-start.19) | collective-permute-done | bytes 262176 | tf_op jit(solution)/shard_map/ppermute | solution.py:21
  127.3 6.1 collective-permute-done.17
  158.5 6.3 collective-permute-done.31
  166.7 6.2 collective-permute-done.29
  178.7 5.9 collective-permute-done.38
  185.6 7.0 %collective-permute-done.40 = bf16[128,1024]{1,0:T(8,128)(2,1)S(1)} collective-permute-done((bf16[128,1024]{1,0:T(8,128)(2,1)S(1)}, bf16[128,1024]{1,0:T(8,128)(2,1)S(1)}, u32[]{:S(2)}, u32[]{:S(2)}) %collective-permute-start.40) | collective-permute-done | bytes 262176 | tf_op jit(solution)/shard_map/ppermute | solution.py:21
  195.5 5.8 collective-permute-done.43
  201.9 7.5 %collective-permute-done.41 = bf16[128,1024]{1,0:T(8,128)(2,1)S(1)} collective-permute-done((bf16[128,1024]{1,0:T(8,128)(2,1)S(1)}, bf16[128,1024]{1,0:T(8,128)(2,1)S(1)}, u32[]{:S(2)}, u32[]{:S(2)}) %collective-permute-start.41) | collective-permute-done | bytes 262176 | tf_op jit(solution)/shard_map/ppermute | solution.py:21
  212.4 5.4 shard_map.222
  228.2 7.6 %collective-permute-done.47 = bf16[128,1024]{1,0:T(8,128)(2,1)S(1)} collective-permute-done((bf16[128,1024]{1,0:T(8,128)(2,1)S(1)}, bf16[128,1024]{1,0:T(8,128)(2,1)S(1)}, u32[]{:S(2)}, u32[]{:S(2)}) %collective-permute-start.47) | collective-permute-done | bytes 262176 | tf_op jit(solution)/shard_map/ppermute | solution.py:21
  276.9 7.6 %collective-permute-done.59 = bf16[128,1024]{1,0:T(8,128)(2,1)S(1)} collective-permute-done((bf16[128,1024]{1,0:T(8,128)(2,1)S(1)}, bf16[128,1024]{1,0:T(8,128)(2,1)S(1)}, u32[]{:S(2)}, u32[]{:S(2)}) %collective-permute-start.59) | collective-permute-done | bytes 262176 | tf_op jit(solution)/shard_map/ppermute | solution.py:21
  288.1 6.6 collective-permute-done.66
  300.9 5.9 collective-permute-done.69
  307.5 7.3 %collective-permute-done.71 = bf16[128,1024]{1,0:T(8,128)(2,1)S(1)} collective-permute-done((bf16[128,1024]{1,0:T(8,128)(2,1)S(1)}, bf16[128,1024]{1,0:T(8,128)(2,1)S(1)}, u32[]{:S(2)}, u32[]{:S(2)}) %collective-permute-start.71) | collective-permute-done | bytes 262176 | tf_op jit(solution)/shard_map/ppermute | solution.py:21
  328.4 6.1 collective-permute-done.76
  336.6 6.4 collective-permute-done.74
  343.7 7.5 %shard_map.225 = (bf16[4,128,256]{2,1,0:T(8,128)(2,1)S(1)}, f32[4,128,512]{2,1,0:T(8,128)S(1)}, bf16[4,128,512]{2,1,0:T(8,128)(2,1)S(1)}) custom-call(s32[2]{0:T(128)S(1)} %pad_add_fusion.place, bf16[4,128,256]{2,1,0:T(8,128)(2,1)S(1)} %bitcast.309, bf16[4,128,512]{2,1,0:T(8,128)(2,1)S(1)} %bitcast.305, ...), custom_call_target="tpu_custom_call" | custom-call | flops 1342177280 | bytes 3416072 | tf_op jit(solution)/shard_map/pallas_call | solution.py:229
  363.3 6.8 %collective-permute-done.80 = bf16[128,1024]{1,0:T(8,128)(2,1)} collective-permute-done((bf16[128,1024]{1,0:T(8,128)(2,1)}, bf16[128,1024]{1,0:T(8,128)(2,1)}, u32[]{:S(2)}, u32[]{:S(2)}) %collective-permute-start.80) | collective-permute-done | bytes 262176 | tf_op jit(solution)/shard_map/ppermute | solution.py:21
  381.0 5.9 collective-permute-done.83
  411.4 7.4 %collective-permute-done.120 = bf16[128,1024]{1,0:T(8,128)(2,1)S(1)} collective-permute-done((bf16[128,1024]{1,0:T(8,128)(2,1)}, bf16[128,1024]{1,0:T(8,128)(2,1)S(1)}, u32[]{:S(2)}, u32[]{:S(2)}) %collective-permute-start.120) | collective-permute-done | bytes 262176 | tf_op jit(solution)/shard_map/ppermute | solution.py:21
  423.7 11.5 %collective-permute-done.123 = bf16[128,1024]{1,0:T(8,128)(2,1)S(1)} collective-permute-done((bf16[128,1024]{1,0:T(8,128)(2,1)S(1)}, bf16[128,1024]{1,0:T(8,128)(2,1)S(1)}, u32[]{:S(2)}, u32[]{:S(2)}) %collective-permute-start.123) | collective-permute-done | bytes 262176 | tf_op jit(solution)/shard_map/ppermute | solution.py:21
  454.5 6.6 collective-permute-done.86
  499.7 7.5 %shard_map.227 = (bf16[4,128,256]{2,1,0:T(8,128)(2,1)S(1)}, f32[4,128,512]{2,1,0:T(8,128)S(1)}, bf16[4,128,512]{2,1,0:T(8,128)(2,1)S(1)}) custom-call(s32[2]{0:T(128)S(1)} %pad_add_fusion.place, bf16[4,128,256]{2,1,0:T(8,128)(2,1)S(1)} %bitcast.307, bf16[4,128,512]{2,1,0:T(8,128)(2,1)S(1)} %bitcast.302, bf16[4,128,512]{2,1,0:T(8,128)(2,1)S(1)} %copy-done.3, ...), custom_call_target="tpu_custom_call" | custom-call | flops 1342177280 | bytes 3416072 | tf_op jit(solution)/shard_map/pallas_call | solution.py:229
  510.5 12.4 %collective-permute-start.92 = (bf16[4,128,512]{2,1,0:T(8,128)(2,1)S(1)}, bf16[4,128,512]{2,1,0:T(8,128)(2,1)S(1)}, u32[]{:S(2)}, u32[]{:S(2)}) collective-permute-start(bf16[4,128,512]{2,1,0:T(8,128)(2,1)S(1)} %get-tuple-element.45), channel_id=1, source_target_pairs={{0,1},{1,0},{2,3},{3,2},{4,5},{5,4},{6,7},{7,6},{8,9},{9,8},{10,11... | collective-permute-start | bytes 1572872 | tf_op jit(solution)/shard_map/ppermute | solution.py:21
  534.0 8.0 %collective-permute-done.135 = bf16[128,1024]{1,0:T(8,128)(2,1)S(1)} collective-permute-done((bf16[128,1024]{1,0:T(8,128)(2,1)S(1)}, bf16[128,1024]{1,0:T(8,128)(2,1)S(1)}, u32[]{:S(2)}, u32[]{:S(2)}) %collective-permute-start.135) | collective-permute-done | bytes 262176 | tf_op jit(solution)/shard_map/ppermute | solution.py:21
  556.7 6.9 %collective-permute-done.64 = bf16[128,1024]{1,0:T(8,128)(2,1)S(1)} collective-permute-done((bf16[128,1024]{1,0:T(8,128)(2,1)S(1)}, bf16[128,1024]{1,0:T(8,128)(2,1)S(1)}, u32[]{:S(2)}, u32[]{:S(2)}) %collective-permute-start.64) | collective-permute-done | bytes 262176 | tf_op jit(solution)/shard_map/ppermute | solution.py:21
  585.0 6.9 %collective-permute-done.93 = bf16[128,1024]{1,0:T(8,128)(2,1)} collective-permute-done((bf16[128,1024]{1,0:T(8,128)(2,1)}, bf16[128,1024]{1,0:T(8,128)(2,1)}, u32[]{:S(2)}, u32[]{:S(2)}) %collective-permute-start.93) | collective-permute-done | bytes 262176 | tf_op jit(solution)/shard_map/ppermute | solution.py:21
  636.2 18.4 %all-gather.4.cloned.1.call-done = bf16[1024,1024]{1,0:T(8,128)(2,1)} async-done(((bf16[128,1024]{1,0:T(8,128)(2,1)}), bf16[1024,1024]{1,0:T(8,128)(2,1)}) %all-gather.4.cloned.1.call-update) | async-done | bytes 2097168 | tf_op jit(solution)/shard_map/all_gather | solution.py:434
  (806 shorter events, 392.9 us)
Async XLA Ops:
  7.2 524.5 %reduce-scatter.11.cloned.1.call-start = ((), (), s32[]{:S(2)}) async-start(), calls=%async_computation.8 | async-start | bytes 2359296 | tf_op jit(solution)/shard_map/reduce_scatter | solution.py:427
  7.3 77.3 %collective-permute-start.10 = (bf16[128,1024]{1,0:T(8,128)(2,1)}, bf16[128,1024]{1,0:T(8,128)(2,1)}, u32[]{:S(2)}, u32[]{:S(2)}) collective-permute-start(bf16[128,1024]{1,0:T(8,128)(2,1)} %bitcast.335), channel_id=1, source_target_pairs={{0,1},{1,0},{2,3},{3,2},{4,5},{5,4},{6,7},{7,6},{8,9},{9,8},{10,11... | collective-permute-start | bytes 786440 | tf_op jit(solution)/shard_map/ppermute | solution.py:21
  8.8 55.2 %collective-permute-start.9 = (bf16[128,1024]{1,0:T(8,128)(2,1)}, bf16[128,1024]{1,0:T(8,128)(2,1)}, u32[]{:S(2)}, u32[]{:S(2)}) collective-permute-start(bf16[128,1024]{1,0:T(8,128)(2,1)} %bitcast.336), channel_id=1, source_target_pairs={{0,64},{64,0},{1,65},{65,1},{2,66},{66,2},{3,67},{67,3},{4,68},{68... | collective-permute-start | bytes 786440 | tf_op jit(solution)/shard_map/ppermute | solution.py:21
  13.2 22.6 %collective-permute-start.1 = (f32[3,1024]{1,0:T(4,128)S(1)}, f32[3,1024]{1,0:T(4,128)S(1)}, u32[]{:S(2)}, u32[]{:S(2)}) collective-permute-start(f32[3,1024]{1,0:T(4,128)S(1)} %bitcast.371), channel_id=1, source_target_pairs={{0,64},{64,0},{1,65},{65,1},{2,66},{66,2},{3,67},{67,3},{4,68},{68... | collective-permute-start | bytes 36872 | tf_op jit(solution)/shard_map/ppermute | solution.py:21
  13.9 22.0 %collective-permute-start = (f32[3,1024]{1,0:T(4,128)S(1)}, f32[3,1024]{1,0:T(4,128)S(1)}, u32[]{:S(2)}, u32[]{:S(2)}) collective-permute-start(f32[3,1024]{1,0:T(4,128)S(1)} %bitcast.370), channel_id=1, source_target_pairs={{0,64},{64,0},{1,65},{65,1},{2,66},{66,2},{3,67},{67,3},{4,68},{68... | collective-permute-start | bytes 36872 | tf_op jit(solution)/shard_map/ppermute | solution.py:21
  18.3 49.1 %collective-permute-start.6 = (bf16[1024,384]{0,1:T(8,128)(2,1)S(1)}, bf16[1024,384]{0,1:T(8,128)(2,1)S(1)}, u32[]{:S(2)}, u32[]{:S(2)}) collective-permute-start(bf16[1024,384]{0,1:T(8,128)(2,1)S(1)} %bitcast.314), channel_id=1, source_target_pairs={{0,1},{1,0},{2,3},{3,2},{4,5},{5,4},{6,7},{7,6},{8,9},{9,8},{10,11... | collective-permute-start | bytes 2359304 | tf_op jit(solution)/shard_map/ppermute | solution.py:21
  35.8 26.4 %collective-permute-start.5 = (bf16[1024,384]{0,1:T(8,128)(2,1)S(1)}, bf16[1024,384]{0,1:T(8,128)(2,1)S(1)}, u32[]{:S(2)}, u32[]{:S(2)}) collective-permute-start(bf16[1024,384]{0,1:T(8,128)(2,1)S(1)} %bitcast.315), channel_id=1, source_target_pairs={{0,64},{64,0},{1,65},{65,1},{2,66},{66,2},{3,67},{67,3},{4,68},{68... | collective-permute-start | bytes 2359304 | tf_op jit(solution)/shard_map/ppermute | solution.py:21
  35.9 26.1 %collective-permute-start.24 = (bf16[128,1024]{1,0:T(8,128)(2,1)S(1)}, bf16[128,1024]{1,0:T(8,128)(2,1)S(1)}, u32[]{:S(2)}, u32[]{:S(2)}) collective-permute-start(bf16[128,1024]{1,0:T(8,128)(2,1)S(1)} %bitcast.334), channel_id=1, source_target_pairs={{0,64},{64,0},{1,65},{65,1},{2,66},{66,2},{3,67},{67,3},{4,68},{68... | collective-permute-start | bytes 786440 | tf_op jit(solution)/shard_map/ppermute | solution.py:21
  62.0 22.2 %collective-permute-start.20 = (bf16[1024,256]{1,0:T(8,128)(2,1)S(1)}, bf16[1024,256]{1,0:T(8,128)(2,1)S(1)}, u32[]{:S(2)}, u32[]{:S(2)}) collective-permute-start(bf16[1024,256]{1,0:T(8,128)(2,1)S(1)} %bitcast.323), channel_id=1, source_target_pairs={{0,64},{64,0},{1,65},{65,1},{2,66},{66,2},{3,67},{67,3},{4,68},{68... | collective-permute-start | bytes 1572872 | tf_op jit(solution)/shard_map/ppermute | solution.py:21
  77.3 18.6 %collective-permute-start.16 = (bf16[1024,128]{1,0:T(8,128)(2,1)S(1)}, bf16[1024,128]{1,0:T(8,128)(2,1)S(1)}, u32[]{:S(2)}, u32[]{:S(2)}) collective-permute-start(bf16[1024,128]{1,0:T(8,128)(2,1)S(1)} %bitcast.337), channel_id=1, source_target_pairs={{0,64},{64,0},{1,65},{65,1},{2,66},{66,2},{3,67},{67,3},{4,68},{68... | collective-permute-start | bytes 786440 | tf_op jit(solution)/shard_map/ppermute | solution.py:21
  80.3 27.8 %collective-permute-start.32 = (bf16[1024,512]{1,0:T(8,128)(2,1)S(1)}, bf16[1024,512]{1,0:T(8,128)(2,1)S(1)}, u32[]{:S(2)}, u32[]{:S(2)}) collective-permute-start(bf16[1024,512]{1,0:T(8,128)(2,1)S(1)} %bitcast.316), channel_id=1, source_target_pairs={{0,64},{64,0},{1,65},{65,1},{2,66},{66,2},{3,67},{67,3},{4,68},{68... | collective-permute-start | bytes 3145736 | tf_op jit(solution)/shard_map/ppermute | solution.py:21
  100.5 51.3 %collective-permute-start.33 = (bf16[1024,512]{1,0:T(8,128)(2,1)S(1)}, bf16[1024,512]{1,0:T(8,128)(2,1)S(1)}, u32[]{:S(2)}, u32[]{:S(2)}) collective-permute-start(bf16[1024,512]{1,0:T(8,128)(2,1)S(1)} %bitcast.317), channel_id=1, source_target_pairs={{0,1},{1,0},{2,3},{3,2},{4,5},{5,4},{6,7},{7,6},{8,9},{9,8},{10,11... | collective-permute-start | bytes 3145736 | tf_op jit(solution)/shard_map/ppermute | solution.py:21
  108.1 26.4 %collective-permute-start.35 = (bf16[512,1024]{1,0:T(8,128)(2,1)S(1)}, bf16[512,1024]{1,0:T(8,128)(2,1)S(1)}, u32[]{:S(2)}, u32[]{:S(2)}) collective-permute-start(bf16[512,1024]{1,0:T(8,128)(2,1)S(1)} %bitcast.318), channel_id=1, source_target_pairs={{0,64},{64,0},{1,65},{65,1},{2,66},{66,2},{3,67},{67,3},{4,68},{68... | collective-permute-start | bytes 3145736 | tf_op jit(solution)/shard_map/ppermute | solution.py:21
  114.9 37.9 %collective-permute-start.34 = (bf16[1024,512]{1,0:T(8,128)(2,1)S(1)}, bf16[1024,512]{1,0:T(8,128)(2,1)}, u32[]{:S(2)}, u32[]{:S(2)}) collective-permute-start(bf16[1024,512]{1,0:T(8,128)(2,1)S(1)} %collective-permute-done.32), channel_id=1, source_target_pairs={{0,1},{1,0},{2,3},{3,2},{4,5},{5,4},{6,7},{7,6},{8,9},{9,8},{10,11... | collective-permute-start | bytes 3145736 | tf_op jit(solution)/shard_map/ppermute | solution.py:21
  220.2 17.8 %collective-permute-start.51 = (bf16[1024,128]{1,0:T(8,128)(2,1)S(1)}, bf16[1024,128]{1,0:T(8,128)(2,1)S(1)}, u32[]{:S(2)}, u32[]{:S(2)}) collective-permute-start(bf16[1024,128]{1,0:T(8,128)(2,1)S(1)} %copy-done.85), channel_id=1, source_target_pairs={{0,6},{2,0},{4,2},{6,4},{1,7},{3,1},{5,3},{7,5},{8,14},{10,8},{12,... | collective-permute-start | bytes 786440 | tf_op jit(solution)/shard_map/ppermute | solution.py:21
  225.9 26.0 %collective-permute-start.49 = (bf16[1024,128]{1,0:T(8,128)(2,1)S(1)}, bf16[1024,128]{1,0:T(8,128)(2,1)S(1)}, u32[]{:S(2)}, u32[]{:S(2)}) collective-permute-start(bf16[1024,128]{1,0:T(8,128)(2,1)S(1)} %copy-done.85), channel_id=1, source_target_pairs={{0,2},{2,4},{4,6},{6,0},{1,3},{3,5},{5,7},{7,1},{8,10},{10,12},{12... | collective-permute-start | bytes 786440 | tf_op jit(solution)/shard_map/ppermute | solution.py:21
  275.3 19.4 %collective-permute-start.66 = (bf16[128,1024]{1,0:T(8,128)(2,1)S(1)}, bf16[128,1024]{1,0:T(8,128)(2,1)S(1)}, u32[]{:S(2)}, u32[]{:S(2)}) collective-permute-start(bf16[128,1024]{1,0:T(8,128)(2,1)S(1)} %dynamic-slice_bitcast_fusion), channel_id=1, source_target_pairs={{0,2},{2,4},{4,6},{6,0},{1,3},{3,5},{5,7},{7,1},{8,10},{10,12},{12... | collective-permute-start | bytes 786440 | tf_op jit(solution)/shard_map/ppermute | solution.py:21
  317.8 34.0 %collective-permute-start.133 = (bf16[512,1024]{1,0:T(8,128)(2,1)S(1)}, bf16[512,1024]{1,0:T(8,128)(2,1)S(1)}, u32[]{:S(2)}, u32[]{:S(2)}) collective-permute-start(bf16[512,1024]{1,0:T(8,128)(2,1)S(1)} %convolution_convert_fusion.1), channel_id=1, source_target_pairs={{0,1},{1,0},{2,3},{3,2},{4,5},{5,4},{6,7},{7,6},{8,9},{9,8},{10,11... | collective-permute-start | bytes 3145736 | tf_op jit(solution)/shard_map/ppermute | solution.py:21
  324.6 28.0 %collective-permute-start.134 = (bf16[512,1024]{1,0:T(8,128)(2,1)S(1)}, bf16[512,1024]{1,0:T(8,128)(2,1)S(1)}, u32[]{:S(2)}, u32[]{:S(2)}) collective-permute-start(bf16[512,1024]{1,0:T(8,128)(2,1)S(1)} %convolution_convert_fusion), channel_id=1, source_target_pairs={{0,1},{1,0},{2,3},{3,2},{4,5},{5,4},{6,7},{7,6},{8,9},{9,8},{10,11... | collective-permute-start | bytes 3145736 | tf_op jit(solution)/shard_map/ppermute | solution.py:21
  361.6 170.2 %reduce-scatter.9.cloned.1.call-start = ((), (), s32[]{:S(2)}) async-start(), calls=%async_computation.7 | async-start | bytes 2359296 | tf_op jit(solution)/shard_map/reduce_scatter | solution.py:427
  378.9 60.6 %collective-permute-start.124 = (bf16[256,256]{1,0:T(8,128)(2,1)}, bf16[256,256]{1,0:T(8,128)(2,1)}, u32[]{:S(2)}, u32[]{:S(2)}) collective-permute-start(bf16[256,256]{1,0:T(8,128)(2,1)} %get-tuple-element.142), channel_id=1, source_target_pairs={{0,6},{2,0},{4,2},{6,4},{1,7},{3,1},{5,3},{7,5},{8,14},{10,8},{12,... | collective-permute-start | bytes 393224 | tf_op jit(solution)/shard_map/ppermute | solution.py:21
  380.9 58.6 %collective-permute-start.126 = (bf16[256,256]{1,0:T(8,128)(2,1)}, bf16[256,256]{1,0:T(8,128)(2,1)}, u32[]{:S(2)}, u32[]{:S(2)}) collective-permute-start(bf16[256,256]{1,0:T(8,128)(2,1)} %get-tuple-element.143), channel_id=1, source_target_pairs={{0,2},{2,4},{4,6},{6,0},{1,3},{3,5},{5,7},{7,1},{8,10},{10,12},{12... | collective-permute-start | bytes 393224 | tf_op jit(solution)/shard_map/ppermute | solution.py:21
  408.5 163.9 %reduce-scatter.7.cloned.1.call-start = ((), (), s32[]{:S(2)}) async-start(), calls=%async_computation.5 | async-start | bytes 2359296 | tf_op jit(solution)/shard_map/reduce_scatter | solution.py:427
  421.3 18.3 %collective-permute-start.125 = (bf16[256,256]{1,0:T(8,128)(2,1)S(1)}, bf16[256,256]{1,0:T(8,128)(2,1)S(1)}, u32[]{:S(2)}, u32[]{:S(2)}) collective-permute-start(bf16[256,256]{1,0:T(8,128)(2,1)S(1)} %copy-done.94), channel_id=1, source_target_pairs={{0,4},{2,6},{4,0},{6,2},{1,5},{3,7},{5,1},{7,3},{8,12},{10,14},{12... | collective-permute-start | bytes 393224 | tf_op jit(solution)/shard_map/ppermute | solution.py:21
  464.3 108.1 %reduce-scatter.5.cloned.1.call-start = ((), (), s32[]{:S(2)}) async-start(), calls=%async_computation.4 | async-start | bytes 2359296 | tf_op jit(solution)/shard_map/reduce_scatter | solution.py:427
  471.1 55.0 %collective-permute-start.112 = (bf16[256,256]{1,0:T(8,128)(2,1)S(1)}, bf16[256,256]{1,0:T(8,128)(2,1)S(1)}, u32[]{:S(2)}, u32[]{:S(2)}) collective-permute-start(bf16[256,256]{1,0:T(8,128)(2,1)S(1)} %get-tuple-element.139), channel_id=1, source_target_pairs={{0,6},{2,0},{4,2},{6,4},{1,7},{3,1},{5,3},{7,5},{8,14},{10,8},{12,... | collective-permute-start | bytes 393224 | tf_op jit(solution)/shard_map/ppermute | solution.py:21
  472.0 55.1 %collective-permute-start.114 = (bf16[256,256]{1,0:T(8,128)(2,1)S(1)}, bf16[256,256]{1,0:T(8,128)(2,1)S(1)}, u32[]{:S(2)}, u32[]{:S(2)}) collective-permute-start(bf16[256,256]{1,0:T(8,128)(2,1)S(1)} %get-tuple-element.140), channel_id=1, source_target_pairs={{0,2},{2,4},{4,6},{6,0},{1,3},{3,5},{5,7},{7,1},{8,10},{10,12},{12... | collective-permute-start | bytes 393224 | tf_op jit(solution)/shard_map/ppermute | solution.py:21
  497.1 25.9 %collective-permute-start.110 = (bf16[128,1024]{1,0:T(8,128)(2,1)S(1)}, bf16[128,1024]{1,0:T(8,128)(2,1)S(1)}, u32[]{:S(2)}, u32[]{:S(2)}) collective-permute-start(bf16[128,1024]{1,0:T(8,128)(2,1)S(1)} %get-tuple-element.125), channel_id=1, source_target_pairs={{0,4},{2,6},{4,0},{6,2},{1,5},{3,7},{5,1},{7,3},{8,12},{10,14},{12... | collective-permute-start | bytes 786440 | tf_op jit(solution)/shard_map/ppermute | solution.py:21
  507.2 20.0 %collective-permute-start.113 = (bf16[256,256]{1,0:T(8,128)(2,1)S(1)}, bf16[256,256]{1,0:T(8,128)(2,1)S(1)}, u32[]{:S(2)}, u32[]{:S(2)}) collective-permute-start(bf16[256,256]{1,0:T(8,128)(2,1)S(1)} %get-tuple-element.141), channel_id=1, source_target_pairs={{0,4},{2,6},{4,0},{6,2},{1,5},{3,7},{5,1},{7,3},{8,12},{10,14},{12... | collective-permute-start | bytes 393224 | tf_op jit(solution)/shard_map/ppermute | solution.py:21
  531.6 98.9 %all-gather.6.cloned.1.call-start = ((), (), s32[]{:S(2)}) async-start(), calls=%async_computation.9 | async-start | bytes 2359296 | tf_op jit(solution)/shard_map/all_gather | solution.py:434
  543.8 110.8 %all-gather.4.cloned.1.call-start = ((), (), s32[]{:S(2)}) async-start(), calls=%async_computation.6 | async-start | bytes 2359296 | tf_op jit(solution)/shard_map/all_gather | solution.py:434
  564.9 30.9 %collective-permute-start.65 = (bf16[128,1024]{1,0:T(8,128)(2,1)}, bf16[128,1024]{1,0:T(8,128)(2,1)}, u32[]{:S(2)}, u32[]{:S(2)}) collective-permute-start(bf16[128,1024]{1,0:T(8,128)(2,1)} %get-tuple-element.187), channel_id=1, source_target_pairs={{0,64},{64,0},{1,65},{65,1},{2,66},{66,2},{3,67},{67,3},{4,68},{68... | collective-permute-start | bytes 786440 | tf_op jit(solution)/shard_map/ppermute | solution.py:21
  (275 other events, 4483.2 us)
Sparse Core Ops, SparseCore 0:
  361.7 37.2 reduce-scatter.10
  408.6 36.6 reduce-scatter.8
  464.4 34.6 reduce-scatter.6
  531.8 36.0 reduce-scatter.4
  569.3 40.2 all-gather.5
  611.7 42.7 all-gather.3

commit v2 on v1

v2 whole, which is shorter than its diff:
```python
import functools
import math

import jax
import jax.numpy as jnp
from jax import lax
from jax.experimental import pallas as pl
from jax.experimental.pallas import tpu as pltpu
from jax.sharding import Mesh, PartitionSpec as P

HD = 64
EPSILON = 1e-05
NEG_FILL = -1000000000.0
BLOCK = 128
RING = 4
BF16 = jnp.bfloat16
F32 = jnp.float32


def shift(value, axis, steps):
    count = lax.axis_size(axis)
    return lax.ppermute(value, axis, [(i, (i + steps) % count) for i in range(count)])


def swap(value, axis):
    return shift(value, axis, 1)


def dot(a, b, dims):
    return lax.dot_general(a, b, ((dims[0], dims[1]), ((), ())), preferred_element_type=F32)


def mm(a, b):
    return dot(a, b, ((1,), (0,)))


def mm_nt(a, b):
    return dot(a, b, ((1,), (1,)))


def mm_tn(a, b):
    return dot(a, b, ((0,), (0,)))


def gather_x(value):
    return [value] + [shift(value, "tx", k) for k in range(1, RING)]


def send_x(others):
    return [shift(block, "tx", -k) for k, block in enumerate(others, 1)]


SMEM = pl.BlockSpec(memory_space=pltpu.SMEM)
VMEM = pl.BlockSpec(memory_space=pltpu.VMEM)
ANY = pl.BlockSpec(memory_space=pl.ANY)
HBM = pl.BlockSpec(memory_space=pltpu.HBM)
CHUNK = 256


def struct(shape, dtype):
    return jax.ShapeDtypeStruct(shape, dtype)


class Cold:
    def __init__(self, array):
        self.array = array


def cold(*arrays):
    return [Cold(array) for array in arrays]


def cold_if(flag, *arrays):
    return cold(*arrays) if flag else list(arrays)


def vmem(o):
    return pltpu.VMEM(o.shape, o.dtype)


class Place:
    axes = ("tx", "core", "dy", "dz", "section")

    def __getitem__(self, at):
        return lax.axis_index(self.axes[at])


PLACE = Place()


def settled(array):
    return pltpu.with_memory_space_constraint(array, pltpu.HBM)


def call(kernel, outs, operands, scalars=(), scratch=(), after=(), room=8, token=False):
    ins = [o if isinstance(o, Cold) else None for o in operands]
    arrays = [o.array if isinstance(o, Cold) else o for o in operands]
    puts = [o if isinstance(o, Cold) else None for o in outs]
    shapes = [o.array if isinstance(o, Cold) else o for o in outs]
    if token:
        puts.append(None)
        shapes.append(struct((8, 128), F32))
    placed = any(o is PLACE for o in scalars)
    scalars = [o for o in scalars if o is not PLACE]
    first, waits = len(scalars), len(after)
    last = first + len(arrays)
    brought = [vmem(o.array) for o in ins if o]
    taken = [vmem(o.array) for o in puts if o]
    held = sum(math.prod(o.shape) * o.dtype.itemsize for o in (*scratch, *brought, *taken))
    name = kernel.func.__name__ if isinstance(kernel, functools.partial) else kernel.__name__

    def body(*refs):
        given = list(refs[first:last])
        results = list(refs[last + waits : last + waits + len(shapes)])
        rest = list(refs[last + waits + len(shapes) :])
        semaphores = rest.pop() if brought or taken else None
        buffers = rest[len(scratch) :]
        moves, stores = [], []
        for at, o in enumerate(ins):
            if o:
                buffer = buffers[len(moves)]
                moves.append(
                    pltpu.make_async_copy(given[at], buffer, semaphores.at[len(moves)])
                )
                moves[-1].start()
                given[at] = buffer
        for at, o in enumerate(puts):
            if o:
                n = len(moves) + len(stores)
                stores.append(pltpu.make_async_copy(buffers[n], results[at], semaphores.at[n]))
                results[at] = buffers[n]
        for move in moves:
            move.wait()
        if token:
            results.pop()[...] = jnp.zeros((8, 128), F32)
        lead = [PLACE] if placed else []
        kernel(*lead, *refs[:first], *given, *results, *rest[: len(scratch)])
        for store in stores:
            store.start()
        for store in stores:
            store.wait()

    kept = [*scratch, *brought, *taken]
    if brought or taken:
        kept.append(pltpu.SemaphoreType.DMA((len(brought) + len(taken),)))
    return pl.pallas_call(
        body,
        name=name,
        out_shape=[pltpu.HBM(o.shape, o.dtype) if c else o for o, c in zip(shapes, puts)],
        in_specs=[SMEM] * first + [HBM if o else VMEM for o in ins] + [ANY] * waits,
        out_specs=[HBM if o else VMEM for o in puts],
        scratch_shapes=kept,
        compiler_params=pltpu.CompilerParams(vmem_limit_bytes=held + room * 1024 * 1024),
    )(*scalars, *(settled(a) if c else a for a, c in zip(arrays, ins)), *after)


ROW = struct((BLOCK, 1024), F32)
ROW16 = struct((BLOCK, 1024), BF16)
COLUMN = struct((BLOCK, 1), F32)
SENT = [ROW] + [ROW16] * (RING - 1)


def stack_rows(refs, cols=slice(None)):
    return jnp.concatenate([ref[:, cols] for ref in refs], axis=0)


def split_rows(total, outs, cols):
    outs[0][:, cols] = total[0:BLOCK]
    for k in range(1, len(outs)):
        outs[k][:, cols] = total[BLOCK * k : BLOCK * (k + 1)].astype(BF16)


def chunks(width=1024):
    return [slice(at, at + CHUNK) for at in range(0, width, CHUNK)]


def norm(v, gain, bias, a_ref, s_ref, r_ref):
    average = jnp.mean(v, axis=-1, keepdims=True)
    centred = v - average
    inv = lax.rsqrt(jnp.mean(centred * centred, axis=-1, keepdims=True) + EPSILON)
    standard = centred * inv
    s_ref[...] = standard
    r_ref[...] = inv
    a_ref[...] = (standard * gain + bias).astype(BF16)


def total_of(v_ref, near, far):
    total = v_ref[...].astype(F32) + near[...]
    for ref in far:
        total = total + ref[...].astype(F32)
    return total


def sum_norm_kernel(j, count, v_ref, near, *refs):
    far, (rows, v_out, a_ref, s_ref, r_ref) = refs[:count], refs[count:]
    v = total_of(v_ref, near, far)
    v_out[...] = v.astype(v_out.dtype)
    v = v_out[...].astype(F32)
    norm(v, rows[j : j + 1], rows[3 + j : 4 + j], a_ref, s_ref, r_ref)


def sum_norm(j, v, near, far, rows, kept, after=(), old=False, new=False):
    outs = [*cold_if(new, kept), ROW16, *cold_if(new, ROW, COLUMN)]
    return call(
        functools.partial(sum_norm_kernel, j, len(far)),
        outs,
        [*cold_if(old, v), near, *far, rows],
        after=after,
    )


def sum_last_kernel(v_ref, near, r1, r2, r3, v_out):
    v_out[...] = total_of(v_ref, near, (r1, r2, r3)).astype(BF16)


def sum_back_kernel(j, count, dv_ref, near, *refs):
    far, (s_ref, r_ref, rows, dv_out, g_out, norms) = refs[:count], refs[count:]
    da = near[...]
    for ref in far:
        da = da + ref[...].astype(F32)
    standard = s_ref[...]
    scaled = da * rows[j : j + 1]
    inner = (
        scaled
        - jnp.mean(scaled, axis=-1, keepdims=True)
        - standard * jnp.mean(scaled * standard, axis=-1, keepdims=True)
    )
    dv = dv_ref[...].astype(F32) + inner * r_ref[...]
    dv_out[...] = dv
    g_out[...] = dv.astype(BF16)
    norms[0:1] = jnp.sum(da * standard, axis=0, keepdims=True)
    norms[1:2] = jnp.sum(da, axis=0, keepdims=True)


def sum_back(j, dv, near, far, s, r, rows, after=(), old=False, new=False):
    return call(
        functools.partial(sum_back_kernel, j, len(far)),
        [*cold_if(new, ROW), ROW16, *cold_if(new, struct((2, 1024), F32))],
        [*cold_if(old, dv), near, *far, *cold_if(old, s, r, rows)],
        after=after,
    )


KEYS = 2 * RING * BLOCK


def block_of(place, b):
    return lax.rem(place[0] - b + RING, RING)


def lay_out_keys(place, own_ref, other_ref, kbuf, vbuf):
    core = place[1]
    for b in range(RING):
        j = block_of(place, b)
        own_at = pl.ds(pl.multiple_of((2 * b + core) * BLOCK, BLOCK), BLOCK)
        other_at = pl.ds(pl.multiple_of((2 * b + 1 - core) * BLOCK, BLOCK), BLOCK)
        for pair in range(2):
            here = slice(pair * 128, pair * 128 + 128)
            kbuf[own_at, here] = own_ref[j, :, 256 * pair : 256 * pair + 128]
            vbuf[own_at, here] = own_ref[j, :, 256 * pair + 128 : 256 * pair + 256]
            theirs = 1 - pair
            kbuf[other_at, here] = other_ref[j, :, 256 * theirs : 256 * theirs + 128]
            vbuf[other_at, here] = other_ref[j, :, 256 * theirs + 128 : 256 * theirs + 256]


def causal_tail(scores, core):
    key_at = lax.broadcasted_iota(jnp.int32, scores.shape, 0)
    query_at = lax.broadcasted_iota(jnp.int32, scores.shape, 1) + core * BLOCK
    return jnp.where(key_at <= query_at, scores, NEG_FILL)


class Tall:
    def __init__(self, *halves):
        self.halves = halves

    def __getitem__(self, key):
        rows, cols = key
        if rows.start is None:
            return jnp.concatenate([half[:, cols] for half in self.halves], axis=0)
        return self.halves[rows.start // 512][rows.start % 512 : rows.stop - 512 * (rows.start // 512), cols]


def qkv_rows(rows, own, far, q_ref, kv_ref):
    weights = (
        jnp.concatenate([own[:, 0:128], far[:, 0:128]], axis=1),
        own[:, 128:384],
        far[:, 128:384],
    )
    for n, weight in enumerate(weights):
        out = mm(rows, weight).astype(BF16)
        for k in range(RING):
            block = out[BLOCK * k : BLOCK * (k + 1)]
            if n == 0:
                q_ref[k] = block
            else:
                kv_ref[k, :, 256 * n - 256 : 256 * n] = block


def qkv_kernel(a0, a1, a2, a3, own0, own1, far0, far1, q_ref, kv_ref):
    own, far = Tall(own0, own1), Tall(far0, far1)
    qkv_rows(stack_rows((a0, a1, a2, a3)), own, far, q_ref, kv_ref)


def first_qkv_kernel(
    x0, x1, x2, x3, own0, own1, far0, far1, norms, q_ref, kv_ref, *refs
):
    outs, (s_ref, r_ref, all_ref) = refs[0:4], refs[4:7]
    own, far = Tall(own0, own1), Tall(far0, far1)
    for k, x_ref in enumerate((x0, x1, x2, x3)):
        x = x_ref[0:BLOCK].astype(F32)
        centred = x - jnp.mean(x, axis=-1, keepdims=True)
        inv = lax.rsqrt(jnp.mean(centred * centred, axis=-1, keepdims=True) + EPSILON)
        standard = centred * inv
        if k == 0:
            s_ref[...] = standard
            r_ref[...] = inv
        all_ref[BLOCK * k : BLOCK * (k + 1)] = standard.astype(BF16)
        outs[k][...] = (standard * norms[0:1] + norms[3:4]).astype(BF16)
    qkv_rows(stack_rows(outs), own, far, q_ref, kv_ref)


def lane_blocks(ref, at, cols):
    return jnp.concatenate(
        [ref[c : c + 128, at : at + 128] for c in range(cols.start, cols.stop, 128)], axis=1
    )


ALL_COLS = slice(0, 1024)


def self_forward_kernel(
    place, q_ref, own_ref, other_ref, w0, w1, w2, w3, o_ref, lse_ref, near, f1, f2, f3, kbuf, vbuf
):
    lay_out_keys(place, own_ref, other_ref, kbuf, vbuf)
    core = place[1]
    for b in range(RING):
        j = block_of(place, b)
        span = 2 * BLOCK * (b + 1)
        head = span - 2 * BLOCK
        for pair in range(2):
            outs = []
            for h in (2 * pair, 2 * pair + 1):
                cols = slice(HD * h, HD * h + HD)
                q = q_ref[j, :, cols] * 0.125
                last = causal_tail(mm_nt(kbuf[head:span, cols], q), core)
                top = jnp.max(last, axis=0, keepdims=True)
                if head:
                    early = mm_nt(kbuf[0:head, cols], q)
                    top = jnp.maximum(top, jnp.max(early, axis=0, keepdims=True))
                    early = jnp.exp(early - top)
                last = jnp.exp(last - top)
                total = jnp.sum(last, axis=0, keepdims=True)
                mixed = mm_tn(vbuf[head:span, cols], last.astype(BF16))
                if head:
                    total = total + jnp.sum(early, axis=0, keepdims=True)
                    mixed = mixed + mm_tn(vbuf[0:head, cols], early.astype(BF16))
                outs.append(mixed / total)
                lse_ref[h, j] = top + jnp.log(total)
            both = jnp.concatenate(outs, axis=0)
            o_ref[j, :, 128 * pair : 128 * pair + 128] = both.T.astype(BF16)
    rows = jnp.concatenate([o_ref[k] for k in range(RING)], axis=0)
    for cols in chunks():
        weight = jnp.concatenate([lane_blocks(w, 384, cols) for w in (Tall(w0, w1), Tall(w2, w3))], axis=0)
        split_rows(mm(rows, weight), (near, f1, f2, f3), cols)


def self_back_kernel(
    place, g0, g1, g2, g3, w0, w1, w2, w3, q_ref, own_ref, other_ref, lse_ref,
    dq_ref, down_ref, dother_ref, kbuf, vbuf, dobuf, dk, dv,
):
    rows = stack_rows((g0, g1, g2, g3))
    weight = jnp.concatenate([lane_blocks(w, 384, ALL_COLS) for w in (Tall(w0, w1), Tall(w2, w3))], axis=0)
    dobuf[...] = mm_nt(rows, weight).astype(BF16).reshape(dobuf.shape)
    lay_out_keys(place, own_ref, other_ref, kbuf, vbuf)
    core = place[1]
    for b in reversed(range(RING)):
        j = block_of(place, b)
        span = 2 * BLOCK * (b + 1)
        head = span - 2 * BLOCK
        for pair in range(2):
            lanes = slice(128 * pair, 128 * pair + 128)
            dqs, dks, dvs = [], [], []
            for h in (2 * pair, 2 * pair + 1):
                cols = slice(HD * h, HD * h + HD)
                q = q_ref[j, :, cols] * 0.125
                do = dobuf[j, :, cols]
                k = kbuf[0:span, cols]
                scores = mm_nt(k, q)
                last = causal_tail(scores[head:span], core)
                scores = jnp.concatenate([scores[0:head], last], axis=0) if head else last
                probs = jnp.exp(scores - lse_ref[h, j])
                dprobs = mm_nt(vbuf[0:span, cols], do)
                delta = jnp.sum(probs * dprobs, axis=0, keepdims=True)
                dscores = (probs * (dprobs - delta)).astype(BF16)
                dqs.append(mm_tn(k, dscores) * 0.125)
                dks.append(mm(dscores, q))
                dvs.append(mm(probs.astype(BF16), do))
            dq_ref[j, :, lanes] = jnp.concatenate(dqs, axis=0).T.astype(BF16)
            dk_new = jnp.concatenate(dks, axis=1)
            dv_new = jnp.concatenate(dvs, axis=1)
            if b == RING - 1:
                dk[0:span, lanes] = dk_new
                dv[0:span, lanes] = dv_new
            else:
                dk[0:span, lanes] += dk_new
                dv[0:span, lanes] += dv_new
    for b in range(RING):
        j = block_of(place, b)
        own_at = pl.ds(pl.multiple_of((2 * b + core) * BLOCK, BLOCK), BLOCK)
        other_at = pl.ds(pl.multiple_of((2 * b + 1 - core) * BLOCK, BLOCK), BLOCK)
        for pair in range(2):
            here = slice(pair * 128, pair * 128 + 128)
            theirs = 1 - pair
            down_ref[j, :, 256 * pair : 256 * pair + 128] = dk[own_at, here]
            down_ref[j, :, 256 * pair + 128 : 256 * pair + 256] = dv[own_at, here]
            dother_ref[j, :, 256 * theirs : 256 * theirs + 128] = dk[other_at, here].astype(BF16)
            dother_ref[j, :, 256 * theirs + 128 : 256 * theirs + 256] = dv[other_at, here].astype(BF16)


def keys_total(down_ref, dother_ref):
    total = [down_ref[k] + dother_ref[k].astype(F32) for k in range(RING)]
    return jnp.concatenate(total, axis=0).astype(BF16)


def self_rows_back_kernel(
    dq_ref, down_ref, dother_ref, own0, own1, far0, far1, near, f1, f2, f3
):
    own, far = Tall(own0, own1), Tall(far0, far1)
    dq = jnp.concatenate([dq_ref[k] for k in range(RING)], axis=0)
    rows = jnp.concatenate([dq, keys_total(down_ref, dother_ref)], axis=1)
    for cols in chunks():
        weight = jnp.concatenate(
            [own[cols, 0:128], far[cols, 0:128], own[cols, 128:384], far[cols, 128:384]], axis=1
        )
        split_rows(mm_nt(rows, weight), (near, f1, f2, f3), cols)


def last_rows_back_kernel(
    dq_ref, down_ref, dother_ref, own0, own1, far0, far1, all_ref, n0, n1, n2, n3, n4,
    near, f1, f2, f3, norms,
):
    own, far = Tall(own0, own1), Tall(far0, far1)
    dq = jnp.concatenate([dq_ref[k] for k in range(RING)], axis=0)
    rows = jnp.concatenate([dq, keys_total(down_ref, dother_ref)], axis=1)
    for n, ref in enumerate((n0, n1, n2, n3, n4), 1):
        norms[2 * n : 2 * n + 2] = ref[...]
    norms[12:16] = jnp.zeros((4, 1024), F32)
    for cols in chunks():
        weight = jnp.concatenate(
            [own[cols, 0:128], far[cols, 0:128], own[cols, 128:384], far[cols, 128:384]], axis=1
        )
        total = mm_nt(rows, weight)
        near[:, cols] = total[0:BLOCK]
        for k, out in enumerate((f1, f2, f3), 1):
            out[0:BLOCK, cols] = total[BLOCK * k : BLOCK * (k + 1)].astype(BF16)
        norms[0:1, cols] = jnp.sum(total * all_ref[:, cols].astype(F32), axis=0, keepdims=True)
        norms[1:2, cols] = jnp.sum(total, axis=0, keepdims=True)
    for out in (f1, f2, f3):
        out[BLOCK : BLOCK + 16] = norms[...].astype(BF16)


def last_sum_back_kernel(dv_ref, near, r1, r2, r3, s_ref, r_ref, rows, norms, g_out, total):
    da = near[...]
    for ref in (r1, r2, r3):
        da = da + ref[0:BLOCK].astype(F32)
    standard = s_ref[...]
    scaled = da * rows[0:1]
    inner = (
        scaled
        - jnp.mean(scaled, axis=-1, keepdims=True)
        - standard * jnp.mean(scaled * standard, axis=-1, keepdims=True)
    )
    g_out[...] = (dv_ref[...].astype(F32) + inner * r_ref[...]).astype(BF16)
    total[...] = norms[...] + sum(ref[BLOCK : BLOCK + 16].astype(F32) for ref in (r1, r2, r3))


def cross_cols(w, layer, place, g, at, rows):
    first = RING * block_of(place, g)
    parts = [
        w[2 * (first + y) + layer, :, at : at + 128]
        for y in range(rows.start // 256, rows.stop // 256)
    ]
    return parts[0] if len(parts) == 1 else jnp.concatenate(parts, axis=0)


def cross_blocks(w, layer, place, g, cols):
    first = RING * block_of(place, g)
    parts = []
    for c in range(cols.start, cols.stop, 128):
        at = c % 256
        parts.append(w[2 * (first + c // 256) + layer, at : at + 128, 128:256])
    return jnp.concatenate(parts, axis=1)


def cross_mask(scores, length):
    slots = lax.broadcasted_iota(jnp.int32, scores.shape, 0)
    return jnp.where(slots < length, scores, NEG_FILL)


def cross_forward_kernel(layer, place, lengths, mine, theirs, *refs):
    w, kv, (q_ref, o_ref, lse_ref, near, far) = refs[0], refs[1:5], refs[5:]
    rows = stack_rows((mine, theirs))
    for g in range(RING):
        lanes = slice(128 * g, 128 * g + 128)
        q_ref[:, lanes] = mm(rows, cross_cols(w, layer, place, g, 0, slice(0, 1024))).astype(BF16)
        outs = []
        for p in range(2):
            h = 2 * g + p
            q = q_ref[:, HD * h : HD * h + HD] * 0.125
            k = kv[g][layer, :, HD * p : HD * p + HD]
            v = kv[g][layer, :, 128 + HD * p : 128 + HD * p + HD]
            scores = cross_mask(mm_nt(k, q), lengths[place[4], 0])
            top = jnp.max(scores, axis=0, keepdims=True)
            raised = jnp.exp(scores - top)
            total = jnp.sum(raised, axis=0, keepdims=True)
            outs.append(mm_tn(v, raised.astype(BF16)) / total)
            lse_ref[h] = top + jnp.log(total)
        o_ref[:, lanes] = jnp.concatenate(outs, axis=0).T.astype(BF16)
    for cols in chunks():
        weight = jnp.concatenate([cross_blocks(w, layer, place, g, cols) for g in range(RING)], axis=0)
        split_rows(mm(o_ref[...], weight), (near, far), cols)


def cross_back_kernel(layer, place, lengths, mine, theirs, *refs):
    w, kv, (q_ref, lse_ref) = refs[0], refs[1:5], refs[5:7]
    dq_ref, dkv, (near, far) = refs[7], refs[8:12], refs[12:14]
    rows = stack_rows((mine, theirs))
    for g in range(RING):
        lanes = slice(128 * g, 128 * g + 128)
        dmixed = mm_nt(rows, cross_blocks(w, layer, place, g, ALL_COLS)).astype(BF16)
        dqs, dks, dvs = [], [], []
        for p in range(2):
            h = 2 * g + p
            q = q_ref[:, HD * h : HD * h + HD] * 0.125
            do = dmixed[:, HD * p : HD * p + HD]
            k = kv[g][layer, :, HD * p : HD * p + HD]
            v = kv[g][layer, :, 128 + HD * p : 128 + HD * p + HD]
            probs = jnp.exp(cross_mask(mm_nt(k, q), lengths[place[4], 0]) - lse_ref[h])
            dprobs = mm_nt(v, do)
            delta = jnp.sum(probs * dprobs, axis=0, keepdims=True)
            dscores = (probs * (dprobs - delta)).astype(BF16)
            dqs.append(mm_tn(k, dscores) * 0.125)
            dks.append(mm(dscores, q))
            dvs.append(mm(probs.astype(BF16), do))
        dq_ref[:, lanes] = jnp.concatenate(dqs, axis=0).T.astype(BF16)
        dkv[g][...] = jnp.concatenate(dks + dvs, axis=1).astype(BF16)
    for cols in chunks():
        weight = jnp.concatenate([cross_cols(w, layer, place, g, 0, cols) for g in range(RING)], axis=1)
        split_rows(mm_nt(dq_ref[...], weight), (near, far), cols)


def up_cols(own, far, at):
    refs, at = (own, at) if at < 512 else (far, at - 512)
    return jnp.concatenate([ref[:, at : at + CHUNK] for ref in refs], axis=0)


def up_rows(own, far, cols):
    half, rows = cols.start // 512, slice(cols.start % 512, cols.start % 512 + CHUNK)
    return jnp.concatenate([own[half][rows, 0:512], far[half][rows, 0:512]], axis=1)


def down_rows(own, far, at):
    refs, at = (own, at) if at < 512 else (far, at - 512)
    return jnp.concatenate([ref[at : at + CHUNK, 512:1024] for ref in refs], axis=1)


def down_cols(own, far, at):
    half, lanes = at // 512, slice(512 + at % 512, 512 + at % 512 + CHUNK)
    return jnp.concatenate([own[half][:, lanes], far[half][:, lanes]], axis=0)


def ffn_forward_kernel(
    a0, a1, a2, a3, own0, own1, far0, far1, hidden_ref, slope_ref, near, f1, f2, f3
):
    own, far = (own0, own1), (far0, far1)
    root = 0.7978845608028654
    rows = stack_rows((a0, a1, a2, a3))
    for cols in chunks():
        pre = mm(rows, up_cols(own, far, cols.start))
        square = pre * pre
        t = jnp.tanh(root * (pre + 0.044715 * pre * square))
        half = 0.5 * (1.0 + t)
        hidden_ref[:, cols] = (pre * half).astype(BF16)
        slope_ref[:, cols] = half + 0.5 * pre * (1.0 - t * t) * (root * (1.0 + 3 * 0.044715 * square))
    for cols in chunks():
        split_rows(mm(hidden_ref[...], down_cols(own, far, cols.start)), (near, f1, f2, f3), cols)


def ffn_back_kernel(
    g0, g1, g2, g3, own0, own1, far0, far1, slope_ref, dpre_ref, near, f1, f2, f3
):
    own, far = (own0, own1), (far0, far1)
    rows = stack_rows((g0, g1, g2, g3))
    for cols in chunks():
        dhidden = mm_nt(rows, down_rows(own, far, cols.start))
        dpre_ref[:, cols] = (dhidden * slope_ref[:, cols]).astype(BF16)
    for cols in chunks():
        split_rows(mm_nt(dpre_ref[...], up_rows(own, far, cols)), (near, f1, f2, f3), cols)


def ffn_grads_kernel(hidden, g0, g1, g2, g3, dpre, a0, a1, a2, a3, ours, t0, t1, t2, t3):
    theirs = (t0, t1, t2, t3)
    g = stack_rows((g0, g1, g2, g3))
    a = stack_rows((a0, a1, a2, a3))
    for n in (2, 3, 0, 1):
        down = mm_tn(hidden[:, CHUNK * n : CHUNK * n + CHUNK], g)
        if n >= 2:
            theirs[n - 2][...] = down.astype(BF16)
        else:
            ours[CHUNK * n : CHUNK * n + CHUNK] = down
    for half in (1, 0):
        for n in range(4):
            up = mm_tn(a[:, CHUNK * n : CHUNK * n + CHUNK], dpre[:, 512 * half : 512 * half + 512])
            lanes = slice(512 * (n // 2), 512 * (n // 2) + 512)
            if half:
                theirs[2 + n % 2][:, lanes] = up.astype(BF16)
            else:
                ours[512 + CHUNK * (n % 2) : 512 + CHUNK * (n % 2) + CHUNK, lanes] = up


def ffn_total(ours, came, rows):
    n, at = rows.start // CHUNK, rows.start % CHUNK
    return ours[rows] + came[n][at : at + rows.stop - rows.start].astype(F32)


def cross_shares(k, g, a, mixed, dq, keys, memory):
    lanes = slice(128 * k, 128 * k + 128)
    return mm_tn(dq[:, lanes], a), mm_tn(mixed[:, lanes], g), mm_tn(keys[...], memory)


def cross_grads_kernel(
    mixed, g_mine, g_theirs, dq, a_mine, a_theirs, k0, k1, k2, k3, b0, b1, b2, b3
):
    g = stack_rows((g_mine, g_theirs))
    a = stack_rows((a_mine, a_theirs))
    for k, (key, out) in enumerate(zip((k0, k1, k2, k3), (b0, b1, b2, b3))):
        lanes = slice(128 * k, 128 * k + 128)
        out[0:128] = mm_tn(dq[:, lanes], a).astype(out.dtype)
        out[128:256] = mm_tn(mixed[:, lanes], g).astype(out.dtype)
        for i in range(4):
            out[256:320, 256 * i : 256 * i + 256] = key[64 * i : 64 * i + 64].astype(out.dtype)


def cross_first_kernel(
    place, ours, q0, q1, q2, q3, mixed, g_mine, g_theirs, dq, a_mine, a_theirs, k0, k1, k2, k3,
    memory, out,
):
    g = stack_rows((g_mine, g_theirs))
    a = stack_rows((a_mine, a_theirs))
    for i in range(8):
        rows = slice(128 * i, 128 * i + 128)
        out[i, 0:128] = ffn_total(ours, (q0, q1, q2, q3), rows).astype(BF16)
    for k, key in enumerate((k0, k1, k2, k3)):
        queries, outs, keys = cross_shares(k, g, a, mixed, dq, key, memory[...])
        for i in range(8):
            part, at = (queries, outs)[i // 4], 32 * (i % 4)
            to = pl.multiple_of(128 + 64 * block_of(place, k), 64)
            out[i, pl.ds(to, 32)] = part[at : at + 32].astype(BF16)
            out[i, pl.ds(pl.multiple_of(to + 32, 32), 32)] = keys[32 * i : 32 * i + 32].astype(BF16)


def self_grads_kernel(
    mixed, g0, g1, g2, g3, dq, down_ref, dother_ref, a0, a1, a2, a3, ours, t0, t1, t2, t3
):
    g = stack_rows((g0, g1, g2, g3))
    a = stack_rows((a0, a1, a2, a3))
    keys = keys_total(down_ref, dother_ref)
    outs, queries = [jnp.concatenate([r[k] for k in range(RING)], axis=0) for r in (mixed, dq)]
    t0[...] = mm_tn(outs[:, 128:256], g).astype(BF16)
    t1[...] = mm_tn(queries[:, 128:256], a).astype(BF16)
    t2[...] = mm_tn(keys[:, 256:384], a).astype(BF16)
    t3[...] = mm_tn(keys[:, 384:512], a).astype(BF16)
    ours[0:128] = mm_tn(outs[:, 0:128], g)
    ours[128:256] = mm_tn(queries[:, 0:128], a)
    ours[256:512] = mm_tn(keys[:, 0:256], a)


def rows_kernel(place, x_ref, memory_ref, g_ref, x, both, g):
    mine = place[4]
    x[...] = x_ref[mine]
    both[0:BLOCK] = x_ref[mine]
    both[BLOCK : BLOCK + 32] = memory_ref[mine]
    g[...] = g_ref[mine]


def norm_rows_kernel(gain, bias, out):
    out[0:3] = gain[0]
    out[3:6] = bias[0]


def both_norms_kernel(place, mine, other, first, second):
    first[...] = jnp.where(place[4] == 0, mine[...], other[...])
    second[...] = jnp.where(place[4] == 0, other[...], mine[...])


def memory_blocks_kernel(x0, x1, x2, x3, out):
    for k, ref in enumerate((x0, x1, x2, x3)):
        out[32 * k : 32 * k + 32] = ref[BLOCK : BLOCK + 32]


def pack_kernel(place, w_ref, out_ref, q_ref, cross_ref, kv_ref, first, second, part, whole):
    for i in range(3):
        whole[:, 128 * i : 128 * i + 128] = w_ref[i]
    for i in range(8):
        rows = slice(128 * i, 128 * i + 128)
        whole[rows, 384:512] = out_ref[:, rows]
        whole[rows, 640:768] = cross_ref[:, rows]
    whole[:, 512:640] = q_ref[...]
    whole[:, 768:1024] = kv_ref[...]
    first[...] = whole[0:512, 0:512]
    second[...] = whole[512:1024, 0:512]
    part[...] = whole[pl.ds(pl.multiple_of(place[2] * 256, 256), 256)]


def pack_ffn_kernel(up_ref, down_ref, out):
    out[:, 0:512] = up_ref[...]
    out[0:512, 512:1024] = down_ref[:, 0:512]
    out[512:1024, 512:1024] = down_ref[:, 512:1024]


def quarter(place, k):
    return pl.ds(pl.multiple_of(lax.rem(place[2] - k + RING, RING) * 256, 256), 256)


def by_section(place, write):
    pl.when(place[4] == 0)(lambda: write(0, 1))
    pl.when(place[4] == 1)(lambda: write(1, 0))


def fill_halves(place, parts, halves, cols):
    for k, ref in enumerate(parts):
        y = lax.rem(place[2] - k + RING, RING)
        rows = pl.ds(pl.multiple_of(lax.rem(y, 2) * 256, 256), 256)

        def put(half, ref=ref, rows=rows):
            halves[half][rows] = ref[:, cols]

        pl.when(y < 2)(functools.partial(put, 0))
        pl.when(y >= 2)(functools.partial(put, 1))


def both_selfs_kernel(
    place, mine0, mine1, r0, r1, r2, r3, a0, a1, b0, b1
):
    def write(own, far):
        halves = ((a0, a1), (b0, b1))
        halves[own][0][...] = mine0[...]
        halves[own][1][...] = mine1[...]
        fill_halves(place, (r0, r1, r2, r3), halves[far], slice(0, 512))

    by_section(place, write)


def rest_kernel(place, mine, other, out, parts):
    def write(own, far):
        parts[own] = mine[:, 512:768]
        parts[far] = other[:, 512:768]

    by_section(place, write)
    out[:, 0:512] = other[:, 0:512]
    out[:, 512:768] = other[:, 768:1024]


def keys_kernel(place, kv_ref, k0, k1, k2, k3, x0, x1, x2, x3, e_far, out, memory, pair):
    for k, ref in enumerate((x0, x1, x2, x3)):
        at = 64 * block_of(place, k)
        memory[pl.ds(pl.multiple_of(at + 32 * place[1], 32), 32)] = ref[BLOCK : BLOCK + 32]
        memory[pl.ds(pl.multiple_of(at + 32 - 32 * place[1], 32), 32)] = e_far[32 * k : 32 * k + 32]
    for k, ref in enumerate((k0, k1, k2, k3)):
        pair[quarter(place, k)] = ref[:, 512:768]
    mine = mm(memory[...], kv_ref[...]).astype(BF16)
    other = mm(memory[...], pair[...]).astype(BF16)

    def write(own, far):
        out[own] = mine
        out[far] = other

    by_section(place, write)


def both_ffns_kernel(place, mine, other, a0, a1, b0, b1):
    def write(own, far):
        halves = ((a0, a1), (b0, b1))
        for half in range(2):
            rows = slice(512 * half, 512 * half + 512)
            halves[own][half][...] = mine[rows]
            halves[far][half][...] = other[rows]

    by_section(place, write)


def cut_chunks(place, total, outs):
    rows = total.shape[0] // 8
    for k, out in enumerate(outs):
        y = lax.rem(place[2] - k + RING, RING)
        for z in range(2):
            at = pl.ds(pl.multiple_of((RING * z + y) * rows, rows), rows)
            out[z] = total[at].astype(out.dtype)


def join_kernel(f, q0, q1, q2, q3, ours, t0, t1, t2, t3, out):
    for i in range(8):
        out[i, 0:128] = ffn_total(f, (q0, q1, q2, q3), slice(128 * i, 128 * i + 128)).astype(BF16)
        theirs = (t0, t1, t2, t3)[i // 2]
        at = 64 * (i % 2)
        out[i, 128:192] = (ours[64 * i : 64 * i + 64] + theirs[at : at + 64].astype(F32)).astype(BF16)


def rest_chunk_kernel(
    place, ours, t0, t1, t2, t3, w0, w1, w2, w3, memory, c0, c1, c2, c3, total
):
    cross = w0[...] + sum(w[...].astype(F32) for w in (w1, w2, w3))
    keys = jnp.concatenate([cross[256:320, 256 * i : 256 * i + 256] for i in range(4)], axis=0)
    keys = mm_tn(keys.astype(BF16), memory[...])
    for i in range(8):
        theirs = (t0, t1, t2, t3)[i // 2]
        at, to = 64 * (i % 2), 128 * i
        total[to : to + 64] = ours[64 * i : 64 * i + 64] + theirs[at : at + 64].astype(F32)
        total[to + 64 : to + 96] = cross[32 * i : 32 * i + 32]
        total[to + 96 : to + 128] = keys[32 * i : 32 * i + 32]
    cut_chunks(place, total, (c0, c1, c2, c3))


def split_kernel(grads, ffn, cross):
    ffn[...] = grads[0:128]
    cross[...] = grads[128:384]


def chunk_shapes(rows):
    return [Cold(struct((2, rows, 1024), F32))] + [struct((2, rows, 1024), BF16)] * 3


def sum_y_kernel(place, c0, r1, r2, r3, first, ffn, cross, keep, over_z, over_s):
    z = place[3]

    def half(n):
        return c0[n] + sum(r[n].astype(F32) for r in (r1, r2, r3))

    over_z[...] = half(1 - z).astype(BF16)
    rest = half(z)

    def write_first():
        keep[0:128] = rest
        keep[128:256] = first[0:128].astype(F32)
        over_s[0:64] = first[128:192]
        over_s[64:128] = cross[...]
        over_s[128:256] = ffn[...]

    def write_second():
        keep[0:64] = first[128:192].astype(F32)
        keep[64:128] = cross[...].astype(F32)
        keep[128:256] = ffn[...].astype(F32)
        over_s[0:128] = rest.astype(BF16)
        over_s[128:256] = first[0:128]

    pl.when(place[4] == 0)(write_first)
    pl.when(place[4] == 1)(write_second)


def sum_rest_kernel(place, keep, from_z, from_s, from_both, norms, came, out):
    rest = keep[0:128] + from_s[0:128].astype(F32)
    other = from_z[...].astype(F32) + from_both[...].astype(F32)
    out[0:128] = jnp.where(place[4] == 0, rest + other, rest).astype(BF16)
    out[128:144] = (norms[...] + came[...]).astype(BF16)
    out[144:272] = (keep[128:256] + from_s[128:256].astype(F32)).astype(BF16)


def exchange(over_z, over_s):
    from_both = lax.ppermute(over_z, ("section", "dz"), [(2, 1), (3, 0)])
    return swap(over_z, "dz"), swap(over_s, "section"), from_both


def norms_kernel(place, all_ref, keep, over_s):
    total = sum(all_ref[272 * i + 128 : 272 * i + 144].astype(F32) for i in range(8))
    first, second = total[0:6], total[6:12]
    keep[0:6] = jnp.where(place[4] == 0, first, second)
    over_s[0:6] = jnp.where(place[4] == 0, second, first)
    keep[6:8] = jnp.zeros((2, 1024), F32)
    over_s[6:8] = jnp.zeros((2, 1024), F32)


def last_norms_kernel(mine, came, gains, biases, ffn):
    norms = mine[...] + came[...]
    for j in range(2):
        gains[j : j + 1] = norms[2 * j : 2 * j + 1]
        biases[j : j + 1] = norms[2 * j + 1 : 2 * j + 2]
    ffn[...] = norms[4:6]


def last_kernel(
    all_ref, out_ref, self_ref, q_ref, cross_ref, kv_ref, up_ref, down_ref
):
    def rows(at, count, span):
        return jnp.concatenate(
            [all_ref[272 * i + at : 272 * i + at + span] for i in range(count, count + 128 // span)],
            axis=0,
        ).astype(F32)

    out_ref[...] = rows(0, 0, 64)
    for i in range(3):
        self_ref[i] = rows(0, 2 + 2 * i, 64).T
    q_ref[...] = rows(64, 0, 32).T
    cross_ref[...] = rows(64, 4, 32)
    kv_ref[pl.ds(0, 1024, stride=2)] = rows(96, 0, 32).T
    kv_ref[pl.ds(1, 1024, stride=2)] = rows(96, 4, 32).T
    for i in range(4):
        here = slice(128 * i, 128 * i + 128)
        down_ref[here] = rows(144, i, 128)
        up = rows(144, 4 + i, 128)
        up_ref[here] = up[:, 0:512]
        up_ref[512 + 128 * i : 640 + 128 * i] = up[:, 512:1024]


def other_layer_kernel(place, first, second, out):
    out[...] = jnp.where(place[4] == 0, second[...], first[...])


def both_batches_kernel(place, first, second, came, out):
    mine = place[4]
    out[mine] = jnp.where(mine == 0, first[...], second[...])
    out[1 - mine] = came[...]


def last_ffn_kernel(whole, up_ref, down_ref):
    down_ref[...] = whole[0:512].astype(F32)
    up_ref[0:512] = whole[512:1024, 0:512].astype(F32)
    up_ref[512:1024] = whole[512:1024, 512:1024].astype(F32)


def layer_forward(layer, v, first, weights, ffns, place, lengths, rows, after):
    own, far, cross, kv = weights
    heads = [struct((RING, BLOCK, 256), BF16), struct((RING, BLOCK, 512), BF16)]
    if layer == 0:
        q, kv_self, *rest = call(
            first_qkv_kernel,
            heads + cold(*[ROW16] * RING, ROW, COLUMN, struct((RING * BLOCK, 1024), BF16)),
            [*cold(*first, *own, *far), rows],
            after=after.get("qkv", ()),
        )
        full1, (s1, r1, all1) = rest[0:4], rest[4:7]
    else:
        a1, s1, r1, all1 = *first, None
        full1 = gather_x(a1)
        q, kv_self = call(qkv_kernel, heads, [*full1, *cold(*own, *far)], after=after.get("qkv", ()))
    kv_other = swap(kv_self, "core")
    if "keys" in after:
        after["keys"](q)
    mixed1, lse1, *sent = call(
        self_forward_kernel,
        cold_if(not layer, struct((RING, BLOCK, 256), BF16), struct((4, RING, 1, BLOCK), F32)) + SENT,
        [q, kv_self, kv_other, *cold(*own, *far)],
        scalars=[place],
        scratch=[pltpu.VMEM((KEYS, 256), BF16), pltpu.VMEM((KEYS, 256), BF16)],
        after=after.get("self", ()),
    )
    waits = after["sum1"](mixed1) if "sum1" in after else ()
    v1, a2, s2, r2 = sum_norm(1, v, sent[0], send_x(sent[1:]), rows, ROW, after=waits, new=not layer)
    a2_theirs = swap(a2, "core")
    cq, mixed2, lse2, near, far2 = call(
        functools.partial(cross_forward_kernel, layer),
        [
            struct((2 * BLOCK, 512), BF16),
            struct((2 * BLOCK, 512), BF16),
            struct((2 * RING, 1, 2 * BLOCK), F32),
            ROW,
            ROW16,
        ],
        [a2, a2_theirs, *cold(cross, *kv[0:4])],
        scalars=[place, lengths],
        after=after.get("cross", ()),
    )
    v2, a3, s3, r3 = sum_norm(
        2, v1, near, [swap(far2, "core")], rows, ROW, after=after.get("sum2", ()), old=not layer
    )
    full3 = gather_x(a3)
    hidden, slope, *sent = call(
        ffn_forward_kernel,
        [struct((RING * BLOCK, 1024), BF16), struct((RING * BLOCK, 1024), F32)] + SENT,
        [*full3, *cold(*ffns[layer])],
        after=after.get("ffn", ()),
    )
    stored = (
        (s1, r1, full1, q, kv_self, kv_other, mixed1, lse1, all1),
        (s2, r2, a2, a2_theirs, cq, mixed2, lse2),
        (s3, r3, full3, hidden, slope),
    )
    return v2, sent[0], send_x(sent[1:]), stored


def layer_back(layer, dv, full_g3, stored, weights, ffns, place, lengths, rows, steps):
    own, far, cross, kv = weights
    (s1, r1, full1, q, kv_self, kv_other, mixed1, lse1, all1), second, third = stored
    s2, r2, a2, a2_theirs, cq, mixed2, lse2 = second
    s3, r3, full3, hidden, slope = third
    old = layer == 0
    dpre, *sent = call(
        ffn_back_kernel,
        [struct((RING * BLOCK, 1024), BF16)] + SENT,
        [*full_g3, *cold(*ffns[layer]), *cold_if(old, slope)],
        after=steps.get("ffn", ()),
    )
    ffn_ours, *ffn_theirs = call(
        ffn_grads_kernel,
        [struct((1024, 1024), F32)] + [struct((CHUNK, 1024), BF16)] * 4,
        [*cold_if(old, hidden), *full_g3, dpre, *cold_if(old, *full3)],
    )
    ffn_parts = [ffn_ours, *(swap(part, "core") for part in ffn_theirs)]
    dv2, g2, norms3 = sum_back(
        2, dv, sent[0], send_x(sent[1:]), s3, r3, rows,
        after=[ffn_theirs[0], *steps.get("sum3", ())], old=old, new=old,
    )
    g2_theirs = swap(g2, "core")
    pair_keys = struct((2 * BLOCK, 256), BF16)
    dcq, *rest = call(
        functools.partial(cross_back_kernel, layer),
        [struct((2 * BLOCK, 512), BF16)] + [pair_keys] * RING + [ROW, ROW16],
        [g2, g2_theirs, *cold(cross, *kv[0:4]), *cold_if(old, cq, lse2)],
        scalars=[place, lengths],
        after=steps.get("cross", lambda parts, g2: ())(ffn_parts, g2),
    )
    dkv_cross, (near, far2) = rest[:RING], rest[RING:]
    dv1, g1, norms2 = sum_back(1, dv2, near, [swap(far2, "core")], s2, r2, rows, old=old, new=True)
    full_g1 = gather_x(g1)
    cross_grads = [*cold_if(old, mixed2), g2, g2_theirs, dcq, *cold_if(old, a2, a2_theirs), *dkv_cross]
    middle, waits = steps["middle"](ffn_parts, cross_grads, g1)
    dq, dkv_own, dkv_theirs = call(
        self_back_kernel,
        [
            struct((RING, BLOCK, 256), BF16),
            struct((RING, BLOCK, 512), F32),
            struct((RING, BLOCK, 512), BF16),
        ],
        [*full_g1, *cold(*own, *far, q, kv_self, kv_other, lse1)],
        scalars=[place],
        scratch=[
            pltpu.VMEM((KEYS, 256), BF16),
            pltpu.VMEM((KEYS, 256), BF16),
            pltpu.VMEM((RING, BLOCK, 256), BF16),
            pltpu.VMEM((KEYS, 256), F32),
            pltpu.VMEM((KEYS, 256), F32),
        ],
        after=waits,
    )
    back = [dq, dkv_own, swap(dkv_theirs, "core")]

    def self_grads(waits=()):
        ours, *theirs = call(
            self_grads_kernel,
            [struct((512, 1024), F32)] + [struct((BLOCK, 1024), BF16)] * 4,
            [*cold(mixed1), *full_g1, *back, *cold(*full1)],
            after=waits,
        )
        return [ours, *(swap(part, "core") for part in theirs)], theirs

    if layer == 0:
        self_parts, theirs = self_grads([*middle[1:4], *steps["before"]])
        waits = steps["late"](middle, self_parts, theirs)
        tall = struct((BLOCK + 16, 1024), BF16)
        near, *others, sums = call(
            last_rows_back_kernel,
            [ROW, tall, tall, tall, struct((16, 1024), F32)],
            [*back, *cold(*own, *far, all1, norms2, norms3, *steps["norms"])],
            after=waits,
        )
        steps["tail"]["near"] = near
        g0, sums = call(
            last_sum_back_kernel,
            [ROW16, struct((16, 1024), F32)],
            [*cold(dv1), near, *send_x(others), *cold(s1, r1, rows, sums)],
        )
        return g0, middle, self_parts, sums
    else:
        sent = call(self_rows_back_kernel, SENT, [*back, *cold(*own, *far)])
        self_parts, theirs = self_grads()
        waits = [theirs[0], *steps["late"]()]
    dv0, g0, norms1 = sum_back(
        0, dv1, sent[0], send_x(sent[1:]), s1, r1, rows, after=waits, old=True
    )
    return g0, middle, self_parts, (norms1, norms2, norms3)


def reduce_dp(grads):
    total = lax.psum_scatter(grads, ("dz", "dy"), scatter_dimension=0, tiled=True)
    return total.reshape(grads.shape[1:])


def shards(
    inputs,
    memory_states,
    source_lengths,
    cotangent,
    norm_gain,
    norm_bias,
    w_self,
    w_self_out,
    w_cross_q,
    w_cross_kv,
    w_cross_out,
    up_weight,
    down_weight,
):
    place = PLACE

    def along_y(part):
        return [part] + [shift(part, "dy", k) for k in range(1, RING)]

    row16 = struct((BLOCK, 1024), BF16)
    kv_mine = w_cross_kv[0].reshape(w_cross_kv.shape[1], -1)
    half = struct((512, 512), BF16)
    *self_mine, mine = call(
        pack_kernel,
        [*cold(half, half), struct((256, 1024), BF16)],
        cold(w_self[0].transpose(1, 0, 2), w_self_out[0], w_cross_q[0], w_cross_out[0], kv_mine),
        scalars=[place],
        scratch=[pltpu.VMEM((1024, 1024), BF16)],
    )
    other = swap(mine, "section")
    x, rows_first, g_top = call(
        rows_kernel,
        cold(row16, struct((BLOCK + 32, 1024), BF16), row16),
        cold(inputs[:, :, 0], memory_states[:, :, 0], cotangent[:, :, 0]),
        scalars=[place],
        after=[mine],
    )
    norms = call(
        norm_rows_kernel, [struct((6, 1024), F32)], [norm_gain, norm_bias], after=[mine]
    )[0]
    norms_other = swap(norms, "section")
    rows_first = gather_x(rows_first)
    ffn_half = struct((512, 1024), BF16)
    ffn_mine, ffn_done = call(
        pack_ffn_kernel,
        cold(struct((1024, 1024), BF16)),
        cold(up_weight[0], down_weight[0]),
        after=[other, *rows_first[1:]],
        token=True,
    )
    ffn_other = swap(ffn_mine, "section")
    norms = call(
        both_norms_kernel, [struct((6, 1024), F32)] * 2, [norms, norms_other], scalars=[place]
    )

    rest, parts = call(
        rest_kernel,
        [struct((256, 768), BF16), Cold(struct((2, 256, 256), BF16))],
        [mine, other],
        scalars=[place],
        after=[norms_other, *rows_first[1:]],
    )
    rests = along_y(rest)
    e_far = swap(call(memory_blocks_kernel, [row16], rows_first)[0], "core")
    a0, a1, b0, b1 = call(
        both_selfs_kernel,
        [half, half, *cold(half, half)],
        [*cold(*self_mine), *rests],
        scalars=[place],
        after=[e_far, norms[0], ffn_done],
    )
    selfs = [(a0, a1), (b0, b1)]
    selfs_far = [tuple(swap(w, "core") for w in pair) for pair in selfs]
    crosses = lax.all_gather(parts, ("tx", "dy"), axis=0, tiled=True)
    ffns, kvs = [], []

    def make_keys(q):
        keyed, memory = call(
            keys_kernel,
            cold(struct((2, 256, 256), BF16), struct((256, 1024), BF16)),
            cold(kv_mine, *rests, *rows_first, e_far),
            scalars=[place],
            scratch=[pltpu.VMEM((1024, 256), BF16)],
            after=[q],
        )
        kvs.extend(gather_x(keyed))
        kvs.append(memory)


    def made(mixed):
        a0, a1, b0, b1, done = call(
            both_ffns_kernel,
            cold(*[ffn_half] * 4),
            cold(ffn_mine, ffn_other),
            scalars=[place],
            after=[mixed],
            token=True,
        )
        for first, second in ((a0, a1), (b0, b1)):
            ffns.append((first, second, swap(first, "core"), swap(second, "core")))
        return [done]

    weights = [(selfs[i], selfs_far[i], crosses, kvs) for i in range(2)]

    v, near, far, stored0 = layer_forward(
        0, x, rows_first, weights[0], ffns, place, source_lengths, norms[0], {"keys": make_keys, "sum1": lambda mixed: [*kvs[1:4], *made(mixed)]}
    )
    text, *normed = sum_norm(0, v, near, far, norms[1], ROW16)
    v, near, far, stored1 = layer_forward(
        1, text, normed, weights[1], ffns, place, source_lengths, norms[1], {}
    )
    memory = kvs[4]
    full_top = gather_x(g_top)
    unit = call(sum_last_kernel, cold(ROW16), [*cold(v), near, *far])[0]

    def middle_second(ffn_parts, cross_grads, after):
        out, done = call(
            cross_first_kernel,
            cold(struct((8, 384, 1024), BF16)),
            [*ffn_parts, *cross_grads, *cold(memory)],
            scalars=[place],
            after=[after],
            token=True,
        )
        return out, [done]

    def by_layer(first, second, after=()):
        lacks = call(other_layer_kernel, [row16], cold(first, second), scalars=[place], after=after)[0]
        return [*cold(first, second), swap(lacks, "section")]

    def both_batches(parts, after=()):
        return call(
            both_batches_kernel,
            cold(struct((2, BLOCK, 1024), BF16)),
            parts,
            scalars=[place],
            after=after,
        )[0]

    states = by_layer(text, unit, ())
    text_grad, grads_a, self1, norms1 = layer_back(
        1, g_top, full_top, stored1, weights[1], ffns, place, source_lengths, norms[1],
        {
            "ffn": full_top[1:],
            "sum3": [unit],
            "middle": middle_second,
            "late": lambda: (),
        },
    )
    grads_a = reduce_dp(grads_a)

    tail = {}

    def join(ffn_parts, g2):
        tail["joined"], done = call(
            join_kernel,
            cold(struct((8, 192, 1024), BF16)),
            [*ffn_parts, *self1],
            after=[g2],
            token=True,
        )
        return [done]

    def middle_first(ffn_parts, cross_grads, after):
        own, *sent = call(
            cross_grads_kernel,
            [struct((320, 1024), F32)] + [struct((320, 1024), BF16)] * 3,
            cross_grads,
            after=[after],
        )
        return [own, *send_x(sent)], [own]

    def late_first(cross_parts, self_parts, theirs):
        tail["chunks"] = call(
            rest_chunk_kernel,
            chunk_shapes(128),
            [*self_parts, *cross_parts, *cold(memory)],
            scalars=[place],
            scratch=[pltpu.VMEM((1024, 1024), F32)],
        )
        return [tail["chunks"][0]]

    input_grad, _, _, norms = layer_back(
        0, text_grad, gather_x(text_grad), stored0, weights[0], ffns, place, source_lengths, norms[0],
        {
            "cross": join,
            "middle": middle_first,
            "late": late_first,
            "norms": norms1,
            "tail": tail,
            "before": [states[2]],
        },
    )
    grads_b = reduce_dp(tail["joined"])
    ffn1, cross1 = call(
        split_kernel,
        cold(row16, struct((256, 1024), BF16)),
        cold(grads_a),
        after=[tail["near"]],
    )
    cross1 = lax.psum_scatter(cross1, "tx", scatter_dimension=0, tiled=True)
    chunks_of = tail["chunks"]
    arrived = [shift(c, "dy", -k) for k, c in enumerate(chunks_of[1:], 1)]
    two = struct((256, 1024), F32)
    keep, over_z, over_s = call(
        sum_y_kernel,
        [Cold(two), row16, struct((256, 1024), BF16)],
        [*cold(chunks_of[0]), *arrived, *cold(grads_b, ffn1, cross1)],
        scalars=[place],
        after=[tail["near"]],
    )
    last = call(
        sum_rest_kernel,
        cold(struct((272, 1024), BF16)),
        [*cold(keep), *exchange(over_z, over_s), norms, swap(norms, "core")],
        scalars=[place],
    )[0]
    whole = lax.all_gather(last, ("dz", "dy"), axis=0, tiled=True)
    states = both_batches(states)
    input_parts = by_layer(input_grad, text_grad, ())
    eight, pair32 = struct((8, 1024), F32), struct((2, 1024), F32)
    own, over_s = call(
        norms_kernel, [eight] * 2, cold(whole), scalars=[place], after=[states]
    )
    grad_out, grad_self, grad_cq, grad_co, grad_ckv, grad_up, grad_down, done = call(
        last_kernel,
        cold(
            struct((128, 1024), F32),
            struct((3, 1024, 128), F32),
            struct((1024, 128), F32),
            struct((128, 1024), F32),
            struct((2048, 128), F32),
            struct((1024, 512), F32),
            struct((512, 1024), F32),
        ),
        cold(whole),
        after=[own],
        token=True,
    )
    input_grads = both_batches(input_parts, [done])
    grad_gain, grad_bias, grad_ffn = call(
        last_norms_kernel, [pair32] * 3, [own, swap(over_s, "section")], after=[done]
    )
    return (
        states[None, :, :, None],
        input_grads[None, :, :, None],
        grad_gain[None],
        grad_bias[None],
        grad_ffn[None],
        grad_self.transpose(1, 0, 2)[None],
        grad_out[None],
        grad_cq[None],
        grad_ckv.reshape(1, 1024, 2, 128),
        grad_co[None],
        grad_up[None],
        grad_down[None],
    )


def solution(mesh):
    sections = mesh.devices.shape[0]
    fine = Mesh(
        mesh.devices.reshape(sections, 2, RING, RING, 2), ("section", "dz", "dy", "tx", "core")
    )
    dp, tensor = ("dz", "dy"), ("tx", "core")
    rows = P(None, tensor, dp, None)
    return jax.shard_map(
        shards,
        mesh=fine,
        in_specs=(
            rows,
            rows,
            P(None, dp),
            rows,
            P("section", None, None),
            P("section", None, None),
            P("section", None, None, tensor),
            P("section", tensor, None),
            P("section", None, tensor),
            P("section", None, None, tensor),
            P("section", tensor, None),
            P("section", None, tensor),
            P("section", tensor, None),
        ),
        out_specs=(
            P("section", None, tensor, dp, None),
            P("section", None, tensor, dp, None),
            P("section", None, None),
            P("section", None, None),
            P("section", None, None),
            P("section", None, None, tensor),
            P("section", tensor, None),
            P("section", None, tensor),
            P("section", None, None, tensor),
            P("section", tensor, None),
            P("section", None, tensor),
            P("section", tensor, None),
        ),
        check_vma=False,
    )
```

time: 683 us -> 613 us (0.90)
  Pallas kernels: 39.2 us -> 180 us
  matrix products: 81.2 us -> 0 us
  starting transfers between devices: 161 us -> 119 us
  other arithmetic: 31.8 us -> 0 us
  waiting for transfers between devices: 301 us -> 276 us
  local copies, waits for them, and re-layouts: 26.7 us -> 13.2 us
  blocking collectives: 13.3 us -> 0 us
    pallas_call x8 -> x56, Pallas kernels: 39.2 us -> 180 us  [call(): pl.pallas_call(body, name=name, out_shape=[pltpu.HBM(o.shape, o.dtype) if...]
    dot_general x90 -> x0, matrix products: 81.2 us -> none  [dot(): lax.dot_general(a, b, ((dims[0], dims[1]), ((), ())), preferred_element_t...]
    ppermute x136 -> x106, waiting for transfers between devices: 283 us -> 227 us  [shift(): lax.ppermute(value, axis, [(i, (i + steps) % count) for i in range(count)])]
    ppermute x136 -> x106, starting transfers between devices: 160 us -> 118 us  [shift(): lax.ppermute(value, axis, [(i, (i + steps) % count) for i in range(count)])]
    all_gather x2, waiting for transfers between devices: 18.4 us -> 49.5 us  [the longest x1 49.5 us: shards(): whole = lax.all_gather(last, ('dz', 'dy'), axis=0, tiled=True)]
    all_gather x1 -> x0, blocking collectives: 13.3 us -> none  [shards(): lax.all_gather(pick(memory_states)[:, 0], ('tx', 'core'), axis=0, tiled=T...]
    convert_element_type x17 -> x0, other arithmetic: 8.8 us -> none  [the longest x2 2.62 us: finish(): total = (mine + swap(theirs, 'section').astype(F32)).astype(BF16)]
    select_n x14 -> x0, other arithmetic: 8.33 us -> none  [the longest x11 5.92 us: both_layers(): return (jnp.where(is_first, mine, other), jnp.where(is_first, other, mine))]
  transfers between devices with their start and end apart: 142 -> 112, of which waited for: 70 -> 61; matrix products, arithmetic and copies ran while one was open for 16% -> 0% of each run, Pallas kernels for 5% -> 25%
where the time goes in v2:
time: 613 us; the launch traced here: 605 us
  waiting for transfers between devices  276 us (45%)
  Pallas kernels  180 us (29%)
  starting transfers between devices  119 us (19%)
  between operations  15.5 us (3%)
  local copies, waits for them, and re-layouts  13.2 us (2%)
    ppermute x106, waiting for transfers between devices, shift(): lax.ppermute(value, axis, [(i, (i + steps) % count) for i in range(count)])  227 us
    pallas_call x56, Pallas kernels, call(): pl.pallas_call(body, name=name, out_shape=[pltpu.HBM(o.shape, o.dtype) if...  180 us
    ppermute x106, starting transfers between devices, shift(): lax.ppermute(value, axis, [(i, (i + steps) % count) for i in range(count)])  118 us
    all_gather x1, waiting for transfers between devices, shards(): whole = lax.all_gather(last, ('dz', 'dy'), axis=0, tiled=True)  49.5 us
    unnamed x152, local copies, waits for them, and re-layouts  13.2 us
  transfers between devices with their start and end apart: 112, of which 61 were waited for; matrix products, arithmetic and copies ran while one was open for 0% of the time, Pallas kernels for 25%

profile of v2, /device:TPU:1, one launch (start us, length us, event | category | flops | bytes accessed | tf_op | source)
XLA Modules:
  0.0 604.9 jit_solution(11104408809914866431)
XLA Ops:
  29.1 7.7 %collective-permute-done.1.refs_4_.refs_2_.refs_7_ = bf16[160,1024]{1,0:T(8,128)(2,1)S(1)} collective-permute-done((bf16[160,1024]{1,0:T(8,128)(2,1)}, bf16[160,1024]{1,0:T(8,128)(2,1)S(1)}, u32[]{:S(2)}, u32[]{:S(2)}) %collective-permute-start.1) | collective-permute-done | bytes 327712 | tf_op jit(solution)/shard_map/ppermute | solution.py:22
  51.4 13.8 %collective-permute-done.6.refs_4_.refs_3_ = bf16[256,768]{1,0:T(8,128)(2,1)S(1)} collective-permute-done((bf16[256,768]{1,0:T(8,128)(2,1)S(1)}, bf16[256,768]{1,0:T(8,128)(2,1)S(1)}, u32[]{:S(2)}, u32[]{:S(2)}) %collective-permute-start.6) | collective-permute-done | bytes 393248 | tf_op jit(solution)/shard_map/ppermute | solution.py:22
  86.7 7.3 %self_forward_kernel.2 = (bf16[4,128,256]{2,1,0:T(8,128)(2,1)}, f32[4,4,1,128]{3,2,1,0:T(1,128)}, f32[128,1024]{1,0:T(8,128)S(1)}, bf16[128,1024]{1,0:T(8,128)(2...) custom-call(bf16[4,128,256]{2,1,0:T(8,128)(2,1)S(1)} %get-tuple-element.215.refs_0_.refs_10_.refs_8_, ...), custom_call_target="tpu_custom_call" | custom-call | tf_op jit(solution)/shard_map/self_forward_kernel/pallas_call | solution.py:146
  113.2 5.2 collective-permute-done.14.refs_4_
  121.5 6.6 %cross_forward_kernel.2 = (bf16[256,512]{1,0:T(8,128)(2,1)S(1)}, bf16[256,512]{1,0:T(8,128)(2,1)S(1)}, f32[8,1,256]{2,1,0:T(1,128)S(1)}, f32[128,1024]{1,0:T(8,128)S(1)}, bf16[128,1024]{1,0:T(8,128)(2,1)S(1)}) custom-call(s32[2,1]{1,0:T(2,128)S(1)} %copy.35.refs_0_, bf16[128,1024]{1,0:T(8,128)(2,1)S(1)} %get-tuple-element.226.refs_1_.refs_4_, ...), custom_call_target="tpu_custom_call" | custom-call | tf_op jit(solution)/shard_map/cross_forward_kernel/pallas_call | solution.py:146
  135.5 5.5 collective-permute-done.21.refs_1_.refs_7_
  146.7 5.7 ffn_forward_kernel.2
  158.6 8.9 %collective-permute-done.26.refs_2_ = bf16[128,1024]{1,0:T(8,128)(2,1)S(1)} collective-permute-done((bf16[128,1024]{1,0:T(8,128)(2,1)S(1)}, bf16[128,1024]{1,0:T(8,128)(2,1)S(1)}, u32[]{:S(2)}, u32[]{:S(2)}) %collective-permute-start.26) | collective-permute-done | bytes 262176 | tf_op jit(solution)/shard_map/ppermute | solution.py:22
  175.5 11.1 %collective-permute-done.29.refs_1_.refs_9_ = bf16[128,1024]{1,0:T(8,128)(2,1)S(1)} collective-permute-done((bf16[128,1024]{1,0:T(8,128)(2,1)S(1)}, bf16[128,1024]{1,0:T(8,128)(2,1)S(1)}, u32[]{:S(2)}, u32[]{:S(2)}) %collective-permute-start.29) | collective-permute-done | bytes 262176 | tf_op jit(solution)/shard_map/ppermute | solution.py:22
  193.3 6.9 %self_forward_kernel.3 = (bf16[4,128,256]{2,1,0:T(8,128)(2,1)S(1)}, f32[4,4,1,128]{3,2,1,0:T(1,128)S(1)}, f32[128,1024]{1,0:T(8,128)S(1)}, bf16[128,1024]{1,0:T(...) custom-call(bf16[4,128,256]{2,1,0:T(8,128)(2,1)S(1)} %get-tuple-element.243.refs_0_.refs_8_, ...), custom_call_target="tpu_custom_call" | custom-call | tf_op jit(solution)/shard_map/self_forward_kernel/pallas_call | solution.py:146
  211.2 6.0 collective-permute-done.37.refs_4_
  219.6 6.6 %cross_forward_kernel.3 = (bf16[256,512]{1,0:T(8,128)(2,1)S(1)}, bf16[256,512]{1,0:T(8,128)(2,1)S(1)}, f32[8,1,256]{2,1,0:T(1,128)S(1)}, f32[128,1024]{1,0:T(8,128)S(1)}, bf16[128,1024]{1,0:T(8,128)(2,1)S(1)}) custom-call(s32[2,1]{1,0:T(2,128)S(1)} %copy.35.refs_0_, bf16[128,1024]{1,0:T(8,128)(2,1)S(1)} %get-tuple-element.250.refs_1_.refs_9_, ...), custom_call_target="tpu_custom_call" | custom-call | tf_op jit(solution)/shard_map/cross_forward_kernel/pallas_call | solution.py:146
  242.9 5.6 ffn_forward_kernel.3
  271.6 6.5 %collective-permute-done.54.refs_4_ = bf16[128,1024]{1,0:T(8,128)(2,1)S(1)} collective-permute-done((bf16[128,1024]{1,0:T(8,128)(2,1)S(1)}, bf16[128,1024]{1,0:T(8,128)(2,1)S(1)}, u32[]{:S(2)}, u32[]{:S(2)}) %collective-permute-start.54) | collective-permute-done | bytes 262176 | tf_op jit(solution)/shard_map/ppermute | solution.py:22
  281.4 8.0 %cross_back_kernel.2 = (bf16[256,512]{1,0:T(8,128)(2,1)S(1)}, bf16[256,256]{1,0:T(8,128)(2,1)S(1)}, bf16[256,256]{1,0:T(8,128)(2,1)S(1)}, bf16[256,256]{1,0:T(8,...) custom-call(s32[2,1]{1,0:T(2,128)S(1)} %copy.35.refs_0_, ...), custom_call_target="tpu_custom_call" | custom-call | tf_op jit(solution)/shard_map/cross_back_kernel/pallas_call | solution.py:146
  292.4 5.3 cross_first_kernel.1
  301.1 5.4 collective-permute-done.57.refs_1_.refs_2_
  306.5 6.0 collective-permute-done.58.refs_2_.refs_3_
  312.5 9.8 %self_back_kernel.2 = (bf16[4,128,256]{2,1,0:T(8,128)(2,1)S(1)}, f32[4,128,512]{2,1,0:T(8,128)S(1)}, bf16[4,128,512]{2,1,0:T(8,128)(2,1)S(1)}) custom-call(bf16[128,1024]{1,0:T(8,128)(2,1)S(1)} %get-tuple-element.281.refs_16_.refs_0_.refs_1_, bf16[128,1024]{1,0:T(8,128)(2,1)S(1)} %collective-permute-done.57.refs_1_.refs_2_, ...), custom_call_target="tpu_custom_call" | custom-call | tf_op jit(solution)/shard_map/self_back_kernel/pallas_call | solution.py:146
  339.4 5.9 collective-permute-done.67.refs_4_
  352.5 10.0 %collective-permute-done.68.refs_1_.refs_2_ = bf16[128,1024]{1,0:T(8,128)(2,1)S(1)} collective-permute-done((bf16[128,1024]{1,0:T(8,128)(2,1)S(1)}, bf16[128,1024]{1,0:T(8,128)(2,1)S(1)}, u32[]{:S(2)}, u32[]{:S(2)}) %collective-permute-start.68) | collective-permute-done | bytes 262176 | tf_op jit(solution)/shard_map/ppermute | solution.py:22
  364.0 5.3 ffn_back_kernel.3
  377.4 6.1 %collective-permute-start.77 = (bf16[256,1024]{1,0:T(8,128)(2,1)S(1)}, bf16[256,1024]{1,0:T(8,128)(2,1)S(1)}, u32[]{:S(2)}, u32[]{:S(2)}) collective-permute-start(bf16[256,1024]{1,0:T(8,128)(2,1)S(1)} %get-tuple-element.323), channel_id=1, source_target_pairs={{0,1},{1,0},{2,3},{3,2},{4,5},{5,4},{6,7},{7,6},{8,9},{9,8},{10,11... | collective-permute-start | bytes 1572872 | tf_op jit(solution)/shard_map/ppermute | solution.py:22
  393.5 8.1 %cross_back_kernel.3 = (bf16[256,512]{1,0:T(8,128)(2,1)S(1)}, bf16[256,256]{1,0:T(8,128)(2,1)S(1)}, bf16[256,256]{1,0:T(8,128)(2,1)S(1)}, bf16[256,256]{1,0:T(8,...) custom-call(s32[2,1]{1,0:T(2,128)S(1)} %copy.35.refs_0_, ...), custom_call_target="tpu_custom_call" | custom-call | tf_op jit(solution)/shard_map/cross_back_kernel/pallas_call | solution.py:146
  413.1 21.5 %collective-permute-done.84.refs_1_.refs_2_ = bf16[128,1024]{1,0:T(8,128)(2,1)S(1)} collective-permute-done((bf16[128,1024]{1,0:T(8,128)(2,1)S(1)}, bf16[128,1024]{1,0:T(8,128)(2,1)S(1)}, u32[]{:S(2)}, u32[]{:S(2)}) %collective-permute-start.84) | collective-permute-done | bytes 262176 | tf_op jit(solution)/shard_map/ppermute | solution.py:22
  434.6 9.8 %self_back_kernel.3 = (bf16[4,128,256]{2,1,0:T(8,128)(2,1)S(1)}, f32[4,128,512]{2,1,0:T(8,128)S(1)}, bf16[4,128,512]{2,1,0:T(8,128)(2,1)S(1)}) custom-call(bf16[128,1024]{1,0:T(8,128)(2,1)S(1)} %get-tuple-element.335.refs_10_.refs_0_.refs_1_, bf16[128,1024]{1,0:T(8,128)(2,1)S(1)} %collective-permute-done.84.refs_1_.refs_2_, ...), custom_call_target="tpu_custom_call" | custom-call | tf_op jit(solution)/shard_map/self_back_kernel/pallas_call | solution.py:146
  449.5 6.6 %collective-permute-done.48.refs_2_.refs_15_ = bf16[128,1024]{1,0:T(8,128)(2,1)S(1)} collective-permute-done((bf16[128,1024]{1,0:T(8,128)(2,1)S(1)}, bf16[128,1024]{1,0:T(8,128)(2,1)S(1)}, u32[]{:S(2)}, u32[]{:S(2)}) %collective-permute-start.48) | collective-permute-done | bytes 262176 | tf_op jit(solution)/shard_map/ppermute | solution.py:22
  483.3 6.6 %collective-permute-done.100.refs_2_ = bf16[2,128,1024]{2,1,0:T(8,128)(2,1)S(1)} collective-permute-done((bf16[2,128,1024]{2,1,0:T(8,128)(2,1)}, bf16[2,128,1024]{2,1,0:T(8,128)(2,1)S(1)}, u32[]{:S(2)}, u32[]{:S(2)}) %collective-permute-start.100) | collective-permute-done | bytes 524320 | tf_op jit(solution)/shard_map/ppermute | solution.py:22
  489.9 11.9 %collective-permute-done.101.refs_3_ = bf16[2,128,1024]{2,1,0:T(8,128)(2,1)S(1)} collective-permute-done((bf16[2,128,1024]{2,1,0:T(8,128)(2,1)}, bf16[2,128,1024]{2,1,0:T(8,128)(2,1)S(1)}, u32[]{:S(2)}, u32[]{:S(2)}) %collective-permute-start.101) | collective-permute-done | bytes 524320 | tf_op jit(solution)/shard_map/ppermute | solution.py:22
  517.0 7.5 %collective-permute-done.97.refs_4_ = bf16[144,1024]{1,0:T(8,128)(2,1)S(1)} collective-permute-done((bf16[144,1024]{1,0:T(8,128)(2,1)S(1)}, bf16[144,1024]{1,0:T(8,128)(2,1)S(1)}, u32[]{:S(2)}, u32[]{:S(2)}) %collective-permute-start.97) | collective-permute-done | bytes 294944 | tf_op jit(solution)/shard_map/ppermute | solution.py:22
  533.7 49.5 %all-gather.5.cloned.1.call-done.refs_0_ = bf16[2176,1024]{1,0:T(8,128)(2,1)} async-done(((bf16[272,1024]{1,0:T(8,128)(2,1)}), bf16[2176,1024]{1,0:T(8,128)(2,1)}) %all-gather.5.cloned.1.call-update) | async-done | bytes 4456464 | tf_op jit(solution)/shard_map/all_gather | solution.py:1305
  589.3 6.1 %last_kernel.1 = (f32[128,1024]{1,0:T(8,128)}, f32[3,1024,128]{2,1,0:T(8,128)}, f32[1024,128]{1,0:T(8,128)}, f32[128,1024]{1,0:T(8,128)}, f32[2048,128]{1,0:T(8,...) custom-call(bf16[2176,1024]{1,0:T(8,128)(2,1)} %all-gather.5.cloned.1.call-done.refs_0_, ...), custom_call_target="tpu_custom_call" | custom-call | tf_op jit(solution)/shard_map/last_kernel/pallas_call | solution.py:146
  (405 shorter events, 296.4 us)
Async XLA Ops:
  7.2 114.4 %all-gather.3.cloned.1.call-start = ((), (), s32[]{:S(2)}) async-start(), calls=%async_computation.3 | async-start | bytes 4456448 | tf_op jit(solution)/shard_map/all_gather | solution.py:1161
  12.2 24.6 %collective-permute-start.3 = (bf16[256,1024]{1,0:T(8,128)(2,1)S(1)}, bf16[256,1024]{1,0:T(8,128)(2,1)S(1)}, u32[]{:S(2)}, u32[]{:S(2)}) collective-permute-start(bf16[256,1024]{1,0:T(8,128)(2,1)S(1)} %get-tuple-element.205.refs_3_.refs_2_.refs_0_), channel_id=1, source_target_pairs={{0,64},{64,0},{1,65},{65,1},{2,66},{66,2},{3,67},{67,3},{4,68},{68... | collective-permute-start | bytes 1572872 | tf_op jit(solution)/shard_map/ppermute | solution.py:22
  37.7 435.1 %reduce-scatter.6.cloned.1.call-start = ((), (), s32[]{:S(2)}) async-start(), calls=%async_computation.5 | async-start | bytes 7077888 | tf_op jit(solution)/shard_map/reduce_scatter | solution.py:1083
  40.9 57.1 %collective-permute-start.18 = (bf16[1024,1024]{1,0:T(8,128)(2,1)}, bf16[1024,1024]{1,0:T(8,128)(2,1)S(1)}, u32[]{:S(2)}, u32[]{:S(2)}) collective-permute-start(bf16[1024,1024]{1,0:T(8,128)(2,1)} %get-tuple-element.222.refs_0_), channel_id=1, source_target_pairs={{0,64},{64,0},{1,65},{65,1},{2,66},{66,2},{3,67},{67,3},{4,68},{68... | collective-permute-start | bytes 6291464 | tf_op jit(solution)/shard_map/ppermute | solution.py:22
  42.6 22.6 %collective-permute-start.6 = (bf16[256,768]{1,0:T(8,128)(2,1)S(1)}, bf16[256,768]{1,0:T(8,128)(2,1)S(1)}, u32[]{:S(2)}, u32[]{:S(2)}) collective-permute-start(bf16[256,768]{1,0:T(8,128)(2,1)S(1)} %get-tuple-element.210.refs_2_.refs_1_), channel_id=1, source_target_pairs={{0,16},{8,24},{16,0},{24,8},{1,17},{9,25},{17,1},{25,9},{2,18},{10... | collective-permute-start | bytes 1179656 | tf_op jit(solution)/shard_map/ppermute | solution.py:22
  45.2 20.6 %collective-permute-start.7 = (bf16[256,768]{1,0:T(8,128)(2,1)S(1)}, bf16[256,768]{1,0:T(8,128)(2,1)S(1)}, u32[]{:S(2)}, u32[]{:S(2)}) collective-permute-start(bf16[256,768]{1,0:T(8,128)(2,1)S(1)} %get-tuple-element.210.refs_2_.refs_1_), channel_id=1, source_target_pairs={{0,24},{8,0},{16,8},{24,16},{1,25},{9,1},{17,9},{25,17},{2,26},{10... | collective-permute-start | bytes 1179656 | tf_op jit(solution)/shard_map/ppermute | solution.py:22
  83.6 24.0 %collective-permute-start.16 = (bf16[2,256,256]{2,1,0:T(8,128)(2,1)}, bf16[2,256,256]{2,1,0:T(8,128)(2,1)S(1)}, u32[]{:S(2)}, u32[]{:S(2)}) collective-permute-start(bf16[2,256,256]{2,1,0:T(8,128)(2,1)} %get-tuple-element.221.refs_4_), channel_id=1, source_target_pairs={{0,4},{2,6},{4,0},{6,2},{1,5},{3,7},{5,1},{7,3},{8,12},{10,14},{12... | collective-permute-start | bytes 786440 | tf_op jit(solution)/shard_map/ppermute | solution.py:22
  86.5 22.0 %collective-permute-start.17 = (bf16[2,256,256]{2,1,0:T(8,128)(2,1)}, bf16[2,256,256]{2,1,0:T(8,128)(2,1)S(1)}, u32[]{:S(2)}, u32[]{:S(2)}) collective-permute-start(bf16[2,256,256]{2,1,0:T(8,128)(2,1)} %get-tuple-element.221.refs_4_), channel_id=1, source_target_pairs={{0,6},{2,0},{4,2},{6,4},{1,7},{3,1},{5,3},{7,5},{8,14},{10,8},{12,... | collective-permute-start | bytes 786440 | tf_op jit(solution)/shard_map/ppermute | solution.py:22
  98.0 20.4 %collective-permute-start.14 = (bf16[128,1024]{1,0:T(8,128)(2,1)S(1)}, bf16[128,1024]{1,0:T(8,128)(2,1)S(1)}, u32[]{:S(2)}, u32[]{:S(2)}) collective-permute-start(bf16[128,1024]{1,0:T(8,128)(2,1)S(1)} %get-tuple-element.220), channel_id=1, source_target_pairs={{0,2},{2,4},{4,6},{6,0},{1,3},{3,5},{5,7},{7,1},{8,10},{10,12},{12... | collective-permute-start | bytes 786440 | tf_op jit(solution)/shard_map/ppermute | solution.py:22
  107.6 27.9 %collective-permute-start.24 = (bf16[512,1024]{1,0:T(8,128)(2,1)}, bf16[512,1024]{1,0:T(8,128)(2,1)S(1)}, u32[]{:S(2)}, u32[]{:S(2)}) collective-permute-start(bf16[512,1024]{1,0:T(8,128)(2,1)} %get-tuple-element.232.refs_4_), channel_id=1, source_target_pairs={{0,1},{1,0},{2,3},{3,2},{4,5},{5,4},{6,7},{7,6},{8,9},{9,8},{10,11... | collective-permute-start | bytes 3145736 | tf_op jit(solution)/shard_map/ppermute | solution.py:22
  108.4 27.1 %collective-permute-start.25 = (bf16[512,1024]{1,0:T(8,128)(2,1)}, bf16[512,1024]{1,0:T(8,128)(2,1)S(1)}, u32[]{:S(2)}, u32[]{:S(2)}) collective-permute-start(bf16[512,1024]{1,0:T(8,128)(2,1)} %get-tuple-element.233.refs_5_), channel_id=1, source_target_pairs={{0,1},{1,0},{2,3},{3,2},{4,5},{5,4},{6,7},{7,6},{8,9},{9,8},{10,11... | collective-permute-start | bytes 3145736 | tf_op jit(solution)/shard_map/ppermute | solution.py:22
  157.5 18.0 %collective-permute-start.32 = (bf16[512,512]{1,0:T(8,128)(2,1)S(1)}, bf16[512,512]{1,0:T(8,128)(2,1)S(1)}, u32[]{:S(2)}, u32[]{:S(2)}) collective-permute-start(bf16[512,512]{1,0:T(8,128)(2,1)S(1)} %copy-done.58), channel_id=1, source_target_pairs={{0,1},{1,0},{2,3},{3,2},{4,5},{5,4},{6,7},{7,6},{8,9},{9,8},{10,11... | collective-permute-start | bytes 1572872 | tf_op jit(solution)/shard_map/ppermute | solution.py:22
  203.1 27.8 %collective-permute-start.43 = (bf16[512,1024]{1,0:T(8,128)(2,1)S(1)}, bf16[512,1024]{1,0:T(8,128)(2,1)S(1)}, u32[]{:S(2)}, u32[]{:S(2)}) collective-permute-start(bf16[512,1024]{1,0:T(8,128)(2,1)S(1)} %copy-done.66), channel_id=1, source_target_pairs={{0,1},{1,0},{2,3},{3,2},{4,5},{5,4},{6,7},{7,6},{8,9},{9,8},{10,11... | collective-permute-start | bytes 3145736 | tf_op jit(solution)/shard_map/ppermute | solution.py:22
  204.2 27.3 %collective-permute-start.44 = (bf16[512,1024]{1,0:T(8,128)(2,1)S(1)}, bf16[512,1024]{1,0:T(8,128)(2,1)S(1)}, u32[]{:S(2)}, u32[]{:S(2)}) collective-permute-start(bf16[512,1024]{1,0:T(8,128)(2,1)S(1)} %copy-done.67), channel_id=1, source_target_pairs={{0,1},{1,0},{2,3},{3,2},{4,5},{5,4},{6,7},{7,6},{8,9},{9,8},{10,11... | collective-permute-start | bytes 3145736 | tf_op jit(solution)/shard_map/ppermute | solution.py:22
  230.9 21.1 %collective-permute-start.49 = (bf16[128,1024]{1,0:T(8,128)(2,1)S(1)}, bf16[128,1024]{1,0:T(8,128)(2,1)S(1)}, u32[]{:S(2)}, u32[]{:S(2)}) collective-permute-start(bf16[128,1024]{1,0:T(8,128)(2,1)S(1)} %copy-done.13), channel_id=1, source_target_pairs={{0,2},{2,4},{4,6},{6,0},{1,3},{3,5},{5,7},{7,1},{8,10},{10,12},{12... | collective-permute-start | bytes 786440 | tf_op jit(solution)/shard_map/ppermute | solution.py:22
  231.5 21.4 %collective-permute-start.50 = (bf16[128,1024]{1,0:T(8,128)(2,1)S(1)}, bf16[128,1024]{1,0:T(8,128)(2,1)S(1)}, u32[]{:S(2)}, u32[]{:S(2)}) collective-permute-start(bf16[128,1024]{1,0:T(8,128)(2,1)S(1)} %copy-done.13), channel_id=1, source_target_pairs={{0,4},{2,6},{4,0},{6,2},{1,5},{3,7},{5,1},{7,3},{8,12},{10,14},{12... | collective-permute-start | bytes 786440 | tf_op jit(solution)/shard_map/ppermute | solution.py:22
  297.7 204.1 %reduce-scatter.4.cloned.1.call-start = ((), (), s32[]{:S(2)}) async-start(), calls=%async_computation.4 | async-start | bytes 3538944 | tf_op jit(solution)/shard_map/reduce_scatter | solution.py:1083
  351.1 24.2 %collective-permute-start.79 = (bf16[128,1024]{1,0:T(8,128)(2,1)S(1)}, bf16[128,1024]{1,0:T(8,128)(2,1)S(1)}, u32[]{:S(2)}, u32[]{:S(2)}) collective-permute-start(bf16[128,1024]{1,0:T(8,128)(2,1)S(1)} %get-tuple-element.305.refs_8_), channel_id=1, source_target_pairs={{0,1},{1,0},{2,3},{3,2},{4,5},{5,4},{6,7},{7,6},{8,9},{9,8},{10,11... | collective-permute-start | bytes 786440 | tf_op jit(solution)/shard_map/ppermute | solution.py:22
  352.3 23.7 %collective-permute-start.80 = (bf16[128,1024]{1,0:T(8,128)(2,1)S(1)}, bf16[128,1024]{1,0:T(8,128)(2,1)S(1)}, u32[]{:S(2)}, u32[]{:S(2)}) collective-permute-start(bf16[128,1024]{1,0:T(8,128)(2,1)S(1)} %get-tuple-element.326), channel_id=1, source_target_pairs={{0,1},{1,0},{2,3},{3,2},{4,5},{5,4},{6,7},{7,6},{8,9},{9,8},{10,11... | collective-permute-start | bytes 786440 | tf_op jit(solution)/shard_map/ppermute | solution.py:22
  391.8 110.0 %reduce-scatter.8.cloned.1.call-start = ((), (), s32[]{:S(2)}) async-start(), calls=%async_computation.6 | async-start | bytes 655360 | tf_op jit(solution)/shard_map/reduce_scatter | solution.py:1288
  405.8 28.8 %collective-permute-start.84 = (bf16[128,1024]{1,0:T(8,128)(2,1)S(1)}, bf16[128,1024]{1,0:T(8,128)(2,1)S(1)}, u32[]{:S(2)}, u32[]{:S(2)}) collective-permute-start(bf16[128,1024]{1,0:T(8,128)(2,1)S(1)} %get-tuple-element.335.refs_10_.refs_0_.refs_1_), channel_id=1, source_target_pairs={{0,2},{2,4},{4,6},{6,0},{1,3},{3,5},{5,7},{7,1},{8,10},{10,12},{12... | collective-permute-start | bytes 786440 | tf_op jit(solution)/shard_map/ppermute | solution.py:22
  405.9 28.7 %collective-permute-start.85 = (bf16[128,1024]{1,0:T(8,128)(2,1)S(1)}, bf16[128,1024]{1,0:T(8,128)(2,1)S(1)}, u32[]{:S(2)}, u32[]{:S(2)}) collective-permute-start(bf16[128,1024]{1,0:T(8,128)(2,1)S(1)} %get-tuple-element.335.refs_10_.refs_0_.refs_1_), channel_id=1, source_target_pairs={{0,4},{2,6},{4,0},{6,2},{1,5},{3,7},{5,1},{7,3},{8,12},{10,14},{12... | collective-permute-start | bytes 786440 | tf_op jit(solution)/shard_map/ppermute | solution.py:22
  407.4 27.2 %collective-permute-start.86 = (bf16[128,1024]{1,0:T(8,128)(2,1)S(1)}, bf16[128,1024]{1,0:T(8,128)(2,1)S(1)}, u32[]{:S(2)}, u32[]{:S(2)}) collective-permute-start(bf16[128,1024]{1,0:T(8,128)(2,1)S(1)} %get-tuple-element.335.refs_10_.refs_0_.refs_1_), channel_id=1, source_target_pairs={{0,6},{2,0},{4,2},{6,4},{1,7},{3,1},{5,3},{7,5},{8,14},{10,8},{12,... | collective-permute-start | bytes 786440 | tf_op jit(solution)/shard_map/ppermute | solution.py:22
  410.6 45.5 %collective-permute-start.88 = (bf16[320,1024]{1,0:T(8,128)(2,1)S(1)}, bf16[320,1024]{1,0:T(8,128)(2,1)S(1)}, u32[]{:S(2)}, u32[]{:S(2)}) collective-permute-start(bf16[320,1024]{1,0:T(8,128)(2,1)S(1)} %get-tuple-element.357), channel_id=1, source_target_pairs={{0,6},{2,0},{4,2},{6,4},{1,7},{3,1},{5,3},{7,5},{8,14},{10,8},{12,... | collective-permute-start | bytes 1966088 | tf_op jit(solution)/shard_map/ppermute | solution.py:22
  411.3 44.8 %collective-permute-start.89 = (bf16[320,1024]{1,0:T(8,128)(2,1)S(1)}, bf16[320,1024]{1,0:T(8,128)(2,1)S(1)}, u32[]{:S(2)}, u32[]{:S(2)}) collective-permute-start(bf16[320,1024]{1,0:T(8,128)(2,1)S(1)} %get-tuple-element.358), channel_id=1, source_target_pairs={{0,4},{2,6},{4,0},{6,2},{1,5},{3,7},{5,1},{7,3},{8,12},{10,14},{12... | collective-permute-start | bytes 1966088 | tf_op jit(solution)/shard_map/ppermute | solution.py:22
  434.6 21.5 %collective-permute-start.90 = (bf16[320,1024]{1,0:T(8,128)(2,1)S(1)}, bf16[320,1024]{1,0:T(8,128)(2,1)S(1)}, u32[]{:S(2)}, u32[]{:S(2)}) collective-permute-start(bf16[320,1024]{1,0:T(8,128)(2,1)S(1)} %get-tuple-element.359), channel_id=1, source_target_pairs={{0,2},{2,4},{4,6},{6,0},{1,3},{3,5},{5,7},{7,1},{8,10},{10,12},{12... | collective-permute-start | bytes 1966088 | tf_op jit(solution)/shard_map/ppermute | solution.py:22
  474.8 108.4 %all-gather.5.cloned.1.call-start = ((), (), s32[]{:S(2)}) async-start(), calls=%async_computation.7 | async-start | bytes 5013504 | tf_op jit(solution)/shard_map/all_gather | solution.py:1305
  477.6 24.1 %collective-permute-start.101 = (bf16[2,128,1024]{2,1,0:T(8,128)(2,1)}, bf16[2,128,1024]{2,1,0:T(8,128)(2,1)S(1)}, u32[]{:S(2)}, u32[]{:S(2)}) collective-permute-start(bf16[2,128,1024]{2,1,0:T(8,128)(2,1)} %get-tuple-element.376), channel_id=1, source_target_pairs={{0,8},{8,16},{16,24},{24,0},{1,9},{9,17},{17,25},{25,1},{2,10},{10... | collective-permute-start | bytes 1572872 | tf_op jit(solution)/shard_map/ppermute | solution.py:22
  478.0 23.8 %collective-permute-start.99 = (bf16[2,128,1024]{2,1,0:T(8,128)(2,1)S(1)}, bf16[2,128,1024]{2,1,0:T(8,128)(2,1)S(1)}, u32[]{:S(2)}, u32[]{:S(2)}) collective-permute-start(bf16[2,128,1024]{2,1,0:T(8,128)(2,1)S(1)} %get-tuple-element.374), channel_id=1, source_target_pairs={{0,24},{8,0},{16,8},{24,16},{1,25},{9,1},{17,9},{25,17},{2,26},{10... | collective-permute-start | bytes 1572872 | tf_op jit(solution)/shard_map/ppermute | solution.py:22
  480.3 31.0 %collective-permute-start.95 = (bf16[144,1024]{1,0:T(8,128)(2,1)}, bf16[144,1024]{1,0:T(8,128)(2,1)S(1)}, u32[]{:S(2)}, u32[]{:S(2)}) collective-permute-start(bf16[144,1024]{1,0:T(8,128)(2,1)} %copy-done.57), channel_id=1, source_target_pairs={{0,6},{2,0},{4,2},{6,4},{1,7},{3,1},{5,3},{7,5},{8,14},{10,8},{12,... | collective-permute-start | bytes 884744 | tf_op jit(solution)/shard_map/ppermute | solution.py:22
  504.6 23.7 %collective-permute-start.103 = (bf16[256,1024]{1,0:T(8,128)(2,1)S(1)}, bf16[256,1024]{1,0:T(8,128)(2,1)S(1)}, u32[]{:S(2)}, u32[]{:S(2)}) collective-permute-start(bf16[256,1024]{1,0:T(8,128)(2,1)S(1)} %get-tuple-element.383), channel_id=1, source_target_pairs={{0,64},{64,0},{1,65},{65,1},{2,66},{66,2},{3,67},{67,3},{4,68},{68... | collective-permute-start | bytes 1572872 | tf_op jit(solution)/shard_map/ppermute | solution.py:22
  531.6 63.8 %collective-permute-start.98 = (bf16[128,1024]{1,0:T(8,128)(2,1)S(1)}, bf16[128,1024]{1,0:T(8,128)(2,1)S(1)}, u32[]{:S(2)}, u32[]{:S(2)}) collective-permute-start(bf16[128,1024]{1,0:T(8,128)(2,1)S(1)} %other_layer_kernel.3), channel_id=1, source_target_pairs={{0,64},{64,0},{1,65},{65,1},{2,66},{66,2},{3,67},{67,3},{4,68},{68... | collective-permute-start | bytes 786440 | tf_op jit(solution)/shard_map/ppermute | solution.py:22
  (154 other events, 2136.6 us)
Sparse Core Ops, SparseCore 0:
  37.8 67.6 all-gather.2
  297.8 73.0 reduce-scatter.5
  391.9 40.8 reduce-scatter.3
  475.0 22.2 reduce-scatter.7
  530.7 52.5 all-gather.4

commit v3 on v2

--- a/solution.py
+++ b/solution.py
@@ -66,6 +66,21 @@
         self.array = array
 
 
+class Awaited:
+    def __init__(self, buffer, move):
+        self.buffer, self.move = buffer, move
+        self.shape, self.dtype = buffer.shape, buffer.dtype
+
+    def arrived(self):
+        if self.move is not None:
+            self.move.wait()
+            self.move = None
+        return self.buffer
+
+    def __getitem__(self, key):
+        return self.arrived()[key]
+
+
 def cold(*arrays):
     return [Cold(array) for array in arrays]
 
@@ -92,7 +107,7 @@
     return pltpu.with_memory_space_constraint(array, pltpu.HBM)
 
 
-def call(kernel, outs, operands, scalars=(), scratch=(), after=(), room=8, token=False):
+def call(kernel, outs, operands, scalars=(), scratch=(), after=(), room=8, token=False, lazy=True):
     ins = [o if isinstance(o, Cold) else None for o in operands]
     arrays = [o.array if isinstance(o, Cold) else o for o in operands]
     puts = [o if isinstance(o, Cold) else None for o in outs]
@@ -103,6 +118,7 @@
     placed = any(o is PLACE for o in scalars)
     scalars = [o for o in scalars if o is not PLACE]
     first, waits = len(scalars), len(after)
+    large = [a.size * a.dtype.itemsize >= 2**21 for a in after]
     last = first + len(arrays)
     brought = [vmem(o.array) for o in ins if o]
     taken = [vmem(o.array) for o in puts if o]
@@ -129,12 +145,18 @@
                 n = len(moves) + len(stores)
                 stores.append(pltpu.make_async_copy(buffers[n], results[at], semaphores.at[n]))
                 results[at] = buffers[n]
-        for move in moves:
+        for at, o in enumerate(ins):
+            if o and lazy:
+                given[at] = Awaited(given[at], moves[sum(1 for p in ins[:at] if p)])
+        for move in () if lazy else moves:
             move.wait()
         if token:
             results.pop()[...] = jnp.zeros((8, 128), F32)
         lead = [PLACE] if placed else []
         kernel(*lead, *refs[:first], *given, *results, *rest[: len(scratch)])
+        for ref in given:
+            if isinstance(ref, Awaited):
+                ref.arrived()
         for store in stores:
             store.start()
         for store in stores:
@@ -147,11 +169,12 @@
         body,
         name=name,
         out_shape=[pltpu.HBM(o.shape, o.dtype) if c else o for o, c in zip(shapes, puts)],
-        in_specs=[SMEM] * first + [HBM if o else VMEM for o in ins] + [ANY] * waits,
+        in_specs=[SMEM] * first + [HBM if o else VMEM for o in ins] + [HBM if b else ANY for b in large],
         out_specs=[HBM if o else VMEM for o in puts],
         scratch_shapes=kept,
         compiler_params=pltpu.CompilerParams(vmem_limit_bytes=held + room * 1024 * 1024),
-    )(*scalars, *(settled(a) if c else a for a, c in zip(arrays, ins)), *after)
+    )(*scalars, *(settled(a) if c else a for a, c in zip(arrays, ins)),
+      *(settled(a) if b else a for a, b in zip(after, large)))
 
 
 ROW = struct((BLOCK, 1024), F32)
@@ -477,7 +500,7 @@
 def cross_cols(w, layer, place, g, at, rows):
     first = RING * block_of(place, g)
     parts = [
-        w[2 * (first + y) + layer, :, at : at + 128]
+        w[first + y, :, at : at + 128]
         for y in range(rows.start // 256, rows.stop // 256)
     ]
     return parts[0] if len(parts) == 1 else jnp.concatenate(parts, axis=0)
@@ -488,7 +511,7 @@
     parts = []
     for c in range(cols.start, cols.stop, 128):
         at = c % 256
-        parts.append(w[2 * (first + c // 256) + layer, at : at + 128, 128:256])
+        parts.append(w[first + c // 256, at : at + 128, 128:256])
     return jnp.concatenate(parts, axis=1)
 
 
@@ -628,17 +651,25 @@
     return mm_tn(dq[:, lanes], a), mm_tn(mixed[:, lanes], g), mm_tn(keys[...], memory)
 
 
-def cross_grads_kernel(
-    mixed, g_mine, g_theirs, dq, a_mine, a_theirs, k0, k1, k2, k3, b0, b1, b2, b3
-):
+def cross_chunk_kernel(place, mixed, g_mine, g_theirs, dq, a_mine, a_theirs, c0, c1, c2, c3, total):
     g = stack_rows((g_mine, g_theirs))
     a = stack_rows((a_mine, a_theirs))
-    for k, (key, out) in enumerate(zip((k0, k1, k2, k3), (b0, b1, b2, b3))):
+    for k in range(RING):
         lanes = slice(128 * k, 128 * k + 128)
-        out[0:128] = mm_tn(dq[:, lanes], a).astype(out.dtype)
-        out[128:256] = mm_tn(mixed[:, lanes], g).astype(out.dtype)
+        parts = (mm_tn(dq[:, lanes], a), mm_tn(mixed[:, lanes], g))
+        for i in range(8):
+            at = 32 * (i % 4)
+            total[128 * i + 32 * k : 128 * i + 32 * k + 32] = parts[i // 4][at : at + 32]
+    cut_chunks(place, total, (c0, c1, c2, c3))
+
+
+def cross_sum_kernel(c0, r1, r2, r3, k0, k1, k2, k3, *outs):
+    sums = [c0[z] + sum(r[z].astype(F32) for r in (r1, r2, r3)) for z in range(2)]
+    for k, (key, out) in enumerate(zip((k0, k1, k2, k3), outs)):
+        for z in range(2):
+            out[32 * z : 32 * z + 32] = sums[z][32 * k : 32 * k + 32].astype(out.dtype)
         for i in range(4):
-            out[256:320, 256 * i : 256 * i + 256] = key[64 * i : 64 * i + 64].astype(out.dtype)
+            out[64:128, 256 * i : 256 * i + 256] = key[64 * i : 64 * i + 64].astype(out.dtype)
 
 
 def cross_first_kernel(
@@ -660,16 +691,15 @@
 
 
 def self_grads_kernel(
-    mixed, g0, g1, g2, g3, dq, down_ref, dother_ref, a0, a1, a2, a3, ours, t0, t1, t2, t3
+    mixed, g0, g1, g2, g3, dq, down_ref, dother_ref, a0, a1, a2, a3, ours, t0, t1
 ):
     g = stack_rows((g0, g1, g2, g3))
     a = stack_rows((a0, a1, a2, a3))
     keys = keys_total(down_ref, dother_ref)
     outs, queries = [jnp.concatenate([r[k] for k in range(RING)], axis=0) for r in (mixed, dq)]
-    t0[...] = mm_tn(outs[:, 128:256], g).astype(BF16)
-    t1[...] = mm_tn(queries[:, 128:256], a).astype(BF16)
-    t2[...] = mm_tn(keys[:, 256:384], a).astype(BF16)
-    t3[...] = mm_tn(keys[:, 384:512], a).astype(BF16)
+    t0[0:128] = mm_tn(outs[:, 128:256], g).astype(BF16)
+    t0[128:256] = mm_tn(queries[:, 128:256], a).astype(BF16)
+    t1[...] = mm_tn(keys[:, 256:512], a).astype(BF16)
     ours[0:128] = mm_tn(outs[:, 0:128], g)
     ours[128:256] = mm_tn(queries[:, 0:128], a)
     ours[256:512] = mm_tn(keys[:, 0:256], a)
@@ -751,10 +781,10 @@
     by_section(place, write)
 
 
-def rest_kernel(place, mine, other, out, parts):
+def rest_kernel(place, mine, other, out, part0, part1):
     def write(own, far):
-        parts[own] = mine[:, 512:768]
-        parts[far] = other[:, 512:768]
+        (part0, part1)[own][0] = mine[:, 512:768]
+        (part0, part1)[far][0] = other[:, 512:768]
 
     by_section(place, write)
     out[:, 0:512] = other[:, 0:512]
@@ -798,26 +828,27 @@
             out[z] = total[at].astype(out.dtype)
 
 
-def join_kernel(f, q0, q1, q2, q3, ours, t0, t1, t2, t3, out):
+def join_kernel(f, q0, q1, q2, q3, ours, t0, t1, out):
     for i in range(8):
         out[i, 0:128] = ffn_total(f, (q0, q1, q2, q3), slice(128 * i, 128 * i + 128)).astype(BF16)
-        theirs = (t0, t1, t2, t3)[i // 2]
-        at = 64 * (i % 2)
+        theirs = (t0, t1)[i // 4]
+        at = 64 * (i % 4)
         out[i, 128:192] = (ours[64 * i : 64 * i + 64] + theirs[at : at + 64].astype(F32)).astype(BF16)
 
 
 def rest_chunk_kernel(
-    place, ours, t0, t1, t2, t3, w0, w1, w2, w3, memory, c0, c1, c2, c3, total
+    place, ours, t0, t1, w0, w1, w2, w3, memory, c0, c1, c2, c3, cross, total
 ):
-    cross = w0[...] + sum(w[...].astype(F32) for w in (w1, w2, w3))
-    keys = jnp.concatenate([cross[256:320, 256 * i : 256 * i + 256] for i in range(4)], axis=0)
+    came = w0[...] + sum(w[...].astype(F32) for w in (w1, w2, w3))
+    for z in range(2):
+        cross[z] = came[32 * z : 32 * z + 32]
+    keys = jnp.concatenate([came[64:128, 256 * i : 256 * i + 256] for i in range(4)], axis=0)
     keys = mm_tn(keys.astype(BF16), memory[...])
     for i in range(8):
-        theirs = (t0, t1, t2, t3)[i // 2]
-        at, to = 64 * (i % 2), 128 * i
+        theirs = (t0, t1)[i // 4]
+        at, to = 64 * (i % 4), 96 * i
         total[to : to + 64] = ours[64 * i : 64 * i + 64] + theirs[at : at + 64].astype(F32)
-        total[to + 64 : to + 96] = cross[32 * i : 32 * i + 32]
-        total[to + 96 : to + 128] = keys[32 * i : 32 * i + 32]
+        total[to + 64 : to + 96] = keys[32 * i : 32 * i + 32]
     cut_chunks(place, total, (c0, c1, c2, c3))
 
 
@@ -830,11 +861,12 @@
     return [Cold(struct((2, rows, 1024), F32))] + [struct((2, rows, 1024), BF16)] * 3
 
 
-def sum_y_kernel(place, c0, r1, r2, r3, first, ffn, cross, keep, over_z, over_s):
+def sum_y_kernel(place, c0, r1, r2, r3, mid, first, ffn, cross, keep, over_z, over_s):
     z = place[3]
 
     def half(n):
-        return c0[n] + sum(r[n].astype(F32) for r in (r1, r2, r3))
+        rest = c0[n] + sum(r[n].astype(F32) for r in (r1, r2, r3))
+        return jnp.concatenate([rest[0:64], mid[n], rest[64:96]], axis=0)
 
     over_z[...] = half(1 - z).astype(BF16)
     rest = half(z)
@@ -911,20 +943,26 @@
         up_ref[512 + 128 * i : 640 + 128 * i] = up[:, 512:1024]
 
 
-def other_layer_kernel(place, first, second, out):
-    out[...] = jnp.where(place[4] == 0, second[...], first[...])
-
-
-def both_batches_kernel(place, first, second, came, out):
+def other_layer_kernel(place, text, unit, input_grad, text_grad, out):
+    def write(rows, grads):
+        out[0:BLOCK] = rows[...]
+        out[BLOCK : 2 * BLOCK] = grads[...]
+
+    pl.when(place[4] == 0)(lambda: write(unit, text_grad))
+    pl.when(place[4] == 1)(lambda: write(text, input_grad))
+
+
+def both_batches_kernel(place, text, unit, input_grad, text_grad, came, states, grads):
     mine = place[4]
-    out[mine] = jnp.where(mine == 0, first[...], second[...])
-    out[1 - mine] = came[...]
-
-
-def last_ffn_kernel(whole, up_ref, down_ref):
-    down_ref[...] = whole[0:512].astype(F32)
-    up_ref[0:512] = whole[512:1024, 0:512].astype(F32)
-    up_ref[512:1024] = whole[512:1024, 512:1024].astype(F32)
+
+    def write(rows, own):
+        states[mine] = rows[...]
+        grads[mine] = own[...]
+
+    pl.when(mine == 0)(lambda: write(text, input_grad))
+    pl.when(mine == 1)(lambda: write(unit, text_grad))
+    states[1 - mine] = came[0:BLOCK]
+    grads[1 - mine] = came[BLOCK : 2 * BLOCK]
 
 
 def layer_forward(layer, v, first, weights, ffns, place, lengths, rows, after):
@@ -1021,8 +1059,8 @@
     dkv_cross, (near, far2) = rest[:RING], rest[RING:]
     dv1, g1, norms2 = sum_back(1, dv2, near, [swap(far2, "core")], s2, r2, rows, old=old, new=True)
     full_g1 = gather_x(g1)
-    cross_grads = [*cold_if(old, mixed2), g2, g2_theirs, dcq, *cold_if(old, a2, a2_theirs), *dkv_cross]
-    middle, waits = steps["middle"](ffn_parts, cross_grads, g1)
+    cross_grads = [*cold_if(old, mixed2), g2, g2_theirs, dcq, *cold_if(old, a2, a2_theirs)]
+    middle, waits = steps["middle"](ffn_parts, cross_grads, dkv_cross, g1)
     dq, dkv_own, dkv_theirs = call(
         self_back_kernel,
         [
@@ -1046,15 +1084,16 @@
     def self_grads(waits=()):
         ours, *theirs = call(
             self_grads_kernel,
-            [struct((512, 1024), F32)] + [struct((BLOCK, 1024), BF16)] * 4,
+            [struct((512, 1024), F32)] + [struct((2 * BLOCK, 1024), BF16)] * 2,
             [*cold(mixed1), *full_g1, *back, *cold(*full1)],
             after=waits,
         )
         return [ours, *(swap(part, "core") for part in theirs)], theirs
 
     if layer == 0:
-        self_parts, theirs = self_grads([*middle[1:4], *steps["before"]])
-        waits = steps["late"](middle, self_parts, theirs)
+        share, *others = call(cross_sum_kernel, [ROW, ROW16, ROW16, ROW16], middle)
+        self_parts, theirs = self_grads([share])
+        waits = steps["late"]([share, *send_x(others)], self_parts, theirs)
         tall = struct((BLOCK + 16, 1024), BF16)
         near, *others, sums = call(
             last_rows_back_kernel,
@@ -1140,13 +1179,12 @@
         both_norms_kernel, [struct((6, 1024), F32)] * 2, [norms, norms_other], scalars=[place]
     )
 
-    rest, parts = call(
+    rest, *parts = call(
         rest_kernel,
-        [struct((256, 768), BF16), Cold(struct((2, 256, 256), BF16))],
+        [struct((256, 768), BF16), *cold(*[struct((1, 256, 256), BF16)] * 2)],
         [mine, other],
         scalars=[place],
-        after=[norms_other, *rows_first[1:]],
-    )
+        after=[norms_other, *rows_first[1:]], lazy=False)
     rests = along_y(rest)
     e_far = swap(call(memory_blocks_kernel, [row16], rows_first)[0], "core")
     a0, a1, b0, b1 = call(
@@ -1154,11 +1192,10 @@
         [half, half, *cold(half, half)],
         [*cold(*self_mine), *rests],
         scalars=[place],
-        after=[e_far, norms[0], ffn_done],
-    )
+        after=[e_far, norms[0], ffn_done], lazy=False)
     selfs = [(a0, a1), (b0, b1)]
     selfs_far = [tuple(swap(w, "core") for w in pair) for pair in selfs]
-    crosses = lax.all_gather(parts, ("tx", "dy"), axis=0, tiled=True)
+    crosses = [lax.all_gather(part, ("tx", "dy"), axis=0, tiled=True) for part in parts]
     ffns, kvs = [], []
 
     def make_keys(q):
@@ -1181,18 +1218,17 @@
             cold(ffn_mine, ffn_other),
             scalars=[place],
             after=[mixed],
-            token=True,
-        )
+            token=True, lazy=False)
         for first, second in ((a0, a1), (b0, b1)):
             ffns.append((first, second, swap(first, "core"), swap(second, "core")))
         return [done]
 
-    weights = [(selfs[i], selfs_far[i], crosses, kvs) for i in range(2)]
+    weights = [(selfs[i], selfs_far[i], crosses[i], kvs) for i in range(2)]
 
     v, near, far, stored0 = layer_forward(
         0, x, rows_first, weights[0], ffns, place, source_lengths, norms[0], {"keys": make_keys, "sum1": lambda mixed: [*kvs[1:4], *made(mixed)]}
     )
-    text, *normed = sum_norm(0, v, near, far, norms[1], ROW16)
+    text, *normed = sum_norm(0, v, near, far, norms[1], ROW16, after=[crosses[1]])
     v, near, far, stored1 = layer_forward(
         1, text, normed, weights[1], ffns, place, source_lengths, norms[1], {}
     )
@@ -1200,31 +1236,17 @@
     full_top = gather_x(g_top)
     unit = call(sum_last_kernel, cold(ROW16), [*cold(v), near, *far])[0]
 
-    def middle_second(ffn_parts, cross_grads, after):
+    def middle_second(ffn_parts, cross_grads, keys, after):
         out, done = call(
             cross_first_kernel,
             cold(struct((8, 384, 1024), BF16)),
-            [*ffn_parts, *cross_grads, *cold(memory)],
+            [*ffn_parts, *cross_grads, *keys, *cold(memory)],
             scalars=[place],
             after=[after],
             token=True,
         )
         return out, [done]
 
-    def by_layer(first, second, after=()):
-        lacks = call(other_layer_kernel, [row16], cold(first, second), scalars=[place], after=after)[0]
-        return [*cold(first, second), swap(lacks, "section")]
-
-    def both_batches(parts, after=()):
-        return call(
-            both_batches_kernel,
-            cold(struct((2, BLOCK, 1024), BF16)),
-            parts,
-            scalars=[place],
-            after=after,
-        )[0]
-
-    states = by_layer(text, unit, ())
     text_grad, grads_a, self1, norms1 = layer_back(
         1, g_top, full_top, stored1, weights[1], ffns, place, source_lengths, norms[1],
         {
@@ -1248,24 +1270,27 @@
         )
         return [done]
 
-    def middle_first(ffn_parts, cross_grads, after):
-        own, *sent = call(
-            cross_grads_kernel,
-            [struct((320, 1024), F32)] + [struct((320, 1024), BF16)] * 3,
+    def middle_first(ffn_parts, cross_grads, keys, after):
+        chunks_of = call(
+            cross_chunk_kernel,
+            chunk_shapes(128),
             cross_grads,
+            scalars=[place],
+            scratch=[pltpu.VMEM((1024, 1024), F32)],
             after=[after],
         )
-        return [own, *send_x(sent)], [own]
+        arrived = [shift(c, "dy", -k) for k, c in enumerate(chunks_of[1:], 1)]
+        return [*cold(chunks_of[0]), *arrived, *keys], [chunks_of[1]]
 
     def late_first(cross_parts, self_parts, theirs):
-        tail["chunks"] = call(
+        *tail["chunks"], tail["cross"] = call(
             rest_chunk_kernel,
-            chunk_shapes(128),
+            chunk_shapes(96) + cold(struct((2, 32, 1024), F32)),
             [*self_parts, *cross_parts, *cold(memory)],
             scalars=[place],
-            scratch=[pltpu.VMEM((1024, 1024), F32)],
+            scratch=[pltpu.VMEM((768, 1024), F32)],
         )
-        return [tail["chunks"][0]]
+        return [tail["chunks"][1]]
 
     input_grad, _, _, norms = layer_back(
         0, text_grad, gather_x(text_grad), stored0, weights[0], ffns, place, source_lengths, norms[0],
@@ -1275,7 +1300,6 @@
             "late": late_first,
             "norms": norms1,
             "tail": tail,
-            "before": [states[2]],
         },
     )
     grads_b = reduce_dp(tail["joined"])
@@ -1292,10 +1316,9 @@
     keep, over_z, over_s = call(
         sum_y_kernel,
         [Cold(two), row16, struct((256, 1024), BF16)],
-        [*cold(chunks_of[0]), *arrived, *cold(grads_b, ffn1, cross1)],
+        [*cold(chunks_of[0]), *arrived, *cold(tail["cross"], grads_b, ffn1, cross1)],
         scalars=[place],
-        after=[tail["near"]],
-    )
+        after=[tail["near"]], lazy=False)
     last = call(
         sum_rest_kernel,
         cold(struct((272, 1024), BF16)),
@@ -1303,11 +1326,13 @@
         scalars=[place],
     )[0]
     whole = lax.all_gather(last, ("dz", "dy"), axis=0, tiled=True)
-    states = both_batches(states)
-    input_parts = by_layer(input_grad, text_grad, ())
+    rows = cold(text, unit, input_grad, text_grad)
+    lacks = call(
+        other_layer_kernel, [struct((256, 1024), BF16)], rows, scalars=[place], after=[last], lazy=False)[0]
+    lacks = swap(lacks, "section")
     eight, pair32 = struct((8, 1024), F32), struct((2, 1024), F32)
     own, over_s = call(
-        norms_kernel, [eight] * 2, cold(whole), scalars=[place], after=[states]
+        norms_kernel, [eight] * 2, cold(whole), scalars=[place]
     )
     grad_out, grad_self, grad_cq, grad_co, grad_ckv, grad_up, grad_down, done = call(
         last_kernel,
@@ -1324,7 +1349,9 @@
         after=[own],
         token=True,
     )
-    input_grads = both_batches(input_parts, [done])
+    both = struct((2, BLOCK, 1024), BF16)
+    states, input_grads = call(
+        both_batches_kernel, cold(both, both), [*rows, lacks], scalars=[place], after=[done], lazy=False)
     grad_gain, grad_bias, grad_ffn = call(
         last_norms_kernel, [pair32] * 3, [own, swap(over_s, "section")], after=[done]
     )

time: 613 us -> 616 us (level)
  waiting for transfers between devices: 276 us -> 298 us
  starting transfers between devices: 119 us -> 104 us
    ppermute x106 -> x104, waiting for transfers between devices: 227 us -> 250 us  [shift(): lax.ppermute(value, axis, [(i, (i + steps) % count) for i in range(count)])]
    ppermute x106 -> x104, starting transfers between devices: 118 us -> 103 us  [shift(): lax.ppermute(value, axis, [(i, (i + steps) % count) for i in range(count)])]
    pallas_call x56 -> x55, Pallas kernels: 180 us -> 175 us  [call(): pl.pallas_call(body, name=name, out_shape=[pltpu.HBM(o.shape, o.dtype) if...]
    unnamed x152 -> x148, local copies, waits for them, and re-layouts: 13.2 us -> 15.7 us
  transfers between devices with their start and end apart: 112 -> 111, of which waited for: 61 -> 63; matrix products, arithmetic and copies ran while one was open for 0% -> 0% of each run, Pallas kernels for 25% -> 25%
where the time goes in v3:
time: 616 us; the launch traced here: 609 us
  waiting for transfers between devices  298 us (48%)
  Pallas kernels  175 us (28%)
  starting transfers between devices  104 us (17%)
  between operations  15.8 us (3%)
  local copies, waits for them, and re-layouts  15.7 us (3%)
    ppermute x104, waiting for transfers between devices, shift(): lax.ppermute(value, axis, [(i, (i + steps) % count) for i in range(count)])  250 us
    pallas_call x55, Pallas kernels, call(): pl.pallas_call(body, name=name, out_shape=[pltpu.HBM(o.shape, o.dtype) if...  175 us
    ppermute x104, starting transfers between devices, shift(): lax.ppermute(value, axis, [(i, (i + steps) % count) for i in range(count)])  103 us
    all_gather x1, waiting for transfers between devices, shards(): whole = lax.all_gather(last, ('dz', 'dy'), axis=0, tiled=True)  47.4 us
    unnamed x148, local copies, waits for them, and re-layouts  15.7 us
  transfers between devices with their start and end apart: 111, of which 63 were waited for; matrix products, arithmetic and copies ran while one was open for 0% of the time, Pallas kernels for 25%

profile of v3, /device:TPU:1, one launch (start us, length us, event | category | flops | bytes accessed | tf_op | source)
XLA Modules:
  0.0 608.6 jit_solution(10847249810842028034)
XLA Ops:
  28.7 7.6 %collective-permute-done.1.refs_4_.refs_2_.refs_7_ = bf16[160,1024]{1,0:T(8,128)(2,1)S(1)} collective-permute-done((bf16[160,1024]{1,0:T(8,128)(2,1)}, bf16[160,1024]{1,0:T(8,128)(2,1)S(1)}, u32[]{:S(2)}, u32[]{:S(2)}) %collective-permute-start.1) | collective-permute-done | bytes 327712 | tf_op jit(solution)/shard_map/ppermute | solution.py:22
  51.5 11.6 %collective-permute-done.6.refs_4_.refs_3_ = bf16[256,768]{1,0:T(8,128)(2,1)S(1)} collective-permute-done((bf16[256,768]{1,0:T(8,128)(2,1)S(1)}, bf16[256,768]{1,0:T(8,128)(2,1)S(1)}, u32[]{:S(2)}, u32[]{:S(2)}) %collective-permute-start.6) | collective-permute-done | bytes 393248 | tf_op jit(solution)/shard_map/ppermute | solution.py:22
  84.2 6.1 self_forward_kernel.2
  105.1 5.5 collective-permute-done.14.refs_4_
  113.5 5.9 cross_forward_kernel.2
  127.2 7.4 %collective-permute-done.21.refs_1_.refs_7_ = bf16[128,1024]{1,0:T(8,128)(2,1)S(1)} collective-permute-done((bf16[128,1024]{1,0:T(8,128)(2,1)S(1)}, bf16[128,1024]{1,0:T(8,128)(2,1)S(1)}, u32[]{:S(2)}, u32[]{:S(2)}) %collective-permute-start.21) | collective-permute-done | bytes 262176 | tf_op jit(solution)/shard_map/ppermute | solution.py:22
  134.6 11.5 %collective-permute-done.22.refs_2_.refs_8_ = bf16[128,1024]{1,0:T(8,128)(2,1)S(1)} collective-permute-done((bf16[128,1024]{1,0:T(8,128)(2,1)S(1)}, bf16[128,1024]{1,0:T(8,128)(2,1)S(1)}, u32[]{:S(2)}, u32[]{:S(2)}) %collective-permute-start.22) | collective-permute-done | bytes 262176 | tf_op jit(solution)/shard_map/ppermute | solution.py:22
  146.1 6.1 ffn_forward_kernel.2
  166.1 5.4 collective-permute-done.28.refs_4_
  176.2 6.1 %collective-permute-done.29.refs_1_.refs_9_ = bf16[128,1024]{1,0:T(8,128)(2,1)S(1)} collective-permute-done((bf16[128,1024]{1,0:T(8,128)(2,1)S(1)}, bf16[128,1024]{1,0:T(8,128)(2,1)S(1)}, u32[]{:S(2)}, u32[]{:S(2)}) %collective-permute-start.29) | collective-permute-done | bytes 262176 | tf_op jit(solution)/shard_map/ppermute | solution.py:22
  193.5 6.2 %self_forward_kernel.3 = (bf16[4,128,256]{2,1,0:T(8,128)(2,1)S(1)}, f32[4,4,1,128]{3,2,1,0:T(1,128)S(1)}, f32[128,1024]{1,0:T(8,128)S(1)}, bf16[128,1024]{1,0:T(...) custom-call(bf16[4,128,256]{2,1,0:T(8,128)(2,1)S(1)} %get-tuple-element.248.refs_0_.refs_8_, ...), custom_call_target="tpu_custom_call" | custom-call | tf_op jit(solution)/shard_map/self_forward_kernel/pallas_call | solution.py:168
  212.0 5.9 collective-permute-done.37.refs_4_
  220.4 5.9 cross_forward_kernel.3
  271.5 5.8 collective-permute-done.53.refs_4_
  280.9 7.6 %cross_back_kernel.2 = (bf16[256,512]{1,0:T(8,128)(2,1)S(1)}, bf16[256,256]{1,0:T(8,128)(2,1)S(1)}, bf16[256,256]{1,0:T(8,128)(2,1)S(1)}, bf16[256,256]{1,0:T(8,...) custom-call(s32[2,1]{1,0:T(2,128)S(1)} %copy.35.refs_0_, ...), custom_call_target="tpu_custom_call" | custom-call | tf_op jit(solution)/shard_map/cross_back_kernel/pallas_call | solution.py:168
  300.2 5.3 collective-permute-done.56.refs_1_.refs_2_
  305.4 6.5 %collective-permute-done.57.refs_2_.refs_3_ = bf16[128,1024]{1,0:T(8,128)(2,1)S(1)} collective-permute-done((bf16[128,1024]{1,0:T(8,128)(2,1)S(1)}, bf16[128,1024]{1,0:T(8,128)(2,1)S(1)}, u32[]{:S(2)}, u32[]{:S(2)}) %collective-permute-start.57) | collective-permute-done | bytes 262176 | tf_op jit(solution)/shard_map/ppermute | solution.py:22
  312.0 9.8 %self_back_kernel.2 = (bf16[4,128,256]{2,1,0:T(8,128)(2,1)S(1)}, f32[4,128,512]{2,1,0:T(8,128)S(1)}, bf16[4,128,512]{2,1,0:T(8,128)(2,1)S(1)}) custom-call(bf16[128,1024]{1,0:T(8,128)(2,1)S(1)} %get-tuple-element.286.refs_16_.refs_0_.refs_1_, bf16[128,1024]{1,0:T(8,128)(2,1)S(1)} %collective-permute-done.56.refs_1_.refs_2_, ...), custom_call_target="tpu_custom_call" | custom-call | tf_op jit(solution)/shard_map/self_back_kernel/pallas_call | solution.py:168
  338.7 6.1 %collective-permute-done.66.refs_4_ = bf16[128,1024]{1,0:T(8,128)(2,1)S(1)} collective-permute-done((bf16[128,1024]{1,0:T(8,128)(2,1)S(1)}, bf16[128,1024]{1,0:T(8,128)(2,1)S(1)}, u32[]{:S(2)}, u32[]{:S(2)}) %collective-permute-start.66) | collective-permute-done | bytes 262176 | tf_op jit(solution)/shard_map/ppermute | solution.py:22
  351.8 10.3 %collective-permute-done.67.refs_1_.refs_2_ = bf16[128,1024]{1,0:T(8,128)(2,1)S(1)} collective-permute-done((bf16[128,1024]{1,0:T(8,128)(2,1)S(1)}, bf16[128,1024]{1,0:T(8,128)(2,1)S(1)}, u32[]{:S(2)}, u32[]{:S(2)}) %collective-permute-start.67) | collective-permute-done | bytes 262176 | tf_op jit(solution)/shard_map/ppermute | solution.py:22
  362.5 5.6 ffn_back_kernel.3
  393.2 7.7 %cross_back_kernel.3 = (bf16[256,512]{1,0:T(8,128)(2,1)S(1)}, bf16[256,256]{1,0:T(8,128)(2,1)S(1)}, bf16[256,256]{1,0:T(8,128)(2,1)S(1)}, bf16[256,256]{1,0:T(8,...) custom-call(s32[2,1]{1,0:T(2,128)S(1)} %copy.35.refs_0_, ...), custom_call_target="tpu_custom_call" | custom-call | tf_op jit(solution)/shard_map/cross_back_kernel/pallas_call | solution.py:168
  413.5 6.3 %collective-permute-done.81.refs_1_.refs_2_ = bf16[128,1024]{1,0:T(8,128)(2,1)S(1)} collective-permute-done((bf16[128,1024]{1,0:T(8,128)(2,1)S(1)}, bf16[128,1024]{1,0:T(8,128)(2,1)S(1)}, u32[]{:S(2)}, u32[]{:S(2)}) %collective-permute-start.81) | collective-permute-done | bytes 262176 | tf_op jit(solution)/shard_map/ppermute | solution.py:22
  420.2 9.8 %self_back_kernel.3 = (bf16[4,128,256]{2,1,0:T(8,128)(2,1)S(1)}, f32[4,128,512]{2,1,0:T(8,128)S(1)}, bf16[4,128,512]{2,1,0:T(8,128)(2,1)S(1)}) custom-call(bf16[128,1024]{1,0:T(8,128)(2,1)S(1)} %get-tuple-element.338.refs_6_.refs_0_.refs_1_, bf16[128,1024]{1,0:T(8,128)(2,1)S(1)} %collective-permute-done.81.refs_1_.refs_2_, ...), custom_call_target="tpu_custom_call" | custom-call | tf_op jit(solution)/shard_map/self_back_kernel/pallas_call | solution.py:168
  437.5 16.2 %collective-permute-done.87.refs_3_ = bf16[2,128,1024]{2,1,0:T(8,128)(2,1)S(1)} collective-permute-done((bf16[2,128,1024]{2,1,0:T(8,128)(2,1)S(1)}, bf16[2,128,1024]{2,1,0:T(8,128)(2,1)S(1)}, u32[]{:S(2)}, u32[]{:S(2)}) %collective-permute-start.87) | collective-permute-done | bytes 524320 | tf_op jit(solution)/shard_map/ppermute | solution.py:22
  460.4 5.8 collective-permute-done.90.refs_4_
  467.5 6.7 %collective-permute-done.92.refs_6_ = bf16[128,1024]{1,0:T(8,128)(2,1)S(1)} collective-permute-done((bf16[128,1024]{1,0:T(8,128)(2,1)S(1)}, bf16[128,1024]{1,0:T(8,128)(2,1)S(1)}, u32[]{:S(2)}, u32[]{:S(2)}) %collective-permute-start.92) | collective-permute-done | bytes 262176 | tf_op jit(solution)/shard_map/ppermute | solution.py:22
  488.5 15.6 %collective-permute-done.96.refs_1_ = bf16[2,96,1024]{2,1,0:T(8,128)(2,1)S(1)} collective-permute-done((bf16[2,96,1024]{2,1,0:T(8,128)(2,1)S(1)}, bf16[2,96,1024]{2,1,0:T(8,128)(2,1)S(1)}, u32[]{:S(2)}, u32[]{:S(2)}) %collective-permute-start.96) | collective-permute-done | bytes 393248 | tf_op jit(solution)/shard_map/ppermute | solution.py:22
  516.1 7.4 %collective-permute-done.94.refs_3_ = bf16[144,1024]{1,0:T(8,128)(2,1)S(1)} collective-permute-done((bf16[144,1024]{1,0:T(8,128)(2,1)S(1)}, bf16[144,1024]{1,0:T(8,128)(2,1)S(1)}, u32[]{:S(2)}, u32[]{:S(2)}) %collective-permute-start.94) | collective-permute-done | bytes 294944 | tf_op jit(solution)/shard_map/ppermute | solution.py:22
  523.5 7.4 %collective-permute-done.95.refs_4_ = bf16[144,1024]{1,0:T(8,128)(2,1)S(1)} collective-permute-done((bf16[144,1024]{1,0:T(8,128)(2,1)S(1)}, bf16[144,1024]{1,0:T(8,128)(2,1)S(1)}, u32[]{:S(2)}, u32[]{:S(2)}) %collective-permute-start.95) | collective-permute-done | bytes 294944 | tf_op jit(solution)/shard_map/ppermute | solution.py:22
  539.8 47.4 %all-gather.8.cloned.1.call-done.refs_0_ = bf16[2176,1024]{1,0:T(8,128)(2,1)} async-done(((bf16[272,1024]{1,0:T(8,128)(2,1)}), bf16[2176,1024]{1,0:T(8,128)(2,1)}) %all-gather.8.cloned.1.call-update) | async-done | bytes 4456464 | tf_op jit(solution)/shard_map/all_gather | solution.py:1328
  592.2 6.1 %last_kernel.1 = (f32[128,1024]{1,0:T(8,128)}, f32[3,1024,128]{2,1,0:T(8,128)}, f32[1024,128]{1,0:T(8,128)}, f32[128,1024]{1,0:T(8,128)}, f32[2048,128]{1,0:T(8,...) custom-call(bf16[2176,1024]{1,0:T(8,128)(2,1)} %all-gather.8.cloned.1.call-done.refs_0_, ...), custom_call_target="tpu_custom_call" | custom-call | tf_op jit(solution)/shard_map/last_kernel/pallas_call | solution.py:168
  (399 shorter events, 308.3 us)
Async XLA Ops:
  7.2 106.4 %all-gather.4.cloned.1.call-start = ((), (), s32[]{:S(2)}) async-start(), calls=%async_computation.3 | async-start | bytes 2228224 | tf_op jit(solution)/shard_map/all_gather | solution.py:1198
  11.8 24.5 %collective-permute-start.3 = (bf16[256,1024]{1,0:T(8,128)(2,1)S(1)}, bf16[256,1024]{1,0:T(8,128)(2,1)S(1)}, u32[]{:S(2)}, u32[]{:S(2)}) collective-permute-start(bf16[256,1024]{1,0:T(8,128)(2,1)S(1)} %get-tuple-element.209.refs_3_.refs_2_.refs_0_), channel_id=1, source_target_pairs={{0,64},{64,0},{1,65},{65,1},{2,66},{66,2},{3,67},{67,3},{4,68},{68... | collective-permute-start | bytes 1572872 | tf_op jit(solution)/shard_map/ppermute | solution.py:22
  37.3 122.3 %all-gather.6.cloned.1.call-start = ((), (), s32[]{:S(2)}) async-start(), calls=%async_computation.4 | async-start | bytes 2228224 | tf_op jit(solution)/shard_map/all_gather | solution.py:1198
  38.0 444.1 %reduce-scatter.6.cloned.1.call-start = ((), (), s32[]{:S(2)}) async-start(), calls=%async_computation.6 | async-start | bytes 7077888 | tf_op jit(solution)/shard_map/reduce_scatter | solution.py:1122
  41.1 53.0 %collective-permute-start.18 = (bf16[1024,1024]{1,0:T(8,128)(2,1)}, bf16[1024,1024]{1,0:T(8,128)(2,1)S(1)}, u32[]{:S(2)}, u32[]{:S(2)}) collective-permute-start(bf16[1024,1024]{1,0:T(8,128)(2,1)} %get-tuple-element.226.refs_0_), channel_id=1, source_target_pairs={{0,64},{64,0},{1,65},{65,1},{2,66},{66,2},{3,67},{67,3},{4,68},{68... | collective-permute-start | bytes 6291464 | tf_op jit(solution)/shard_map/ppermute | solution.py:22
  42.7 20.4 %collective-permute-start.6 = (bf16[256,768]{1,0:T(8,128)(2,1)S(1)}, bf16[256,768]{1,0:T(8,128)(2,1)S(1)}, u32[]{:S(2)}, u32[]{:S(2)}) collective-permute-start(bf16[256,768]{1,0:T(8,128)(2,1)S(1)} %get-tuple-element.214.refs_2_.refs_1_), channel_id=1, source_target_pairs={{0,16},{8,24},{16,0},{24,8},{1,17},{9,25},{17,1},{25,9},{2,18},{10... | collective-permute-start | bytes 1179656 | tf_op jit(solution)/shard_map/ppermute | solution.py:22
  45.3 18.5 %collective-permute-start.7 = (bf16[256,768]{1,0:T(8,128)(2,1)S(1)}, bf16[256,768]{1,0:T(8,128)(2,1)S(1)}, u32[]{:S(2)}, u32[]{:S(2)}) collective-permute-start(bf16[256,768]{1,0:T(8,128)(2,1)S(1)} %get-tuple-element.214.refs_2_.refs_1_), channel_id=1, source_target_pairs={{0,24},{8,0},{16,8},{24,16},{1,25},{9,1},{17,9},{25,17},{2,26},{10... | collective-permute-start | bytes 1179656 | tf_op jit(solution)/shard_map/ppermute | solution.py:22
  81.3 19.6 %collective-permute-start.16 = (bf16[2,256,256]{2,1,0:T(8,128)(2,1)}, bf16[2,256,256]{2,1,0:T(8,128)(2,1)S(1)}, u32[]{:S(2)}, u32[]{:S(2)}) collective-permute-start(bf16[2,256,256]{2,1,0:T(8,128)(2,1)} %get-tuple-element.225.refs_4_), channel_id=1, source_target_pairs={{0,4},{2,6},{4,0},{6,2},{1,5},{3,7},{5,1},{7,3},{8,12},{10,14},{12... | collective-permute-start | bytes 786440 | tf_op jit(solution)/shard_map/ppermute | solution.py:22
  100.9 26.3 %collective-permute-start.24 = (bf16[512,1024]{1,0:T(8,128)(2,1)}, bf16[512,1024]{1,0:T(8,128)(2,1)}, u32[]{:S(2)}, u32[]{:S(2)}) collective-permute-start(bf16[512,1024]{1,0:T(8,128)(2,1)} %get-tuple-element.236.refs_4_), channel_id=1, source_target_pairs={{0,1},{1,0},{2,3},{3,2},{4,5},{5,4},{6,7},{7,6},{8,9},{9,8},{10,11... | collective-permute-start | bytes 3145736 | tf_op jit(solution)/shard_map/ppermute | solution.py:22
  102.2 25.0 %collective-permute-start.25 = (bf16[512,1024]{1,0:T(8,128)(2,1)}, bf16[512,1024]{1,0:T(8,128)(2,1)}, u32[]{:S(2)}, u32[]{:S(2)}) collective-permute-start(bf16[512,1024]{1,0:T(8,128)(2,1)} %get-tuple-element.237.refs_5_), channel_id=1, source_target_pairs={{0,1},{1,0},{2,3},{3,2},{4,5},{5,4},{6,7},{7,6},{8,9},{9,8},{10,11... | collective-permute-start | bytes 3145736 | tf_op jit(solution)/shard_map/ppermute | solution.py:22
  124.3 21.7 %collective-permute-start.22 = (bf16[128,1024]{1,0:T(8,128)(2,1)S(1)}, bf16[128,1024]{1,0:T(8,128)(2,1)S(1)}, u32[]{:S(2)}, u32[]{:S(2)}) collective-permute-start(bf16[128,1024]{1,0:T(8,128)(2,1)S(1)} %get-tuple-element.235.refs_0_.refs_6_), channel_id=1, source_target_pairs={{0,4},{2,6},{4,0},{6,2},{1,5},{3,7},{5,1},{7,3},{8,12},{10,14},{12... | collective-permute-start | bytes 786440 | tf_op jit(solution)/shard_map/ppermute | solution.py:22
  127.0 19.1 %collective-permute-start.23 = (bf16[128,1024]{1,0:T(8,128)(2,1)S(1)}, bf16[128,1024]{1,0:T(8,128)(2,1)S(1)}, u32[]{:S(2)}, u32[]{:S(2)}) collective-permute-start(bf16[128,1024]{1,0:T(8,128)(2,1)S(1)} %get-tuple-element.235.refs_0_.refs_6_), channel_id=1, source_target_pairs={{0,6},{2,0},{4,2},{6,4},{1,7},{3,1},{5,3},{7,5},{8,14},{10,8},{12,... | collective-permute-start | bytes 786440 | tf_op jit(solution)/shard_map/ppermute | solution.py:22
  157.6 18.6 %collective-permute-start.32 = (bf16[512,512]{1,0:T(8,128)(2,1)}, bf16[512,512]{1,0:T(8,128)(2,1)}, u32[]{:S(2)}, u32[]{:S(2)}) collective-permute-start(bf16[512,512]{1,0:T(8,128)(2,1)} %get-tuple-element.246.refs_4_.refs_3_), channel_id=1, source_target_pairs={{0,1},{1,0},{2,3},{3,2},{4,5},{5,4},{6,7},{7,6},{8,9},{9,8},{10,11... | collective-permute-start | bytes 1572872 | tf_op jit(solution)/shard_map/ppermute | solution.py:22
  203.9 27.0 %collective-permute-start.43 = (bf16[512,1024]{1,0:T(8,128)(2,1)S(1)}, bf16[512,1024]{1,0:T(8,128)(2,1)S(1)}, u32[]{:S(2)}, u32[]{:S(2)}) collective-permute-start(bf16[512,1024]{1,0:T(8,128)(2,1)S(1)} %copy-done.64), channel_id=1, source_target_pairs={{0,1},{1,0},{2,3},{3,2},{4,5},{5,4},{6,7},{7,6},{8,9},{9,8},{10,11... | collective-permute-start | bytes 3145736 | tf_op jit(solution)/shard_map/ppermute | solution.py:22
  204.8 26.8 %collective-permute-start.44 = (bf16[512,1024]{1,0:T(8,128)(2,1)S(1)}, bf16[512,1024]{1,0:T(8,128)(2,1)S(1)}, u32[]{:S(2)}, u32[]{:S(2)}) collective-permute-start(bf16[512,1024]{1,0:T(8,128)(2,1)S(1)} %copy-done.65), channel_id=1, source_target_pairs={{0,1},{1,0},{2,3},{3,2},{4,5},{5,4},{6,7},{7,6},{8,9},{9,8},{10,11... | collective-permute-start | bytes 3145736 | tf_op jit(solution)/shard_map/ppermute | solution.py:22
  230.9 20.6 %collective-permute-start.48 = (bf16[128,1024]{1,0:T(8,128)(2,1)S(1)}, bf16[128,1024]{1,0:T(8,128)(2,1)S(1)}, u32[]{:S(2)}, u32[]{:S(2)}) collective-permute-start(bf16[128,1024]{1,0:T(8,128)(2,1)S(1)} %copy-done.12), channel_id=1, source_target_pairs={{0,2},{2,4},{4,6},{6,0},{1,3},{3,5},{5,7},{7,1},{8,10},{10,12},{12... | collective-permute-start | bytes 786440 | tf_op jit(solution)/shard_map/ppermute | solution.py:22
  231.6 21.4 %collective-permute-start.49 = (bf16[128,1024]{1,0:T(8,128)(2,1)S(1)}, bf16[128,1024]{1,0:T(8,128)(2,1)S(1)}, u32[]{:S(2)}, u32[]{:S(2)}) collective-permute-start(bf16[128,1024]{1,0:T(8,128)(2,1)S(1)} %copy-done.12), channel_id=1, source_target_pairs={{0,4},{2,6},{4,0},{6,2},{1,5},{3,7},{5,1},{7,3},{8,12},{10,14},{12... | collective-permute-start | bytes 786440 | tf_op jit(solution)/shard_map/ppermute | solution.py:22
  296.6 212.2 %reduce-scatter.4.cloned.1.call-start = ((), (), s32[]{:S(2)}) async-start(), calls=%async_computation.5 | async-start | bytes 3538944 | tf_op jit(solution)/shard_map/reduce_scatter | solution.py:1122
  350.6 26.4 %collective-permute-start.78 = (bf16[256,1024]{1,0:T(8,128)(2,1)S(1)}, bf16[256,1024]{1,0:T(8,128)(2,1)S(1)}, u32[]{:S(2)}, u32[]{:S(2)}) collective-permute-start(bf16[256,1024]{1,0:T(8,128)(2,1)S(1)} %get-tuple-element.310.refs_8_), channel_id=1, source_target_pairs={{0,1},{1,0},{2,3},{3,2},{4,5},{5,4},{6,7},{7,6},{8,9},{9,8},{10,11... | collective-permute-start | bytes 1572872 | tf_op jit(solution)/shard_map/ppermute | solution.py:22
  391.4 117.4 %reduce-scatter.8.cloned.1.call-start = ((), (), s32[]{:S(2)}) async-start(), calls=%async_computation.7 | async-start | bytes 655360 | tf_op jit(solution)/shard_map/reduce_scatter | solution.py:1312
  411.4 24.9 %collective-permute-start.85 = (bf16[2,128,1024]{2,1,0:T(8,128)(2,1)S(1)}, bf16[2,128,1024]{2,1,0:T(8,128)(2,1)S(1)}, u32[]{:S(2)}, u32[]{:S(2)}) collective-permute-start(bf16[2,128,1024]{2,1,0:T(8,128)(2,1)S(1)} %get-tuple-element.342.refs_12_), channel_id=1, source_target_pairs={{0,24},{8,0},{16,8},{24,16},{1,25},{9,1},{17,9},{25,17},{2,26},{10... | collective-permute-start | bytes 1572872 | tf_op jit(solution)/shard_map/ppermute | solution.py:22
  412.8 24.7 %collective-permute-start.86 = (bf16[2,128,1024]{2,1,0:T(8,128)(2,1)S(1)}, bf16[2,128,1024]{2,1,0:T(8,128)(2,1)S(1)}, u32[]{:S(2)}, u32[]{:S(2)}) collective-permute-start(bf16[2,128,1024]{2,1,0:T(8,128)(2,1)S(1)} %get-tuple-element.357), channel_id=1, source_target_pairs={{0,16},{8,24},{16,0},{24,8},{1,17},{9,25},{17,1},{25,9},{2,18},{10... | collective-permute-start | bytes 1572872 | tf_op jit(solution)/shard_map/ppermute | solution.py:22
  419.8 33.8 %collective-permute-start.87 = (bf16[2,128,1024]{2,1,0:T(8,128)(2,1)S(1)}, bf16[2,128,1024]{2,1,0:T(8,128)(2,1)S(1)}, u32[]{:S(2)}, u32[]{:S(2)}) collective-permute-start(bf16[2,128,1024]{2,1,0:T(8,128)(2,1)S(1)} %get-tuple-element.358), channel_id=1, source_target_pairs={{0,8},{8,16},{16,24},{24,0},{1,9},{9,17},{17,25},{25,1},{2,10},{10... | collective-permute-start | bytes 1572872 | tf_op jit(solution)/shard_map/ppermute | solution.py:22
  430.0 25.2 %collective-permute-start.84 = (bf16[4,128,512]{2,1,0:T(8,128)(2,1)S(1)}, bf16[4,128,512]{2,1,0:T(8,128)(2,1)S(1)}, u32[]{:S(2)}, u32[]{:S(2)}) collective-permute-start(bf16[4,128,512]{2,1,0:T(8,128)(2,1)S(1)} %get-tuple-element.345), channel_id=1, source_target_pairs={{0,1},{1,0},{2,3},{3,2},{4,5},{5,4},{6,7},{7,6},{8,9},{9,8},{10,11... | collective-permute-start | bytes 1572872 | tf_op jit(solution)/shard_map/ppermute | solution.py:22
  484.3 102.9 %all-gather.8.cloned.1.call-start = ((), (), s32[]{:S(2)}) async-start(), calls=%async_computation.8 | async-start | bytes 5013504 | tf_op jit(solution)/shard_map/all_gather | solution.py:1328
  484.3 19.8 %collective-permute-start.96 = (bf16[2,96,1024]{2,1,0:T(8,128)(2,1)S(1)}, bf16[2,96,1024]{2,1,0:T(8,128)(2,1)S(1)}, u32[]{:S(2)}, u32[]{:S(2)}) collective-permute-start(bf16[2,96,1024]{2,1,0:T(8,128)(2,1)S(1)} %get-tuple-element.370.refs_13_), channel_id=1, source_target_pairs={{0,24},{8,0},{16,8},{24,16},{1,25},{9,1},{17,9},{25,17},{2,26},{10... | collective-permute-start | bytes 1179656 | tf_op jit(solution)/shard_map/ppermute | solution.py:22
  488.5 20.3 %collective-permute-start.98 = (bf16[2,96,1024]{2,1,0:T(8,128)(2,1)S(1)}, bf16[2,96,1024]{2,1,0:T(8,128)(2,1)S(1)}, u32[]{:S(2)}, u32[]{:S(2)}) collective-permute-start(bf16[2,96,1024]{2,1,0:T(8,128)(2,1)S(1)} %get-tuple-element.381), channel_id=1, source_target_pairs={{0,8},{8,16},{16,24},{24,0},{1,9},{9,17},{17,25},{25,1},{2,10},{10... | collective-permute-start | bytes 1179656 | tf_op jit(solution)/shard_map/ppermute | solution.py:22
  488.5 26.3 %collective-permute-start.93 = (bf16[144,1024]{1,0:T(8,128)(2,1)}, bf16[144,1024]{1,0:T(8,128)(2,1)S(1)}, u32[]{:S(2)}, u32[]{:S(2)}) collective-permute-start(bf16[144,1024]{1,0:T(8,128)(2,1)} %copy-done.61), channel_id=1, source_target_pairs={{0,6},{2,0},{4,2},{6,4},{1,7},{3,1},{5,3},{7,5},{8,14},{10,8},{12,... | collective-permute-start | bytes 884744 | tf_op jit(solution)/shard_map/ppermute | solution.py:22
  511.6 23.1 %collective-permute-start.100 = (bf16[256,1024]{1,0:T(8,128)(2,1)S(1)}, bf16[256,1024]{1,0:T(8,128)(2,1)S(1)}, u32[]{:S(2)}, u32[]{:S(2)}) collective-permute-start(bf16[256,1024]{1,0:T(8,128)(2,1)S(1)} %get-tuple-element.389), channel_id=1, source_target_pairs={{0,64},{64,0},{1,65},{65,1},{2,66},{66,2},{3,67},{67,3},{4,68},{68... | collective-permute-start | bytes 1572872 | tf_op jit(solution)/shard_map/ppermute | solution.py:22
  514.8 19.9 %collective-permute-start.99 = (bf16[128,1024]{1,0:T(8,128)(2,1)S(1)}, bf16[128,1024]{1,0:T(8,128)(2,1)S(1)}, u32[]{:S(2)}, u32[]{:S(2)}) collective-permute-start(bf16[128,1024]{1,0:T(8,128)(2,1)S(1)} %get-tuple-element.388), channel_id=1, source_target_pairs={{0,32},{32,0},{1,33},{33,1},{2,34},{34,2},{3,35},{35,3},{4,36},{36... | collective-permute-start | bytes 786440 | tf_op jit(solution)/shard_map/ppermute | solution.py:22
  514.8 19.9 %collective-permute-start.101 = (bf16[128,1024]{1,0:T(8,128)(2,1)S(1)}, bf16[128,1024]{1,0:T(8,128)(2,1)S(1)}, u32[]{:S(2)}, u32[]{:S(2)}) collective-permute-start(bf16[128,1024]{1,0:T(8,128)(2,1)S(1)} %get-tuple-element.388), channel_id=1, source_target_pairs={{64,32},{96,0},{65,33},{97,1},{66,34},{98,2},{67,35},{99,3},{68,36... | collective-permute-start | bytes 786440 | tf_op jit(solution)/shard_map/ppermute | solution.py:901
  539.3 59.0 %collective-permute-start.103 = (bf16[256,1024]{1,0:T(8,128)(2,1)S(1)}, bf16[256,1024]{1,0:T(8,128)(2,1)S(1)}, u32[]{:S(2)}, u32[]{:S(2)}) collective-permute-start(bf16[256,1024]{1,0:T(8,128)(2,1)S(1)} %other_layer_kernel.1), channel_id=1, source_target_pairs={{0,64},{64,0},{1,65},{65,1},{2,66},{66,2},{3,67},{67,3},{4,68},{68... | collective-permute-start | bytes 1572872 | tf_op jit(solution)/shard_map/ppermute | solution.py:22
  (151 other events, 2074.2 us)
Sparse Core Ops, SparseCore 0:
  37.4 55.4 all-gather.3
  95.0 53.4 all-gather.5
  296.7 72.4 reduce-scatter.5
  391.5 61.6 reduce-scatter.3
  484.4 19.9 reduce-scatter.7
  537.1 50.0 all-gather.7

commit v4 on v3

--- a/solution.py
+++ b/solution.py
@@ -118,7 +118,6 @@
     placed = any(o is PLACE for o in scalars)
     scalars = [o for o in scalars if o is not PLACE]
     first, waits = len(scalars), len(after)
-    large = [a.size * a.dtype.itemsize >= 2**21 for a in after]
     last = first + len(arrays)
     brought = [vmem(o.array) for o in ins if o]
     taken = [vmem(o.array) for o in puts if o]
@@ -169,12 +168,11 @@
         body,
         name=name,
         out_shape=[pltpu.HBM(o.shape, o.dtype) if c else o for o, c in zip(shapes, puts)],
-        in_specs=[SMEM] * first + [HBM if o else VMEM for o in ins] + [HBM if b else ANY for b in large],
+        in_specs=[SMEM] * first + [HBM if o else VMEM for o in ins] + [ANY] * waits,
         out_specs=[HBM if o else VMEM for o in puts],
         scratch_shapes=kept,
         compiler_params=pltpu.CompilerParams(vmem_limit_bytes=held + room * 1024 * 1024),
-    )(*scalars, *(settled(a) if c else a for a, c in zip(arrays, ins)),
-      *(settled(a) if b else a for a, b in zip(after, large)))
+    )(*scalars, *(settled(a) if c else a for a, c in zip(arrays, ins)), *after)
 
 
 ROW = struct((BLOCK, 1024), F32)
@@ -500,7 +498,7 @@
 def cross_cols(w, layer, place, g, at, rows):
     first = RING * block_of(place, g)
     parts = [
-        w[first + y, :, at : at + 128]
+        w[2 * (first + y) + layer, :, at : at + 128]
         for y in range(rows.start // 256, rows.stop // 256)
     ]
     return parts[0] if len(parts) == 1 else jnp.concatenate(parts, axis=0)
@@ -511,7 +509,7 @@
     parts = []
     for c in range(cols.start, cols.stop, 128):
         at = c % 256
-        parts.append(w[first + c // 256, at : at + 128, 128:256])
+        parts.append(w[2 * (first + c // 256) + layer, at : at + 128, 128:256])
     return jnp.concatenate(parts, axis=1)
 
 
@@ -781,10 +779,10 @@
     by_section(place, write)
 
 
-def rest_kernel(place, mine, other, out, part0, part1):
+def rest_kernel(place, mine, other, out, parts):
     def write(own, far):
-        (part0, part1)[own][0] = mine[:, 512:768]
-        (part0, part1)[far][0] = other[:, 512:768]
+        parts[own] = mine[:, 512:768]
+        parts[far] = other[:, 512:768]
 
     by_section(place, write)
     out[:, 0:512] = other[:, 0:512]
@@ -1179,9 +1177,9 @@
         both_norms_kernel, [struct((6, 1024), F32)] * 2, [norms, norms_other], scalars=[place]
     )
 
-    rest, *parts = call(
+    rest, parts = call(
         rest_kernel,
-        [struct((256, 768), BF16), *cold(*[struct((1, 256, 256), BF16)] * 2)],
+        [struct((256, 768), BF16), Cold(struct((2, 256, 256), BF16))],
         [mine, other],
         scalars=[place],
         after=[norms_other, *rows_first[1:]], lazy=False)
@@ -1195,7 +1193,7 @@
         after=[e_far, norms[0], ffn_done], lazy=False)
     selfs = [(a0, a1), (b0, b1)]
     selfs_far = [tuple(swap(w, "core") for w in pair) for pair in selfs]
-    crosses = [lax.all_gather(part, ("tx", "dy"), axis=0, tiled=True) for part in parts]
+    crosses = lax.all_gather(parts, ("tx", "dy"), axis=0, tiled=True)
     ffns, kvs = [], []
 
     def make_keys(q):
@@ -1223,12 +1221,12 @@
             ffns.append((first, second, swap(first, "core"), swap(second, "core")))
         return [done]
 
-    weights = [(selfs[i], selfs_far[i], crosses[i], kvs) for i in range(2)]
+    weights = [(selfs[i], selfs_far[i], crosses, kvs) for i in range(2)]
 
     v, near, far, stored0 = layer_forward(
         0, x, rows_first, weights[0], ffns, place, source_lengths, norms[0], {"keys": make_keys, "sum1": lambda mixed: [*kvs[1:4], *made(mixed)]}
     )
-    text, *normed = sum_norm(0, v, near, far, norms[1], ROW16, after=[crosses[1]])
+    text, *normed = sum_norm(0, v, near, far, norms[1], ROW16)
     v, near, far, stored1 = layer_forward(
         1, text, normed, weights[1], ffns, place, source_lengths, norms[1], {}
     )

time: 616 us -> 612 us (level)
  waiting for transfers between devices: 298 us -> 312 us
  starting transfers between devices: 104 us -> 90.3 us
    ppermute x104, starting transfers between devices: 103 us -> 88.8 us  [shift(): lax.ppermute(value, axis, [(i, (i + steps) % count) for i in range(count)])]
    ppermute x104, waiting for transfers between devices: 250 us -> 263 us  [shift(): lax.ppermute(value, axis, [(i, (i + steps) % count) for i in range(count)])]
  transfers between devices with their start and end apart: 111 -> 110, of which waited for: 63 -> 67; matrix products, arithmetic and copies ran while one was open for 0% -> 0% of each run, Pallas kernels for 25% -> 25%
where the time goes in v4:
time: 612 us; the launch traced here: 605 us
  waiting for transfers between devices  312 us (51%)
  Pallas kernels  176 us (29%)
  starting transfers between devices  90.3 us (15%)
  between operations  15.5 us (3%)
  local copies, waits for them, and re-layouts  11.3 us (2%)
    ppermute x104, waiting for transfers between devices, shift(): lax.ppermute(value, axis, [(i, (i + steps) % count) for i in range(count)])  263 us
    pallas_call x55, Pallas kernels, call(): pl.pallas_call(body, name=name, out_shape=[pltpu.HBM(o.shape, o.dtype) if...  176 us
    ppermute x104, starting transfers between devices, shift(): lax.ppermute(value, axis, [(i, (i + steps) % count) for i in range(count)])  88.8 us
    all_gather x1, waiting for transfers between devices, shards(): whole = lax.all_gather(last, ('dz', 'dy'), axis=0, tiled=True)  48.4 us
  transfers between devices with their start and end apart: 110, of which 67 were waited for; matrix products, arithmetic and copies ran while one was open for 0% of the time, Pallas kernels for 25%

profile of v4, /device:TPU:1, one launch (start us, length us, event | category | flops | bytes accessed | tf_op | source)
XLA Modules:
  0.0 604.7 jit_solution(9575257340269212357)
XLA Ops:
  22.4 6.3 %collective-permute-done.4.refs_2_.refs_1_ = f32[6,1024]{1,0:T(8,128)S(1)} collective-permute-done((f32[6,1024]{1,0:T(8,128)S(1)}, f32[6,1024]{1,0:T(8,128)S(1)}, u32[]{:S(2)}, u32[]{:S(2)}) %collective-permute-start.4) | collective-permute-done | bytes 24608 | tf_op jit(solution)/shard_map/ppermute | solution.py:22
  30.8 8.6 %collective-permute-done.refs_3_.refs_1_.refs_6_ = bf16[160,1024]{1,0:T(8,128)(2,1)S(1)} collective-permute-done((bf16[160,1024]{1,0:T(8,128)(2,1)}, bf16[160,1024]{1,0:T(8,128)(2,1)S(1)}, u32[]{:S(2)}, u32[]{:S(2)}) %collective-permute-start) | collective-permute-done | bytes 327712 | tf_op jit(solution)/shard_map/ppermute | solution.py:22
  50.3 5.9 collective-permute-done.7.refs_5_.refs_4_
  59.7 11.5 %collective-permute-done.5.refs_3_.refs_2_ = bf16[256,768]{1,0:T(8,128)(2,1)S(1)} collective-permute-done((bf16[256,768]{1,0:T(8,128)(2,1)S(1)}, bf16[256,768]{1,0:T(8,128)(2,1)S(1)}, u32[]{:S(2)}, u32[]{:S(2)}) %collective-permute-start.5) | collective-permute-done | bytes 393248 | tf_op jit(solution)/shard_map/ppermute | solution.py:22
  87.2 6.0 self_forward_kernel.2
  108.6 5.9 collective-permute-done.12.refs_2_
  124.3 6.5 %cross_forward_kernel.2 = (bf16[256,512]{1,0:T(8,128)(2,1)S(1)}, bf16[256,512]{1,0:T(8,128)(2,1)S(1)}, f32[8,1,256]{2,1,0:T(1,128)S(1)}, f32[128,1024]{1,0:T(8,128)S(1)}, bf16[128,1024]{1,0:T(8,128)(2,1)S(1)}) custom-call(s32[2,1]{1,0:T(2,128)S(1)} %copy.35.refs_0_, bf16[128,1024]{1,0:T(8,128)(2,1)S(1)} %get-tuple-element.229.refs_1_.refs_4_, ...), custom_call_target="tpu_custom_call" | custom-call | tf_op jit(solution)/shard_map/cross_forward_kernel/pallas_call | solution.py:167
  144.7 6.6 %collective-permute-done.21.refs_1_.refs_7_ = bf16[128,1024]{1,0:T(8,128)(2,1)S(1)} collective-permute-done((bf16[128,1024]{1,0:T(8,128)(2,1)S(1)}, bf16[128,1024]{1,0:T(8,128)(2,1)S(1)}, u32[]{:S(2)}, u32[]{:S(2)}) %collective-permute-start.21) | collective-permute-done | bytes 262176 | tf_op jit(solution)/shard_map/ppermute | solution.py:22
  165.8 7.1 %collective-permute-done.28.refs_4_ = bf16[128,1024]{1,0:T(8,128)(2,1)S(1)} collective-permute-done((bf16[128,1024]{1,0:T(8,128)(2,1)S(1)}, bf16[128,1024]{1,0:T(8,128)(2,1)S(1)}, u32[]{:S(2)}, u32[]{:S(2)}) %collective-permute-start.28) | collective-permute-done | bytes 262176 | tf_op jit(solution)/shard_map/ppermute | solution.py:22
  181.9 7.6 %collective-permute-done.29.refs_1_.refs_9_ = bf16[128,1024]{1,0:T(8,128)(2,1)S(1)} collective-permute-done((bf16[128,1024]{1,0:T(8,128)(2,1)S(1)}, bf16[128,1024]{1,0:T(8,128)(2,1)S(1)}, u32[]{:S(2)}, u32[]{:S(2)}) %collective-permute-start.29) | collective-permute-done | bytes 262176 | tf_op jit(solution)/shard_map/ppermute | solution.py:22
  194.3 6.2 %self_forward_kernel.3 = (bf16[4,128,256]{2,1,0:T(8,128)(2,1)S(1)}, f32[4,4,1,128]{3,2,1,0:T(1,128)S(1)}, f32[128,1024]{1,0:T(8,128)S(1)}, bf16[128,1024]{1,0:T(...) custom-call(bf16[4,128,256]{2,1,0:T(8,128)(2,1)S(1)} %get-tuple-element.246.refs_0_.refs_8_, ...), custom_call_target="tpu_custom_call" | custom-call | tf_op jit(solution)/shard_map/self_forward_kernel/pallas_call | solution.py:167
  210.7 6.6 %collective-permute-done.37.refs_4_ = bf16[128,1024]{1,0:T(8,128)(2,1)S(1)} collective-permute-done((bf16[128,1024]{1,0:T(8,128)(2,1)S(1)}, bf16[128,1024]{1,0:T(8,128)(2,1)S(1)}, u32[]{:S(2)}, u32[]{:S(2)}) %collective-permute-start.37) | collective-permute-done | bytes 262176 | tf_op jit(solution)/shard_map/ppermute | solution.py:22
  219.5 6.5 %cross_forward_kernel.3 = (bf16[256,512]{1,0:T(8,128)(2,1)S(1)}, bf16[256,512]{1,0:T(8,128)(2,1)S(1)}, f32[8,1,256]{2,1,0:T(1,128)S(1)}, f32[128,1024]{1,0:T(8,128)S(1)}, bf16[128,1024]{1,0:T(8,128)(2,1)S(1)}) custom-call(s32[2,1]{1,0:T(2,128)S(1)} %copy.35.refs_0_, bf16[128,1024]{1,0:T(8,128)(2,1)S(1)} %get-tuple-element.253.refs_1_.refs_9_, ...), custom_call_target="tpu_custom_call" | custom-call | tf_op jit(solution)/shard_map/cross_forward_kernel/pallas_call | solution.py:167
  237.0 7.6 %collective-permute-done.40.refs_1_.refs_7_ = bf16[128,1024]{1,0:T(8,128)(2,1)S(1)} collective-permute-done((bf16[128,1024]{1,0:T(8,128)(2,1)S(1)}, bf16[128,1024]{1,0:T(8,128)(2,1)S(1)}, u32[]{:S(2)}, u32[]{:S(2)}) %collective-permute-start.40) | collective-permute-done | bytes 262176 | tf_op jit(solution)/shard_map/ppermute | solution.py:22
  271.1 6.0 collective-permute-done.53.refs_4_
  280.4 8.1 %cross_back_kernel.2 = (bf16[256,512]{1,0:T(8,128)(2,1)S(1)}, bf16[256,256]{1,0:T(8,128)(2,1)S(1)}, bf16[256,256]{1,0:T(8,128)(2,1)S(1)}, bf16[256,256]{1,0:T(8,...) custom-call(s32[2,1]{1,0:T(2,128)S(1)} %copy.35.refs_0_, ...), custom_call_target="tpu_custom_call" | custom-call | tf_op jit(solution)/shard_map/cross_back_kernel/pallas_call | solution.py:167
  298.3 6.0 collective-permute-done.58.refs_3_.refs_4_
  306.2 6.7 %collective-permute-done.56.refs_1_.refs_2_ = bf16[128,1024]{1,0:T(8,128)(2,1)S(1)} collective-permute-done((bf16[128,1024]{1,0:T(8,128)(2,1)S(1)}, bf16[128,1024]{1,0:T(8,128)(2,1)S(1)}, u32[]{:S(2)}, u32[]{:S(2)}) %collective-permute-start.56) | collective-permute-done | bytes 262176 | tf_op jit(solution)/shard_map/ppermute | solution.py:22
  312.9 9.8 %self_back_kernel.2 = (bf16[4,128,256]{2,1,0:T(8,128)(2,1)S(1)}, f32[4,128,512]{2,1,0:T(8,128)S(1)}, bf16[4,128,512]{2,1,0:T(8,128)(2,1)S(1)}) custom-call(bf16[128,1024]{1,0:T(8,128)(2,1)S(1)} %get-tuple-element.284.refs_16_.refs_0_.refs_1_, bf16[128,1024]{1,0:T(8,128)(2,1)S(1)} %collective-permute-done.56.refs_1_.refs_2_, ...), custom_call_target="tpu_custom_call" | custom-call | tf_op jit(solution)/shard_map/self_back_kernel/pallas_call | solution.py:167
  336.9 6.6 %collective-permute-done.66.refs_4_ = bf16[128,1024]{1,0:T(8,128)(2,1)S(1)} collective-permute-done((bf16[128,1024]{1,0:T(8,128)(2,1)S(1)}, bf16[128,1024]{1,0:T(8,128)(2,1)S(1)}, u32[]{:S(2)}, u32[]{:S(2)}) %collective-permute-start.66) | collective-permute-done | bytes 262176 | tf_op jit(solution)/shard_map/ppermute | solution.py:22
  355.1 7.0 %collective-permute-done.67.refs_1_.refs_2_ = bf16[128,1024]{1,0:T(8,128)(2,1)S(1)} collective-permute-done((bf16[128,1024]{1,0:T(8,128)(2,1)S(1)}, bf16[128,1024]{1,0:T(8,128)(2,1)S(1)}, u32[]{:S(2)}, u32[]{:S(2)}) %collective-permute-start.67) | collective-permute-done | bytes 262176 | tf_op jit(solution)/shard_map/ppermute | solution.py:22
  390.3 8.3 %cross_back_kernel.3 = (bf16[256,512]{1,0:T(8,128)(2,1)S(1)}, bf16[256,256]{1,0:T(8,128)(2,1)S(1)}, bf16[256,256]{1,0:T(8,128)(2,1)S(1)}, bf16[256,256]{1,0:T(8,...) custom-call(s32[2,1]{1,0:T(2,128)S(1)} %copy.35.refs_0_, ...), custom_call_target="tpu_custom_call" | custom-call | tf_op jit(solution)/shard_map/cross_back_kernel/pallas_call | solution.py:167
  413.5 5.6 collective-permute-done.81.refs_1_.refs_2_
  419.1 9.8 %self_back_kernel.3 = (bf16[4,128,256]{2,1,0:T(8,128)(2,1)S(1)}, f32[4,128,512]{2,1,0:T(8,128)S(1)}, bf16[4,128,512]{2,1,0:T(8,128)(2,1)S(1)}) custom-call(bf16[128,1024]{1,0:T(8,128)(2,1)S(1)} %get-tuple-element.336.refs_6_.refs_0_.refs_1_, bf16[128,1024]{1,0:T(8,128)(2,1)S(1)} %collective-permute-done.81.refs_1_.refs_2_, ...), custom_call_target="tpu_custom_call" | custom-call | tf_op jit(solution)/shard_map/self_back_kernel/pallas_call | solution.py:167
  431.4 16.1 %collective-permute-done.87.refs_3_ = bf16[2,128,1024]{2,1,0:T(8,128)(2,1)S(1)} collective-permute-done((bf16[2,128,1024]{2,1,0:T(8,128)(2,1)S(1)}, bf16[2,128,1024]{2,1,0:T(8,128)(2,1)S(1)}, u32[]{:S(2)}, u32[]{:S(2)}) %collective-permute-start.87) | collective-permute-done | bytes 524320 | tf_op jit(solution)/shard_map/ppermute | solution.py:22
  466.6 6.7 %collective-permute-done.92.refs_6_ = bf16[128,1024]{1,0:T(8,128)(2,1)S(1)} collective-permute-done((bf16[128,1024]{1,0:T(8,128)(2,1)S(1)}, bf16[128,1024]{1,0:T(8,128)(2,1)S(1)}, u32[]{:S(2)}, u32[]{:S(2)}) %collective-permute-start.92) | collective-permute-done | bytes 262176 | tf_op jit(solution)/shard_map/ppermute | solution.py:22
  488.2 6.8 %collective-permute-done.97.refs_2_ = bf16[2,96,1024]{2,1,0:T(8,128)(2,1)S(1)} collective-permute-done((bf16[2,96,1024]{2,1,0:T(8,128)(2,1)S(1)}, bf16[2,96,1024]{2,1,0:T(8,128)(2,1)S(1)}, u32[]{:S(2)}, u32[]{:S(2)}) %collective-permute-start.97) | collective-permute-done | bytes 393248 | tf_op jit(solution)/shard_map/ppermute | solution.py:22
  495.1 9.2 %collective-permute-done.98.refs_3_ = bf16[2,96,1024]{2,1,0:T(8,128)(2,1)S(1)} collective-permute-done((bf16[2,96,1024]{2,1,0:T(8,128)(2,1)S(1)}, bf16[2,96,1024]{2,1,0:T(8,128)(2,1)S(1)}, u32[]{:S(2)}, u32[]{:S(2)}) %collective-permute-start.98) | collective-permute-done | bytes 393248 | tf_op jit(solution)/shard_map/ppermute | solution.py:22
  512.0 6.9 %collective-permute-done.94.refs_3_ = bf16[144,1024]{1,0:T(8,128)(2,1)S(1)} collective-permute-done((bf16[144,1024]{1,0:T(8,128)(2,1)S(1)}, bf16[144,1024]{1,0:T(8,128)(2,1)S(1)}, u32[]{:S(2)}, u32[]{:S(2)}) %collective-permute-start.94) | collective-permute-done | bytes 294944 | tf_op jit(solution)/shard_map/ppermute | solution.py:22
  519.0 7.4 %collective-permute-done.95.refs_4_ = bf16[144,1024]{1,0:T(8,128)(2,1)S(1)} collective-permute-done((bf16[144,1024]{1,0:T(8,128)(2,1)S(1)}, bf16[144,1024]{1,0:T(8,128)(2,1)S(1)}, u32[]{:S(2)}, u32[]{:S(2)}) %collective-permute-start.95) | collective-permute-done | bytes 294944 | tf_op jit(solution)/shard_map/ppermute | solution.py:22
  535.3 48.4 %all-gather.5.cloned.1.call-done.refs_0_ = bf16[2176,1024]{1,0:T(8,128)(2,1)} async-done(((bf16[272,1024]{1,0:T(8,128)(2,1)}), bf16[2176,1024]{1,0:T(8,128)(2,1)}) %all-gather.5.cloned.1.call-update) | async-done | bytes 4456464 | tf_op jit(solution)/shard_map/all_gather | solution.py:1326
  588.7 6.1 %last_kernel.1 = (f32[128,1024]{1,0:T(8,128)}, f32[3,1024,128]{2,1,0:T(8,128)}, f32[1024,128]{1,0:T(8,128)}, f32[128,1024]{1,0:T(8,128)}, f32[2048,128]{1,0:T(8,...) custom-call(bf16[2176,1024]{1,0:T(8,128)(2,1)} %all-gather.5.cloned.1.call-done.refs_0_, ...), custom_call_target="tpu_custom_call" | custom-call | tf_op jit(solution)/shard_map/last_kernel/pallas_call | solution.py:167
  (396 shorter events, 308.4 us)
Async XLA Ops:
  7.2 117.2 %all-gather.3.cloned.1.call-start = ((), (), s32[]{:S(2)}) async-start(), calls=%async_computation.3 | async-start | bytes 4456448 | tf_op jit(solution)/shard_map/all_gather | solution.py:1196
  11.8 27.6 %collective-permute-start.3 = (bf16[256,1024]{1,0:T(8,128)(2,1)S(1)}, bf16[256,1024]{1,0:T(8,128)(2,1)S(1)}, u32[]{:S(2)}, u32[]{:S(2)}) collective-permute-start(bf16[256,1024]{1,0:T(8,128)(2,1)S(1)} %get-tuple-element.208.refs_3_.refs_2_.refs_0_), channel_id=1, source_target_pairs={{0,64},{64,0},{1,65},{65,1},{2,66},{66,2},{3,67},{67,3},{4,68},{68... | collective-permute-start | bytes 1572872 | tf_op jit(solution)/shard_map/ppermute | solution.py:22
  40.3 440.7 %reduce-scatter.6.cloned.1.call-start = ((), (), s32[]{:S(2)}) async-start(), calls=%async_computation.5 | async-start | bytes 7077888 | tf_op jit(solution)/shard_map/reduce_scatter | solution.py:1120
  43.5 56.4 %collective-permute-start.18 = (bf16[1024,1024]{1,0:T(8,128)(2,1)}, bf16[1024,1024]{1,0:T(8,128)(2,1)S(1)}, u32[]{:S(2)}, u32[]{:S(2)}) collective-permute-start(bf16[1024,1024]{1,0:T(8,128)(2,1)} %get-tuple-element.225.refs_0_), channel_id=1, source_target_pairs={{0,64},{64,0},{1,65},{65,1},{2,66},{66,2},{3,67},{67,3},{4,68},{68... | collective-permute-start | bytes 6291464 | tf_op jit(solution)/shard_map/ppermute | solution.py:22
  46.8 24.5 %collective-permute-start.5 = (bf16[256,768]{1,0:T(8,128)(2,1)S(1)}, bf16[256,768]{1,0:T(8,128)(2,1)S(1)}, u32[]{:S(2)}, u32[]{:S(2)}) collective-permute-start(bf16[256,768]{1,0:T(8,128)(2,1)S(1)} %get-tuple-element.213.refs_2_.refs_1_), channel_id=1, source_target_pairs={{0,8},{8,16},{16,24},{24,0},{1,9},{9,17},{17,25},{25,1},{2,10},{10... | collective-permute-start | bytes 1179656 | tf_op jit(solution)/shard_map/ppermute | solution.py:22
  85.5 21.3 %collective-permute-start.16 = (bf16[2,256,256]{2,1,0:T(8,128)(2,1)}, bf16[2,256,256]{2,1,0:T(8,128)(2,1)S(1)}, u32[]{:S(2)}, u32[]{:S(2)}) collective-permute-start(bf16[2,256,256]{2,1,0:T(8,128)(2,1)} %get-tuple-element.224.refs_4_), channel_id=1, source_target_pairs={{0,4},{2,6},{4,0},{6,2},{1,5},{3,7},{5,1},{7,3},{8,12},{10,14},{12... | collective-permute-start | bytes 786440 | tf_op jit(solution)/shard_map/ppermute | solution.py:22
  86.0 22.5 %collective-permute-start.15 = (bf16[2,256,256]{2,1,0:T(8,128)(2,1)}, bf16[2,256,256]{2,1,0:T(8,128)(2,1)S(1)}, u32[]{:S(2)}, u32[]{:S(2)}) collective-permute-start(bf16[2,256,256]{2,1,0:T(8,128)(2,1)} %get-tuple-element.224.refs_4_), channel_id=1, source_target_pairs={{0,2},{2,4},{4,6},{6,0},{1,3},{3,5},{5,7},{7,1},{8,10},{10,12},{12... | collective-permute-start | bytes 786440 | tf_op jit(solution)/shard_map/ppermute | solution.py:22
  93.2 21.4 %collective-permute-start.12 = (bf16[128,1024]{1,0:T(8,128)(2,1)S(1)}, bf16[128,1024]{1,0:T(8,128)(2,1)S(1)}, u32[]{:S(2)}, u32[]{:S(2)}) collective-permute-start(bf16[128,1024]{1,0:T(8,128)(2,1)S(1)} %get-tuple-element.221), channel_id=1, source_target_pairs={{0,6},{2,0},{4,2},{6,4},{1,7},{3,1},{5,3},{7,5},{8,14},{10,8},{12,... | collective-permute-start | bytes 786440 | tf_op jit(solution)/shard_map/ppermute | solution.py:22
  99.9 21.4 %collective-permute-start.14 = (bf16[128,1024]{1,0:T(8,128)(2,1)S(1)}, bf16[128,1024]{1,0:T(8,128)(2,1)S(1)}, u32[]{:S(2)}, u32[]{:S(2)}) collective-permute-start(bf16[128,1024]{1,0:T(8,128)(2,1)S(1)} %get-tuple-element.223), channel_id=1, source_target_pairs={{0,2},{2,4},{4,6},{6,0},{1,3},{3,5},{5,7},{7,1},{8,10},{10,12},{12... | collective-permute-start | bytes 786440 | tf_op jit(solution)/shard_map/ppermute | solution.py:22
  106.8 30.5 %collective-permute-start.24 = (bf16[512,1024]{1,0:T(8,128)(2,1)}, bf16[512,1024]{1,0:T(8,128)(2,1)}, u32[]{:S(2)}, u32[]{:S(2)}) collective-permute-start(bf16[512,1024]{1,0:T(8,128)(2,1)} %get-tuple-element.235.refs_4_), channel_id=1, source_target_pairs={{0,1},{1,0},{2,3},{3,2},{4,5},{5,4},{6,7},{7,6},{8,9},{9,8},{10,11... | collective-permute-start | bytes 3145736 | tf_op jit(solution)/shard_map/ppermute | solution.py:22
  108.5 28.8 %collective-permute-start.25 = (bf16[512,1024]{1,0:T(8,128)(2,1)}, bf16[512,1024]{1,0:T(8,128)(2,1)}, u32[]{:S(2)}, u32[]{:S(2)}) collective-permute-start(bf16[512,1024]{1,0:T(8,128)(2,1)} %get-tuple-element.236.refs_5_), channel_id=1, source_target_pairs={{0,1},{1,0},{2,3},{3,2},{4,5},{5,4},{6,7},{7,6},{8,9},{9,8},{10,11... | collective-permute-start | bytes 3145736 | tf_op jit(solution)/shard_map/ppermute | solution.py:22
  203.2 26.2 %collective-permute-start.43 = (bf16[512,1024]{1,0:T(8,128)(2,1)S(1)}, bf16[512,1024]{1,0:T(8,128)(2,1)S(1)}, u32[]{:S(2)}, u32[]{:S(2)}) collective-permute-start(bf16[512,1024]{1,0:T(8,128)(2,1)S(1)} %copy-done.64), channel_id=1, source_target_pairs={{0,1},{1,0},{2,3},{3,2},{4,5},{5,4},{6,7},{7,6},{8,9},{9,8},{10,11... | collective-permute-start | bytes 3145736 | tf_op jit(solution)/shard_map/ppermute | solution.py:22
  204.4 27.5 %collective-permute-start.44 = (bf16[512,1024]{1,0:T(8,128)(2,1)S(1)}, bf16[512,1024]{1,0:T(8,128)(2,1)S(1)}, u32[]{:S(2)}, u32[]{:S(2)}) collective-permute-start(bf16[512,1024]{1,0:T(8,128)(2,1)S(1)} %copy-done.65), channel_id=1, source_target_pairs={{0,1},{1,0},{2,3},{3,2},{4,5},{5,4},{6,7},{7,6},{8,9},{9,8},{10,11... | collective-permute-start | bytes 3145736 | tf_op jit(solution)/shard_map/ppermute | solution.py:22
  229.4 21.1 %collective-permute-start.50 = (bf16[128,1024]{1,0:T(8,128)(2,1)S(1)}, bf16[128,1024]{1,0:T(8,128)(2,1)S(1)}, u32[]{:S(2)}, u32[]{:S(2)}) collective-permute-start(bf16[128,1024]{1,0:T(8,128)(2,1)S(1)} %copy-done.12), channel_id=1, source_target_pairs={{0,6},{2,0},{4,2},{6,4},{1,7},{3,1},{5,3},{7,5},{8,14},{10,8},{12,... | collective-permute-start | bytes 786440 | tf_op jit(solution)/shard_map/ppermute | solution.py:22
  231.9 19.6 %collective-permute-start.49 = (bf16[128,1024]{1,0:T(8,128)(2,1)S(1)}, bf16[128,1024]{1,0:T(8,128)(2,1)S(1)}, u32[]{:S(2)}, u32[]{:S(2)}) collective-permute-start(bf16[128,1024]{1,0:T(8,128)(2,1)S(1)} %copy-done.12), channel_id=1, source_target_pairs={{0,4},{2,6},{4,0},{6,2},{1,5},{3,7},{5,1},{7,3},{8,12},{10,14},{12... | collective-permute-start | bytes 786440 | tf_op jit(solution)/shard_map/ppermute | solution.py:22
  235.4 20.1 %collective-permute-start.48 = (bf16[128,1024]{1,0:T(8,128)(2,1)S(1)}, bf16[128,1024]{1,0:T(8,128)(2,1)S(1)}, u32[]{:S(2)}, u32[]{:S(2)}) collective-permute-start(bf16[128,1024]{1,0:T(8,128)(2,1)S(1)} %copy-done.12), channel_id=1, source_target_pairs={{0,2},{2,4},{4,6},{6,0},{1,3},{3,5},{5,7},{7,1},{8,10},{10,12},{12... | collective-permute-start | bytes 786440 | tf_op jit(solution)/shard_map/ppermute | solution.py:22
  296.7 207.6 %reduce-scatter.4.cloned.1.call-start = ((), (), s32[]{:S(2)}) async-start(), calls=%async_computation.4 | async-start | bytes 3538944 | tf_op jit(solution)/shard_map/reduce_scatter | solution.py:1120
  348.2 26.1 %collective-permute-start.79 = (bf16[256,1024]{1,0:T(8,128)(2,1)S(1)}, bf16[256,1024]{1,0:T(8,128)(2,1)S(1)}, u32[]{:S(2)}, u32[]{:S(2)}) collective-permute-start(bf16[256,1024]{1,0:T(8,128)(2,1)S(1)} %get-tuple-element.329), channel_id=1, source_target_pairs={{0,1},{1,0},{2,3},{3,2},{4,5},{5,4},{6,7},{7,6},{8,9},{9,8},{10,11... | collective-permute-start | bytes 1572872 | tf_op jit(solution)/shard_map/ppermute | solution.py:22
  388.5 115.9 %reduce-scatter.8.cloned.1.call-start = ((), (), s32[]{:S(2)}) async-start(), calls=%async_computation.6 | async-start | bytes 655360 | tf_op jit(solution)/shard_map/reduce_scatter | solution.py:1310
  408.0 23.5 %collective-permute-start.86 = (bf16[2,128,1024]{2,1,0:T(8,128)(2,1)S(1)}, bf16[2,128,1024]{2,1,0:T(8,128)(2,1)S(1)}, u32[]{:S(2)}, u32[]{:S(2)}) collective-permute-start(bf16[2,128,1024]{2,1,0:T(8,128)(2,1)S(1)} %get-tuple-element.355), channel_id=1, source_target_pairs={{0,16},{8,24},{16,0},{24,8},{1,17},{9,25},{17,1},{25,9},{2,18},{10... | collective-permute-start | bytes 1572872 | tf_op jit(solution)/shard_map/ppermute | solution.py:22
  410.6 37.0 %collective-permute-start.87 = (bf16[2,128,1024]{2,1,0:T(8,128)(2,1)S(1)}, bf16[2,128,1024]{2,1,0:T(8,128)(2,1)S(1)}, u32[]{:S(2)}, u32[]{:S(2)}) collective-permute-start(bf16[2,128,1024]{2,1,0:T(8,128)(2,1)S(1)} %get-tuple-element.356), channel_id=1, source_target_pairs={{0,8},{8,16},{16,24},{24,0},{1,9},{9,17},{17,25},{25,1},{2,10},{10... | collective-permute-start | bytes 1572872 | tf_op jit(solution)/shard_map/ppermute | solution.py:22
  411.1 39.0 %collective-permute-start.85 = (bf16[2,128,1024]{2,1,0:T(8,128)(2,1)S(1)}, bf16[2,128,1024]{2,1,0:T(8,128)(2,1)S(1)}, u32[]{:S(2)}, u32[]{:S(2)}) collective-permute-start(bf16[2,128,1024]{2,1,0:T(8,128)(2,1)S(1)} %get-tuple-element.340.refs_12_), channel_id=1, source_target_pairs={{0,24},{8,0},{16,8},{24,16},{1,25},{9,1},{17,9},{25,17},{2,26},{10... | collective-permute-start | bytes 1572872 | tf_op jit(solution)/shard_map/ppermute | solution.py:22
  428.8 22.8 %collective-permute-start.84 = (bf16[4,128,512]{2,1,0:T(8,128)(2,1)S(1)}, bf16[4,128,512]{2,1,0:T(8,128)(2,1)S(1)}, u32[]{:S(2)}, u32[]{:S(2)}) collective-permute-start(bf16[4,128,512]{2,1,0:T(8,128)(2,1)S(1)} %get-tuple-element.343), channel_id=1, source_target_pairs={{0,1},{1,0},{2,3},{3,2},{4,5},{5,4},{6,7},{7,6},{8,9},{9,8},{10,11... | collective-permute-start | bytes 1572872 | tf_op jit(solution)/shard_map/ppermute | solution.py:22
  454.4 18.9 %collective-permute-start.88 = (bf16[256,1024]{1,0:T(8,128)(2,1)S(1)}, bf16[256,1024]{1,0:T(8,128)(2,1)S(1)}, u32[]{:S(2)}, u32[]{:S(2)}) collective-permute-start(bf16[256,1024]{1,0:T(8,128)(2,1)S(1)} %get-tuple-element.363), channel_id=1, source_target_pairs={{0,1},{1,0},{2,3},{3,2},{4,5},{5,4},{6,7},{7,6},{8,9},{9,8},{10,11... | collective-permute-start | bytes 1572872 | tf_op jit(solution)/shard_map/ppermute | solution.py:22
  483.2 100.5 %all-gather.5.cloned.1.call-start = ((), (), s32[]{:S(2)}) async-start(), calls=%async_computation.7 | async-start | bytes 5013504 | tf_op jit(solution)/shard_map/all_gather | solution.py:1326
  485.6 18.7 %collective-permute-start.98 = (bf16[2,96,1024]{2,1,0:T(8,128)(2,1)S(1)}, bf16[2,96,1024]{2,1,0:T(8,128)(2,1)S(1)}, u32[]{:S(2)}, u32[]{:S(2)}) collective-permute-start(bf16[2,96,1024]{2,1,0:T(8,128)(2,1)S(1)} %get-tuple-element.379), channel_id=1, source_target_pairs={{0,8},{8,16},{16,24},{24,0},{1,9},{9,17},{17,25},{25,1},{2,10},{10... | collective-permute-start | bytes 1179656 | tf_op jit(solution)/shard_map/ppermute | solution.py:22
  485.6 18.7 %collective-permute-start.96 = (bf16[2,96,1024]{2,1,0:T(8,128)(2,1)S(1)}, bf16[2,96,1024]{2,1,0:T(8,128)(2,1)S(1)}, u32[]{:S(2)}, u32[]{:S(2)}) collective-permute-start(bf16[2,96,1024]{2,1,0:T(8,128)(2,1)S(1)} %get-tuple-element.368.refs_13_), channel_id=1, source_target_pairs={{0,24},{8,0},{16,8},{24,16},{1,25},{9,1},{17,9},{25,17},{2,26},{10... | collective-permute-start | bytes 1179656 | tf_op jit(solution)/shard_map/ppermute | solution.py:22
  488.2 23.7 %collective-permute-start.93 = (bf16[144,1024]{1,0:T(8,128)(2,1)}, bf16[144,1024]{1,0:T(8,128)(2,1)S(1)}, u32[]{:S(2)}, u32[]{:S(2)}) collective-permute-start(bf16[144,1024]{1,0:T(8,128)(2,1)} %copy-done.57), channel_id=1, source_target_pairs={{0,6},{2,0},{4,2},{6,4},{1,7},{3,1},{5,3},{7,5},{8,14},{10,8},{12,... | collective-permute-start | bytes 884744 | tf_op jit(solution)/shard_map/ppermute | solution.py:22
  507.1 23.1 %collective-permute-start.100 = (bf16[256,1024]{1,0:T(8,128)(2,1)S(1)}, bf16[256,1024]{1,0:T(8,128)(2,1)S(1)}, u32[]{:S(2)}, u32[]{:S(2)}) collective-permute-start(bf16[256,1024]{1,0:T(8,128)(2,1)S(1)} %get-tuple-element.387), channel_id=1, source_target_pairs={{0,64},{64,0},{1,65},{65,1},{2,66},{66,2},{3,67},{67,3},{4,68},{68... | collective-permute-start | bytes 1572872 | tf_op jit(solution)/shard_map/ppermute | solution.py:22
  510.7 19.5 %collective-permute-start.101 = (bf16[128,1024]{1,0:T(8,128)(2,1)S(1)}, bf16[128,1024]{1,0:T(8,128)(2,1)S(1)}, u32[]{:S(2)}, u32[]{:S(2)}) collective-permute-start(bf16[128,1024]{1,0:T(8,128)(2,1)S(1)} %get-tuple-element.386), channel_id=1, source_target_pairs={{64,32},{96,0},{65,33},{97,1},{66,34},{98,2},{67,35},{99,3},{68,36... | collective-permute-start | bytes 786440 | tf_op jit(solution)/shard_map/ppermute | solution.py:899
  512.0 18.2 %collective-permute-start.99 = (bf16[128,1024]{1,0:T(8,128)(2,1)S(1)}, bf16[128,1024]{1,0:T(8,128)(2,1)S(1)}, u32[]{:S(2)}, u32[]{:S(2)}) collective-permute-start(bf16[128,1024]{1,0:T(8,128)(2,1)S(1)} %get-tuple-element.386), channel_id=1, source_target_pairs={{0,32},{32,0},{1,33},{33,1},{2,34},{34,2},{3,35},{35,3},{4,36},{36... | collective-permute-start | bytes 786440 | tf_op jit(solution)/shard_map/ppermute | solution.py:22
  534.8 60.0 %collective-permute-start.103 = (bf16[256,1024]{1,0:T(8,128)(2,1)S(1)}, bf16[256,1024]{1,0:T(8,128)(2,1)S(1)}, u32[]{:S(2)}, u32[]{:S(2)}) collective-permute-start(bf16[256,1024]{1,0:T(8,128)(2,1)S(1)} %other_layer_kernel.1), channel_id=1, source_target_pairs={{0,64},{64,0},{1,65},{65,1},{2,66},{66,2},{3,67},{67,3},{4,68},{68... | collective-permute-start | bytes 1572872 | tf_op jit(solution)/shard_map/ppermute | solution.py:22
  (150 other events, 2078.4 us)
Sparse Core Ops, SparseCore 0:
  40.5 77.5 all-gather.2
  296.8 71.9 reduce-scatter.5
  388.6 64.7 reduce-scatter.3
  483.3 18.8 reduce-scatter.7
  532.6 51.0 all-gather.4

commit v5 on v4

--- a/solution.py
+++ b/solution.py
@@ -1091,14 +1091,15 @@
     if layer == 0:
         share, *others = call(cross_sum_kernel, [ROW, ROW16, ROW16, ROW16], middle)
         self_parts, theirs = self_grads([share])
-        waits = steps["late"]([share, *send_x(others)], self_parts, theirs)
+        shares = [share, *send_x(others)]
         tall = struct((BLOCK + 16, 1024), BF16)
         near, *others, sums = call(
             last_rows_back_kernel,
             [ROW, tall, tall, tall, struct((16, 1024), F32)],
             [*back, *cold(*own, *far, all1, norms2, norms3, *steps["norms"])],
-            after=waits,
+            after=[theirs[0]],
         )
+        steps["late"](shares, self_parts, near)
         steps["tail"]["near"] = near
         g0, sums = call(
             last_sum_back_kernel,
@@ -1280,15 +1281,15 @@
         arrived = [shift(c, "dy", -k) for k, c in enumerate(chunks_of[1:], 1)]
         return [*cold(chunks_of[0]), *arrived, *keys], [chunks_of[1]]
 
-    def late_first(cross_parts, self_parts, theirs):
+    def late_first(cross_parts, self_parts, near):
         *tail["chunks"], tail["cross"] = call(
             rest_chunk_kernel,
             chunk_shapes(96) + cold(struct((2, 32, 1024), F32)),
             [*self_parts, *cross_parts, *cold(memory)],
             scalars=[place],
             scratch=[pltpu.VMEM((768, 1024), F32)],
+            after=[near],
         )
-        return [tail["chunks"][1]]
 
     input_grad, _, _, norms = layer_back(
         0, text_grad, gather_x(text_grad), stored0, weights[0], ffns, place, source_lengths, norms[0],
@@ -1305,7 +1306,7 @@
         split_kernel,
         cold(row16, struct((256, 1024), BF16)),
         cold(grads_a),
-        after=[tail["near"]],
+        after=[tail["chunks"][1]],
     )
     cross1 = lax.psum_scatter(cross1, "tx", scatter_dimension=0, tiled=True)
     chunks_of = tail["chunks"]

time: 612 us -> 607 us (level)
    ppermute x104, waiting for transfers between devices: 263 us -> 257 us  [shift(): lax.ppermute(value, axis, [(i, (i + steps) % count) for i in range(count)])]
  transfers between devices with their start and end apart: 110 -> 110, of which waited for: 67 -> 66; matrix products, arithmetic and copies ran while one was open for 0% -> 0% of each run, Pallas kernels for 25% -> 25%
where the time goes in v5:
time: 607 us; the launch traced here: 600 us
  waiting for transfers between devices  306 us (50%)
  Pallas kernels  176 us (29%)
  starting transfers between devices  90.1 us (15%)
  between operations  15.5 us (3%)
  local copies, waits for them, and re-layouts  12 us (2%)
    ppermute x104, waiting for transfers between devices, shift(): lax.ppermute(value, axis, [(i, (i + steps) % count) for i in range(count)])  257 us
    pallas_call x55, Pallas kernels, call(): pl.pallas_call(body, name=name, out_shape=[pltpu.HBM(o.shape, o.dtype) if...  176 us
    ppermute x104, starting transfers between devices, shift(): lax.ppermute(value, axis, [(i, (i + steps) % count) for i in range(count)])  88.7 us
    all_gather x1, waiting for transfers between devices, shards(): whole = lax.all_gather(last, ('dz', 'dy'), axis=0, tiled=True)  48.4 us
  transfers between devices with their start and end apart: 110, of which 66 were waited for; matrix products, arithmetic and copies ran while one was open for 0% of the time, Pallas kernels for 25%

profile of v5, /device:TPU:1, one launch (start us, length us, event | category | flops | bytes accessed | tf_op | source)
XLA Modules:
  0.0 599.5 jit_solution(3872309192223626055)
XLA Ops:
  22.4 6.3 %collective-permute-done.4.refs_2_.refs_1_ = f32[6,1024]{1,0:T(8,128)S(1)} collective-permute-done((f32[6,1024]{1,0:T(8,128)S(1)}, f32[6,1024]{1,0:T(8,128)S(1)}, u32[]{:S(2)}, u32[]{:S(2)}) %collective-permute-start.4) | collective-permute-done | bytes 24608 | tf_op jit(solution)/shard_map/ppermute | solution.py:22
  30.9 8.6 %collective-permute-done.refs_3_.refs_1_.refs_6_ = bf16[160,1024]{1,0:T(8,128)(2,1)S(1)} collective-permute-done((bf16[160,1024]{1,0:T(8,128)(2,1)}, bf16[160,1024]{1,0:T(8,128)(2,1)S(1)}, u32[]{:S(2)}, u32[]{:S(2)}) %collective-permute-start) | collective-permute-done | bytes 327712 | tf_op jit(solution)/shard_map/ppermute | solution.py:22
  50.3 5.9 collective-permute-done.7.refs_5_.refs_4_
  59.7 11.5 %collective-permute-done.5.refs_3_.refs_2_ = bf16[256,768]{1,0:T(8,128)(2,1)S(1)} collective-permute-done((bf16[256,768]{1,0:T(8,128)(2,1)S(1)}, bf16[256,768]{1,0:T(8,128)(2,1)S(1)}, u32[]{:S(2)}, u32[]{:S(2)}) %collective-permute-start.5) | collective-permute-done | bytes 393248 | tf_op jit(solution)/shard_map/ppermute | solution.py:22
  87.2 6.0 %self_forward_kernel.2 = (bf16[4,128,256]{2,1,0:T(8,128)(2,1)}, f32[4,4,1,128]{3,2,1,0:T(1,128)}, f32[128,1024]{1,0:T(8,128)S(1)}, bf16[128,1024]{1,0:T(8,128)(2...) custom-call(bf16[4,128,256]{2,1,0:T(8,128)(2,1)S(1)} %get-tuple-element.218.refs_0_.refs_10_.refs_8_, ...), custom_call_target="tpu_custom_call" | custom-call | tf_op jit(solution)/shard_map/self_forward_kernel/pallas_call | solution.py:167
  108.7 5.9 collective-permute-done.12.refs_2_
  124.4 6.5 %cross_forward_kernel.2 = (bf16[256,512]{1,0:T(8,128)(2,1)S(1)}, bf16[256,512]{1,0:T(8,128)(2,1)S(1)}, f32[8,1,256]{2,1,0:T(1,128)S(1)}, f32[128,1024]{1,0:T(8,128)S(1)}, bf16[128,1024]{1,0:T(8,128)(2,1)S(1)}) custom-call(s32[2,1]{1,0:T(2,128)S(1)} %copy.35.refs_0_, bf16[128,1024]{1,0:T(8,128)(2,1)S(1)} %get-tuple-element.229.refs_1_.refs_4_, ...), custom_call_target="tpu_custom_call" | custom-call | tf_op jit(solution)/shard_map/cross_forward_kernel/pallas_call | solution.py:167
  144.7 6.6 %collective-permute-done.21.refs_1_.refs_7_ = bf16[128,1024]{1,0:T(8,128)(2,1)S(1)} collective-permute-done((bf16[128,1024]{1,0:T(8,128)(2,1)S(1)}, bf16[128,1024]{1,0:T(8,128)(2,1)S(1)}, u32[]{:S(2)}, u32[]{:S(2)}) %collective-permute-start.21) | collective-permute-done | bytes 262176 | tf_op jit(solution)/shard_map/ppermute | solution.py:22
  165.9 7.1 %collective-permute-done.28.refs_4_ = bf16[128,1024]{1,0:T(8,128)(2,1)S(1)} collective-permute-done((bf16[128,1024]{1,0:T(8,128)(2,1)S(1)}, bf16[128,1024]{1,0:T(8,128)(2,1)S(1)}, u32[]{:S(2)}, u32[]{:S(2)}) %collective-permute-start.28) | collective-permute-done | bytes 262176 | tf_op jit(solution)/shard_map/ppermute | solution.py:22
  182.0 7.6 %collective-permute-done.29.refs_1_.refs_9_ = bf16[128,1024]{1,0:T(8,128)(2,1)S(1)} collective-permute-done((bf16[128,1024]{1,0:T(8,128)(2,1)S(1)}, bf16[128,1024]{1,0:T(8,128)(2,1)S(1)}, u32[]{:S(2)}, u32[]{:S(2)}) %collective-permute-start.29) | collective-permute-done | bytes 262176 | tf_op jit(solution)/shard_map/ppermute | solution.py:22
  194.4 6.3 %self_forward_kernel.3 = (bf16[4,128,256]{2,1,0:T(8,128)(2,1)S(1)}, f32[4,4,1,128]{3,2,1,0:T(1,128)S(1)}, f32[128,1024]{1,0:T(8,128)S(1)}, bf16[128,1024]{1,0:T(...) custom-call(bf16[4,128,256]{2,1,0:T(8,128)(2,1)S(1)} %get-tuple-element.246.refs_0_.refs_8_, ...), custom_call_target="tpu_custom_call" | custom-call | tf_op jit(solution)/shard_map/self_forward_kernel/pallas_call | solution.py:167
  210.8 6.6 %collective-permute-done.37.refs_4_ = bf16[128,1024]{1,0:T(8,128)(2,1)S(1)} collective-permute-done((bf16[128,1024]{1,0:T(8,128)(2,1)S(1)}, bf16[128,1024]{1,0:T(8,128)(2,1)S(1)}, u32[]{:S(2)}, u32[]{:S(2)}) %collective-permute-start.37) | collective-permute-done | bytes 262176 | tf_op jit(solution)/shard_map/ppermute | solution.py:22
  219.5 6.5 %cross_forward_kernel.3 = (bf16[256,512]{1,0:T(8,128)(2,1)S(1)}, bf16[256,512]{1,0:T(8,128)(2,1)S(1)}, f32[8,1,256]{2,1,0:T(1,128)S(1)}, f32[128,1024]{1,0:T(8,128)S(1)}, bf16[128,1024]{1,0:T(8,128)(2,1)S(1)}) custom-call(s32[2,1]{1,0:T(2,128)S(1)} %copy.35.refs_0_, bf16[128,1024]{1,0:T(8,128)(2,1)S(1)} %get-tuple-element.253.refs_1_.refs_9_, ...), custom_call_target="tpu_custom_call" | custom-call | tf_op jit(solution)/shard_map/cross_forward_kernel/pallas_call | solution.py:167
  237.0 7.6 %collective-permute-done.40.refs_1_.refs_7_ = bf16[128,1024]{1,0:T(8,128)(2,1)S(1)} collective-permute-done((bf16[128,1024]{1,0:T(8,128)(2,1)S(1)}, bf16[128,1024]{1,0:T(8,128)(2,1)S(1)}, u32[]{:S(2)}, u32[]{:S(2)}) %collective-permute-start.40) | collective-permute-done | bytes 262176 | tf_op jit(solution)/shard_map/ppermute | solution.py:22
  271.2 6.0 %collective-permute-done.53.refs_4_ = bf16[128,1024]{1,0:T(8,128)(2,1)S(1)} collective-permute-done((bf16[128,1024]{1,0:T(8,128)(2,1)S(1)}, bf16[128,1024]{1,0:T(8,128)(2,1)S(1)}, u32[]{:S(2)}, u32[]{:S(2)}) %collective-permute-start.53) | collective-permute-done | bytes 262176 | tf_op jit(solution)/shard_map/ppermute | solution.py:22
  280.5 8.2 %cross_back_kernel.2 = (bf16[256,512]{1,0:T(8,128)(2,1)S(1)}, bf16[256,256]{1,0:T(8,128)(2,1)S(1)}, bf16[256,256]{1,0:T(8,128)(2,1)S(1)}, bf16[256,256]{1,0:T(8,...) custom-call(s32[2,1]{1,0:T(2,128)S(1)} %copy.35.refs_0_, ...), custom_call_target="tpu_custom_call" | custom-call | tf_op jit(solution)/shard_map/cross_back_kernel/pallas_call | solution.py:167
  298.4 6.0 %collective-permute-done.58.refs_3_.refs_4_ = bf16[128,1024]{1,0:T(8,128)(2,1)S(1)} collective-permute-done((bf16[128,1024]{1,0:T(8,128)(2,1)S(1)}, bf16[128,1024]{1,0:T(8,128)(2,1)S(1)}, u32[]{:S(2)}, u32[]{:S(2)}) %collective-permute-start.58) | collective-permute-done | bytes 262176 | tf_op jit(solution)/shard_map/ppermute | solution.py:22
  306.4 6.7 %collective-permute-done.56.refs_1_.refs_2_ = bf16[128,1024]{1,0:T(8,128)(2,1)S(1)} collective-permute-done((bf16[128,1024]{1,0:T(8,128)(2,1)S(1)}, bf16[128,1024]{1,0:T(8,128)(2,1)S(1)}, u32[]{:S(2)}, u32[]{:S(2)}) %collective-permute-start.56) | collective-permute-done | bytes 262176 | tf_op jit(solution)/shard_map/ppermute | solution.py:22
  313.1 9.8 %self_back_kernel.2 = (bf16[4,128,256]{2,1,0:T(8,128)(2,1)S(1)}, f32[4,128,512]{2,1,0:T(8,128)S(1)}, bf16[4,128,512]{2,1,0:T(8,128)(2,1)S(1)}) custom-call(bf16[128,1024]{1,0:T(8,128)(2,1)S(1)} %get-tuple-element.284.refs_16_.refs_0_.refs_1_, bf16[128,1024]{1,0:T(8,128)(2,1)S(1)} %collective-permute-done.56.refs_1_.refs_2_, ...), custom_call_target="tpu_custom_call" | custom-call | tf_op jit(solution)/shard_map/self_back_kernel/pallas_call | solution.py:167
  336.7 6.6 %collective-permute-done.66.refs_4_ = bf16[128,1024]{1,0:T(8,128)(2,1)S(1)} collective-permute-done((bf16[128,1024]{1,0:T(8,128)(2,1)S(1)}, bf16[128,1024]{1,0:T(8,128)(2,1)S(1)}, u32[]{:S(2)}, u32[]{:S(2)}) %collective-permute-start.66) | collective-permute-done | bytes 262176 | tf_op jit(solution)/shard_map/ppermute | solution.py:22
  354.7 7.3 %collective-permute-done.67.refs_1_.refs_2_ = bf16[128,1024]{1,0:T(8,128)(2,1)S(1)} collective-permute-done((bf16[128,1024]{1,0:T(8,128)(2,1)S(1)}, bf16[128,1024]{1,0:T(8,128)(2,1)S(1)}, u32[]{:S(2)}, u32[]{:S(2)}) %collective-permute-start.67) | collective-permute-done | bytes 262176 | tf_op jit(solution)/shard_map/ppermute | solution.py:22
  390.0 8.3 %cross_back_kernel.3 = (bf16[256,512]{1,0:T(8,128)(2,1)S(1)}, bf16[256,256]{1,0:T(8,128)(2,1)S(1)}, bf16[256,256]{1,0:T(8,128)(2,1)S(1)}, bf16[256,256]{1,0:T(8,...) custom-call(s32[2,1]{1,0:T(2,128)S(1)} %copy.35.refs_0_, ...), custom_call_target="tpu_custom_call" | custom-call | tf_op jit(solution)/shard_map/cross_back_kernel/pallas_call | solution.py:167
  413.2 5.6 collective-permute-done.81.refs_1_.refs_2_
  418.8 9.8 %self_back_kernel.3 = (bf16[4,128,256]{2,1,0:T(8,128)(2,1)S(1)}, f32[4,128,512]{2,1,0:T(8,128)S(1)}, bf16[4,128,512]{2,1,0:T(8,128)(2,1)S(1)}) custom-call(bf16[128,1024]{1,0:T(8,128)(2,1)S(1)} %get-tuple-element.336.refs_6_.refs_0_.refs_1_, bf16[128,1024]{1,0:T(8,128)(2,1)S(1)} %collective-permute-done.81.refs_1_.refs_2_, ...), custom_call_target="tpu_custom_call" | custom-call | tf_op jit(solution)/shard_map/self_back_kernel/pallas_call | solution.py:167
  431.1 16.2 %collective-permute-done.87.refs_3_ = bf16[2,128,1024]{2,1,0:T(8,128)(2,1)S(1)} collective-permute-done((bf16[2,128,1024]{2,1,0:T(8,128)(2,1)S(1)}, bf16[2,128,1024]{2,1,0:T(8,128)(2,1)S(1)}, u32[]{:S(2)}, u32[]{:S(2)}) %collective-permute-start.87) | collective-permute-done | bytes 524320 | tf_op jit(solution)/shard_map/ppermute | solution.py:22
  466.3 6.7 %collective-permute-done.95.refs_6_ = bf16[128,1024]{1,0:T(8,128)(2,1)S(1)} collective-permute-done((bf16[128,1024]{1,0:T(8,128)(2,1)S(1)}, bf16[128,1024]{1,0:T(8,128)(2,1)S(1)}, u32[]{:S(2)}, u32[]{:S(2)}) %collective-permute-start.95) | collective-permute-done | bytes 262176 | tf_op jit(solution)/shard_map/ppermute | solution.py:22
  482.8 6.8 %collective-permute-done.97.refs_2_ = bf16[2,96,1024]{2,1,0:T(8,128)(2,1)S(1)} collective-permute-done((bf16[2,96,1024]{2,1,0:T(8,128)(2,1)S(1)}, bf16[2,96,1024]{2,1,0:T(8,128)(2,1)S(1)}, u32[]{:S(2)}, u32[]{:S(2)}) %collective-permute-start.97) | collective-permute-done | bytes 393248 | tf_op jit(solution)/shard_map/ppermute | solution.py:22
  489.6 9.2 %collective-permute-done.98.refs_3_ = bf16[2,96,1024]{2,1,0:T(8,128)(2,1)S(1)} collective-permute-done((bf16[2,96,1024]{2,1,0:T(8,128)(2,1)S(1)}, bf16[2,96,1024]{2,1,0:T(8,128)(2,1)S(1)}, u32[]{:S(2)}, u32[]{:S(2)}) %collective-permute-start.98) | collective-permute-done | bytes 393248 | tf_op jit(solution)/shard_map/ppermute | solution.py:22
  506.5 7.3 %collective-permute-done.89.refs_3_ = bf16[144,1024]{1,0:T(8,128)(2,1)S(1)} collective-permute-done((bf16[144,1024]{1,0:T(8,128)(2,1)}, bf16[144,1024]{1,0:T(8,128)(2,1)S(1)}, u32[]{:S(2)}, u32[]{:S(2)}) %collective-permute-start.89) | collective-permute-done | bytes 294944 | tf_op jit(solution)/shard_map/ppermute | solution.py:22
  513.8 7.4 %collective-permute-done.90.refs_4_ = bf16[144,1024]{1,0:T(8,128)(2,1)S(1)} collective-permute-done((bf16[144,1024]{1,0:T(8,128)(2,1)S(1)}, bf16[144,1024]{1,0:T(8,128)(2,1)S(1)}, u32[]{:S(2)}, u32[]{:S(2)}) %collective-permute-start.90) | collective-permute-done | bytes 294944 | tf_op jit(solution)/shard_map/ppermute | solution.py:22
  530.1 48.4 %all-gather.5.cloned.1.call-done.refs_0_ = bf16[2176,1024]{1,0:T(8,128)(2,1)} async-done(((bf16[272,1024]{1,0:T(8,128)(2,1)}), bf16[2176,1024]{1,0:T(8,128)(2,1)}) %all-gather.5.cloned.1.call-update) | async-done | bytes 4456464 | tf_op jit(solution)/shard_map/all_gather | solution.py:1327
  583.5 6.1 %last_kernel.1 = (f32[128,1024]{1,0:T(8,128)}, f32[3,1024,128]{2,1,0:T(8,128)}, f32[1024,128]{1,0:T(8,128)}, f32[128,1024]{1,0:T(8,128)}, f32[2048,128]{1,0:T(8,...) custom-call(bf16[2176,1024]{1,0:T(8,128)(2,1)} %all-gather.5.cloned.1.call-done.refs_0_, ...), custom_call_target="tpu_custom_call" | custom-call | tf_op jit(solution)/shard_map/last_kernel/pallas_call | solution.py:167
  (398 shorter events, 302.4 us)
Async XLA Ops:
  7.2 117.2 %all-gather.3.cloned.1.call-start = ((), (), s32[]{:S(2)}) async-start(), calls=%async_computation.3 | async-start | bytes 4456448 | tf_op jit(solution)/shard_map/all_gather | solution.py:1197
  11.8 27.7 %collective-permute-start.3 = (bf16[256,1024]{1,0:T(8,128)(2,1)S(1)}, bf16[256,1024]{1,0:T(8,128)(2,1)S(1)}, u32[]{:S(2)}, u32[]{:S(2)}) collective-permute-start(bf16[256,1024]{1,0:T(8,128)(2,1)S(1)} %get-tuple-element.208.refs_3_.refs_2_.refs_0_), channel_id=1, source_target_pairs={{0,64},{64,0},{1,65},{65,1},{2,66},{66,2},{3,67},{67,3},{4,68},{68... | collective-permute-start | bytes 1572872 | tf_op jit(solution)/shard_map/ppermute | solution.py:22
  40.4 435.3 %reduce-scatter.6.cloned.1.call-start = ((), (), s32[]{:S(2)}) async-start(), calls=%async_computation.5 | async-start | bytes 7077888 | tf_op jit(solution)/shard_map/reduce_scatter | solution.py:1121
  43.5 56.4 %collective-permute-start.18 = (bf16[1024,1024]{1,0:T(8,128)(2,1)}, bf16[1024,1024]{1,0:T(8,128)(2,1)S(1)}, u32[]{:S(2)}, u32[]{:S(2)}) collective-permute-start(bf16[1024,1024]{1,0:T(8,128)(2,1)} %get-tuple-element.225.refs_0_), channel_id=1, source_target_pairs={{0,64},{64,0},{1,65},{65,1},{2,66},{66,2},{3,67},{67,3},{4,68},{68... | collective-permute-start | bytes 6291464 | tf_op jit(solution)/shard_map/ppermute | solution.py:22
  46.8 24.5 %collective-permute-start.5 = (bf16[256,768]{1,0:T(8,128)(2,1)S(1)}, bf16[256,768]{1,0:T(8,128)(2,1)S(1)}, u32[]{:S(2)}, u32[]{:S(2)}) collective-permute-start(bf16[256,768]{1,0:T(8,128)(2,1)S(1)} %get-tuple-element.213.refs_2_.refs_1_), channel_id=1, source_target_pairs={{0,8},{8,16},{16,24},{24,0},{1,9},{9,17},{17,25},{25,1},{2,10},{10... | collective-permute-start | bytes 1179656 | tf_op jit(solution)/shard_map/ppermute | solution.py:22
  85.6 21.3 %collective-permute-start.16 = (bf16[2,256,256]{2,1,0:T(8,128)(2,1)}, bf16[2,256,256]{2,1,0:T(8,128)(2,1)S(1)}, u32[]{:S(2)}, u32[]{:S(2)}) collective-permute-start(bf16[2,256,256]{2,1,0:T(8,128)(2,1)} %get-tuple-element.224.refs_4_), channel_id=1, source_target_pairs={{0,4},{2,6},{4,0},{6,2},{1,5},{3,7},{5,1},{7,3},{8,12},{10,14},{12... | collective-permute-start | bytes 786440 | tf_op jit(solution)/shard_map/ppermute | solution.py:22
  86.1 22.4 %collective-permute-start.15 = (bf16[2,256,256]{2,1,0:T(8,128)(2,1)}, bf16[2,256,256]{2,1,0:T(8,128)(2,1)S(1)}, u32[]{:S(2)}, u32[]{:S(2)}) collective-permute-start(bf16[2,256,256]{2,1,0:T(8,128)(2,1)} %get-tuple-element.224.refs_4_), channel_id=1, source_target_pairs={{0,2},{2,4},{4,6},{6,0},{1,3},{3,5},{5,7},{7,1},{8,10},{10,12},{12... | collective-permute-start | bytes 786440 | tf_op jit(solution)/shard_map/ppermute | solution.py:22
  93.2 21.3 %collective-permute-start.12 = (bf16[128,1024]{1,0:T(8,128)(2,1)S(1)}, bf16[128,1024]{1,0:T(8,128)(2,1)S(1)}, u32[]{:S(2)}, u32[]{:S(2)}) collective-permute-start(bf16[128,1024]{1,0:T(8,128)(2,1)S(1)} %get-tuple-element.221), channel_id=1, source_target_pairs={{0,6},{2,0},{4,2},{6,4},{1,7},{3,1},{5,3},{7,5},{8,14},{10,8},{12,... | collective-permute-start | bytes 786440 | tf_op jit(solution)/shard_map/ppermute | solution.py:22
  99.9 21.4 %collective-permute-start.14 = (bf16[128,1024]{1,0:T(8,128)(2,1)S(1)}, bf16[128,1024]{1,0:T(8,128)(2,1)S(1)}, u32[]{:S(2)}, u32[]{:S(2)}) collective-permute-start(bf16[128,1024]{1,0:T(8,128)(2,1)S(1)} %get-tuple-element.223), channel_id=1, source_target_pairs={{0,2},{2,4},{4,6},{6,0},{1,3},{3,5},{5,7},{7,1},{8,10},{10,12},{12... | collective-permute-start | bytes 786440 | tf_op jit(solution)/shard_map/ppermute | solution.py:22
  106.9 30.5 %collective-permute-start.24 = (bf16[512,1024]{1,0:T(8,128)(2,1)}, bf16[512,1024]{1,0:T(8,128)(2,1)S(1)}, u32[]{:S(2)}, u32[]{:S(2)}) collective-permute-start(bf16[512,1024]{1,0:T(8,128)(2,1)} %get-tuple-element.235.refs_4_), channel_id=1, source_target_pairs={{0,1},{1,0},{2,3},{3,2},{4,5},{5,4},{6,7},{7,6},{8,9},{9,8},{10,11... | collective-permute-start | bytes 3145736 | tf_op jit(solution)/shard_map/ppermute | solution.py:22
  108.6 28.8 %collective-permute-start.25 = (bf16[512,1024]{1,0:T(8,128)(2,1)}, bf16[512,1024]{1,0:T(8,128)(2,1)S(1)}, u32[]{:S(2)}, u32[]{:S(2)}) collective-permute-start(bf16[512,1024]{1,0:T(8,128)(2,1)} %get-tuple-element.236.refs_5_), channel_id=1, source_target_pairs={{0,1},{1,0},{2,3},{3,2},{4,5},{5,4},{6,7},{7,6},{8,9},{9,8},{10,11... | collective-permute-start | bytes 3145736 | tf_op jit(solution)/shard_map/ppermute | solution.py:22
  203.2 26.2 %collective-permute-start.43 = (bf16[512,1024]{1,0:T(8,128)(2,1)S(1)}, bf16[512,1024]{1,0:T(8,128)(2,1)S(1)}, u32[]{:S(2)}, u32[]{:S(2)}) collective-permute-start(bf16[512,1024]{1,0:T(8,128)(2,1)S(1)} %copy-done.65), channel_id=1, source_target_pairs={{0,1},{1,0},{2,3},{3,2},{4,5},{5,4},{6,7},{7,6},{8,9},{9,8},{10,11... | collective-permute-start | bytes 3145736 | tf_op jit(solution)/shard_map/ppermute | solution.py:22
  204.4 27.5 %collective-permute-start.44 = (bf16[512,1024]{1,0:T(8,128)(2,1)S(1)}, bf16[512,1024]{1,0:T(8,128)(2,1)S(1)}, u32[]{:S(2)}, u32[]{:S(2)}) collective-permute-start(bf16[512,1024]{1,0:T(8,128)(2,1)S(1)} %copy-done.66), channel_id=1, source_target_pairs={{0,1},{1,0},{2,3},{3,2},{4,5},{5,4},{6,7},{7,6},{8,9},{9,8},{10,11... | collective-permute-start | bytes 3145736 | tf_op jit(solution)/shard_map/ppermute | solution.py:22
  229.5 21.1 %collective-permute-start.50 = (bf16[128,1024]{1,0:T(8,128)(2,1)S(1)}, bf16[128,1024]{1,0:T(8,128)(2,1)S(1)}, u32[]{:S(2)}, u32[]{:S(2)}) collective-permute-start(bf16[128,1024]{1,0:T(8,128)(2,1)S(1)} %copy-done.12), channel_id=1, source_target_pairs={{0,6},{2,0},{4,2},{6,4},{1,7},{3,1},{5,3},{7,5},{8,14},{10,8},{12,... | collective-permute-start | bytes 786440 | tf_op jit(solution)/shard_map/ppermute | solution.py:22
  231.9 19.6 %collective-permute-start.49 = (bf16[128,1024]{1,0:T(8,128)(2,1)S(1)}, bf16[128,1024]{1,0:T(8,128)(2,1)S(1)}, u32[]{:S(2)}, u32[]{:S(2)}) collective-permute-start(bf16[128,1024]{1,0:T(8,128)(2,1)S(1)} %copy-done.12), channel_id=1, source_target_pairs={{0,4},{2,6},{4,0},{6,2},{1,5},{3,7},{5,1},{7,3},{8,12},{10,14},{12... | collective-permute-start | bytes 786440 | tf_op jit(solution)/shard_map/ppermute | solution.py:22
  235.5 20.0 %collective-permute-start.48 = (bf16[128,1024]{1,0:T(8,128)(2,1)S(1)}, bf16[128,1024]{1,0:T(8,128)(2,1)S(1)}, u32[]{:S(2)}, u32[]{:S(2)}) collective-permute-start(bf16[128,1024]{1,0:T(8,128)(2,1)S(1)} %copy-done.12), channel_id=1, source_target_pairs={{0,2},{2,4},{4,6},{6,0},{1,3},{3,5},{5,7},{7,1},{8,10},{10,12},{12... | collective-permute-start | bytes 786440 | tf_op jit(solution)/shard_map/ppermute | solution.py:22
  296.8 202.0 %reduce-scatter.4.cloned.1.call-start = ((), (), s32[]{:S(2)}) async-start(), calls=%async_computation.4 | async-start | bytes 3538944 | tf_op jit(solution)/shard_map/reduce_scatter | solution.py:1121
  348.0 26.1 %collective-permute-start.79 = (bf16[256,1024]{1,0:T(8,128)(2,1)S(1)}, bf16[256,1024]{1,0:T(8,128)(2,1)S(1)}, u32[]{:S(2)}, u32[]{:S(2)}) collective-permute-start(bf16[256,1024]{1,0:T(8,128)(2,1)S(1)} %get-tuple-element.329), channel_id=1, source_target_pairs={{0,1},{1,0},{2,3},{3,2},{4,5},{5,4},{6,7},{7,6},{8,9},{9,8},{10,11... | collective-permute-start | bytes 1572872 | tf_op jit(solution)/shard_map/ppermute | solution.py:22
  388.2 110.7 %reduce-scatter.8.cloned.1.call-start = ((), (), s32[]{:S(2)}) async-start(), calls=%async_computation.6 | async-start | bytes 655360 | tf_op jit(solution)/shard_map/reduce_scatter | solution.py:1311
  407.7 23.4 %collective-permute-start.86 = (bf16[2,128,1024]{2,1,0:T(8,128)(2,1)S(1)}, bf16[2,128,1024]{2,1,0:T(8,128)(2,1)S(1)}, u32[]{:S(2)}, u32[]{:S(2)}) collective-permute-start(bf16[2,128,1024]{2,1,0:T(8,128)(2,1)S(1)} %get-tuple-element.355), channel_id=1, source_target_pairs={{0,16},{8,24},{16,0},{24,8},{1,17},{9,25},{17,1},{25,9},{2,18},{10... | collective-permute-start | bytes 1572872 | tf_op jit(solution)/shard_map/ppermute | solution.py:22
  410.3 37.0 %collective-permute-start.87 = (bf16[2,128,1024]{2,1,0:T(8,128)(2,1)S(1)}, bf16[2,128,1024]{2,1,0:T(8,128)(2,1)S(1)}, u32[]{:S(2)}, u32[]{:S(2)}) collective-permute-start(bf16[2,128,1024]{2,1,0:T(8,128)(2,1)S(1)} %get-tuple-element.356), channel_id=1, source_target_pairs={{0,8},{8,16},{16,24},{24,0},{1,9},{9,17},{17,25},{25,1},{2,10},{10... | collective-permute-start | bytes 1572872 | tf_op jit(solution)/shard_map/ppermute | solution.py:22
  410.8 38.9 %collective-permute-start.85 = (bf16[2,128,1024]{2,1,0:T(8,128)(2,1)S(1)}, bf16[2,128,1024]{2,1,0:T(8,128)(2,1)S(1)}, u32[]{:S(2)}, u32[]{:S(2)}) collective-permute-start(bf16[2,128,1024]{2,1,0:T(8,128)(2,1)S(1)} %get-tuple-element.340.refs_12_), channel_id=1, source_target_pairs={{0,24},{8,0},{16,8},{24,16},{1,25},{9,1},{17,9},{25,17},{2,26},{10... | collective-permute-start | bytes 1572872 | tf_op jit(solution)/shard_map/ppermute | solution.py:22
  428.7 22.6 %collective-permute-start.84 = (bf16[4,128,512]{2,1,0:T(8,128)(2,1)S(1)}, bf16[4,128,512]{2,1,0:T(8,128)(2,1)S(1)}, u32[]{:S(2)}, u32[]{:S(2)}) collective-permute-start(bf16[4,128,512]{2,1,0:T(8,128)(2,1)S(1)} %get-tuple-element.343), channel_id=1, source_target_pairs={{0,1},{1,0},{2,3},{3,2},{4,5},{5,4},{6,7},{7,6},{8,9},{9,8},{10,11... | collective-permute-start | bytes 1572872 | tf_op jit(solution)/shard_map/ppermute | solution.py:22
  454.0 18.9 %collective-permute-start.92 = (bf16[256,1024]{1,0:T(8,128)(2,1)S(1)}, bf16[256,1024]{1,0:T(8,128)(2,1)S(1)}, u32[]{:S(2)}, u32[]{:S(2)}) collective-permute-start(bf16[256,1024]{1,0:T(8,128)(2,1)S(1)} %get-tuple-element.372), channel_id=1, source_target_pairs={{0,1},{1,0},{2,3},{3,2},{4,5},{5,4},{6,7},{7,6},{8,9},{9,8},{10,11... | collective-permute-start | bytes 1572872 | tf_op jit(solution)/shard_map/ppermute | solution.py:22
  477.8 100.8 %all-gather.5.cloned.1.call-start = ((), (), s32[]{:S(2)}) async-start(), calls=%async_computation.7 | async-start | bytes 5013504 | tf_op jit(solution)/shard_map/all_gather | solution.py:1327
  480.1 18.7 %collective-permute-start.98 = (bf16[2,96,1024]{2,1,0:T(8,128)(2,1)S(1)}, bf16[2,96,1024]{2,1,0:T(8,128)(2,1)S(1)}, u32[]{:S(2)}, u32[]{:S(2)}) collective-permute-start(bf16[2,96,1024]{2,1,0:T(8,128)(2,1)S(1)} %get-tuple-element.379), channel_id=1, source_target_pairs={{0,8},{8,16},{16,24},{24,0},{1,9},{9,17},{17,25},{25,1},{2,10},{10... | collective-permute-start | bytes 1179656 | tf_op jit(solution)/shard_map/ppermute | solution.py:22
  480.1 18.7 %collective-permute-start.96 = (bf16[2,96,1024]{2,1,0:T(8,128)(2,1)S(1)}, bf16[2,96,1024]{2,1,0:T(8,128)(2,1)S(1)}, u32[]{:S(2)}, u32[]{:S(2)}) collective-permute-start(bf16[2,96,1024]{2,1,0:T(8,128)(2,1)S(1)} %get-tuple-element.377.refs_1_), channel_id=1, source_target_pairs={{0,24},{8,0},{16,8},{24,16},{1,25},{9,1},{17,9},{25,17},{2,26},{10... | collective-permute-start | bytes 1179656 | tf_op jit(solution)/shard_map/ppermute | solution.py:22
  482.8 23.5 %collective-permute-start.88 = (bf16[144,1024]{1,0:T(8,128)(2,1)}, bf16[144,1024]{1,0:T(8,128)(2,1)S(1)}, u32[]{:S(2)}, u32[]{:S(2)}) collective-permute-start(bf16[144,1024]{1,0:T(8,128)(2,1)} %copy-done.56), channel_id=1, source_target_pairs={{0,6},{2,0},{4,2},{6,4},{1,7},{3,1},{5,3},{7,5},{8,14},{10,8},{12,... | collective-permute-start | bytes 884744 | tf_op jit(solution)/shard_map/ppermute | solution.py:22
  501.6 23.4 %collective-permute-start.100 = (bf16[256,1024]{1,0:T(8,128)(2,1)S(1)}, bf16[256,1024]{1,0:T(8,128)(2,1)S(1)}, u32[]{:S(2)}, u32[]{:S(2)}) collective-permute-start(bf16[256,1024]{1,0:T(8,128)(2,1)S(1)} %get-tuple-element.387), channel_id=1, source_target_pairs={{0,64},{64,0},{1,65},{65,1},{2,66},{66,2},{3,67},{67,3},{4,68},{68... | collective-permute-start | bytes 1572872 | tf_op jit(solution)/shard_map/ppermute | solution.py:22
  505.1 19.9 %collective-permute-start.101 = (bf16[128,1024]{1,0:T(8,128)(2,1)S(1)}, bf16[128,1024]{1,0:T(8,128)(2,1)S(1)}, u32[]{:S(2)}, u32[]{:S(2)}) collective-permute-start(bf16[128,1024]{1,0:T(8,128)(2,1)S(1)} %get-tuple-element.386), channel_id=1, source_target_pairs={{64,32},{96,0},{65,33},{97,1},{66,34},{98,2},{67,35},{99,3},{68,36... | collective-permute-start | bytes 786440 | tf_op jit(solution)/shard_map/ppermute | solution.py:899
  506.4 18.6 %collective-permute-start.99 = (bf16[128,1024]{1,0:T(8,128)(2,1)S(1)}, bf16[128,1024]{1,0:T(8,128)(2,1)S(1)}, u32[]{:S(2)}, u32[]{:S(2)}) collective-permute-start(bf16[128,1024]{1,0:T(8,128)(2,1)S(1)} %get-tuple-element.386), channel_id=1, source_target_pairs={{0,32},{32,0},{1,33},{33,1},{2,34},{34,2},{3,35},{35,3},{4,36},{36... | collective-permute-start | bytes 786440 | tf_op jit(solution)/shard_map/ppermute | solution.py:22
  529.6 60.0 %collective-permute-start.103 = (bf16[256,1024]{1,0:T(8,128)(2,1)S(1)}, bf16[256,1024]{1,0:T(8,128)(2,1)S(1)}, u32[]{:S(2)}, u32[]{:S(2)}) collective-permute-start(bf16[256,1024]{1,0:T(8,128)(2,1)S(1)} %other_layer_kernel.1), channel_id=1, source_target_pairs={{0,64},{64,0},{1,65},{65,1},{2,66},{66,2},{3,67},{67,3},{4,68},{68... | collective-permute-start | bytes 1572872 | tf_op jit(solution)/shard_map/ppermute | solution.py:22
  (151 other events, 2087.9 us)
Sparse Core Ops, SparseCore 0:
  40.5 77.5 all-gather.2
  297.0 71.9 reduce-scatter.5
  388.3 64.6 reduce-scatter.3
  477.9 18.9 reduce-scatter.7
  527.4 51.0 all-gather.4
